TPU v7x, 32 devices: a whole 2x2x4 slice. The times are simulated.
32 devices in a mesh: groups: 2 (over y), param: 8 (over z, x), dp: 2 (over core).
Axes of the slice: x: 2, y: 2, z: 4, core: 2. Of those that a mesh axis runs over, the one named last changes fastest.
Arguments:
- hidden: bfloat16 [12, 128, 14336], P(('groups', 'dp'), None, 'param'), parts along dimension 0, may hold values from -6 to 6
- cotangent: bfloat16 [12, 128, 4096], P(('groups', 'dp'), None, 'param'), parts along dimension 0, may hold values from -0.5 to 0.5
- sign_flips: int32 [14336, 4096], P('param'), may hold values from -1 to 1, as said below
- offsets: int32 [8192], P('param'), may hold values from 0 to 7340031
Outputs:
- sketch: float32 [12, 8192], P(('groups', 'dp')), parts along dimension 0
There are 2 independent parts, one for each index of `groups`. A program takes and returns all parts, laid end to end along the dimension named above; an argument that names none is the same for every part. Nothing has to cross between parts.
Inputs may be any that keep to these rules, and one draw needn't show every extreme that they name: `sign_flips`: every entry is -1 or +1.
All inputs are finite; a program needn't handle non-finite values.
Results may differ from a plain program's by a relative error of at most 0.003.
Values may be sent and summed in bfloat16 or wider, within the bound.
No kernel may reach another device: no remote copies, remote signals or barrier semaphores. Data moves between devices by JAX's collectives and lax.ppermute only.
A program may use at most 448 MiB of HBM per device.

v0:
```python
import math

import jax
import jax.numpy as jnp
from jax import lax
from jax.sharding import PartitionSpec as P


def bit_parity(common_bits, bit_count):
    parity = jnp.zeros_like(common_bits)
    for position in range(bit_count):
        parity = jnp.bitwise_xor(parity, jnp.bitwise_and(jnp.right_shift(common_bits, position), 1))
    return parity


def sylvester(length, num_type):
    positions = lax.iota(jnp.int32, length)
    common_bits = jnp.bitwise_and(positions[:, None], positions[None, :])
    parity = bit_parity(common_bits, length.bit_length())
    return (1 - 2 * parity).astype(num_type)


def local(hidden, cotangent, sign_flips, offsets):
    examples, tokens, rows = hidden.shape
    width = sign_flips.shape[1]
    parties = lax.axis_size("param")
    own_index = lax.axis_index("param")
    per_shard = offsets.shape[0]
    norm_scale = 1.0 / math.sqrt(parties * width)
    block = jnp.einsum(
        "etr,etd->erd",
        hidden,
        lax.all_gather(cotangent, "param", axis=2, tiled=True),
        preferred_element_type=jnp.float32,
    )
    flipped = block.astype(jnp.bfloat16) * sign_flips.astype(jnp.bfloat16)
    tile_width = min(width, 512)
    outer_count = width // tile_width
    inner_table = sylvester(tile_width, jnp.bfloat16)
    outer_table = sylvester(outer_count, jnp.float32)
    tiled = flipped.reshape(examples, rows, outer_count, tile_width)
    section_one = jnp.einsum(
        "erab,bc->erac", tiled, inner_table, preferred_element_type=jnp.float32
    )
    row_mixed = jnp.einsum(
        "ab,erbc->erac", outer_table, section_one, precision=lax.Precision.HIGHEST
    )
    row_mixed = row_mixed.reshape(examples, rows, width)
    all_offsets = lax.all_gather(offsets, "param", axis=0, tiled=True)
    flattened = row_mixed.reshape(examples, rows * width)
    picked = jnp.take(flattened, all_offsets, axis=1).reshape(examples, parties, per_shard)
    incoming = lax.all_to_all(picked, "param", split_axis=1, concat_axis=1, tiled=True)
    sources = lax.iota(jnp.int32, parties)
    row_parity = bit_parity(jnp.bitwise_and(sources, own_index), parties.bit_length())
    row_signs = (1 - 2 * row_parity).astype(jnp.float32)
    segment = (
        jnp.einsum("q,eqk->ek", row_signs, incoming, precision=lax.Precision.HIGHEST) * norm_scale
    )
    sketch = lax.all_gather(segment, "param", axis=1, tiled=True)
    return sketch


def solution(mesh):
    return jax.shard_map(
        local,
        mesh=mesh,
        in_specs=(
            P(("groups", "dp"), None, "param"),
            P(("groups", "dp"), None, "param"),
            P("param", None),
            P("param"),
        ),
        out_specs=P(("groups", "dp"), None),
        check_vma=False,
    )
```

profile of v0, /device:TPU:0, one launch (start us, length us, event | category | flops | bytes accessed | tf_op | source)
XLA Modules:
  0.0 510.0 jit_solution(2090012371067125703)
XLA Ops:
  6.5 0.0 copy-start
  6.5 0.0 all-gather.2.cloned.1.call-start
  6.5 0.7 all-gather.2.cloned.1.call-update
  7.3 16.6 %convert_element_type.17 = bf16[1792,4096]{1,0:T(8,128)(2,1)} convert(s32[1792,4096]{1,0:T(8,128)} %param.6) | non-fusion elementwise | flops 7340032 | bytes 44040192 | tf_op jit(solution)/shard_map/convert_element_type | solution.py:36
  23.9 0.0 copy-done.4
  23.9 32.7 %all_gather.9 = s32[8192]{0:T(1024)S(1)} all-gather(s32[1024]{0:T(1024)S(1)} %copy-done.4), channel_id=1, replica_groups=mesh['groups'=2,'param'=8,'dp'=2] {'param'}, dimensions={0}, use_global_device_ids=true | all-gather | bytes 36864 | tf_op jit(solution)/shard_map/all_gather | solution.py:49
  56.5 0.6 broadcast_in_dim.19
  57.2 0.6 fusion.16
  57.8 17.5 %all-gather.2.cloned.1.call-done = bf16[3,128,4096]{2,1,0:T(8,128)(2,1)} async-done(((bf16[3,128,512]{2,1,0:T(8,128)(2,1)}), bf16[3,128,4096]{2,1,0:T(8,128)(2,1)}) %all-gather.2.cloned.1.call-update) | async-done | bytes 3145744 | tf_op jit(solution)/shard_map/all_gather | solution.py:33
  75.3 0.0 copy-done
  75.3 23.3 %convert_multiply_fusion = bf16[3,1792,4096]{2,1,0:T(8,128)(2,1)} fusion(bf16[3,128,1792]{2,1,0:T(8,128)(2,1)S(1)} %copy-done, bf16[3,128,4096]{2,1,0:T(8,128)(2,1)} %all-gather.2.cloned.1.call-done, bf16[1792,4096]{1,0:T(8,128)(2,1)} %convert_element_type.17), kind=kOutput, calls=%fused_computation.3 | convolution fusion | flops 5681184768 | bytes 63242240 | tf_op jit(solution)/shard_map/etr,etd->erd/dot_general | solution.py:30
  98.6 29.5 %copy.13 = bf16[672,8,8,512]{3,2,1,0:T(8,128)(2,1)} copy(bf16[672,8,8,512]{3,1,2,0:T(8,128)(2,1)} %bitcast.41) | data formatting | bytes 88080384
  128.1 47.6 %fusion = f32[3,1792,8,512]{3,2,1,0:T(8,128)} fusion(bf16[3,1792,8,512]{3,2,1,0:T(8,128)(2,1)} %bitcast.42), kind=kOutput, calls=%fused_computation.1 | convolution fusion | flops 22557229056 | bytes 132120576 | tf_op jit(solution)/shard_map/erab,bc->erac/dot_general | solution.py:42
  175.7 81.5 %convolution_bitcast_fusion = f32[1,3,14336,512]{3,2,1,0:T(8,128)} fusion(f32[3,1792,8,512]{3,2,1,0:T(8,128)} %fusion), kind=kOutput, calls=%fused_computation.4 | convolution fusion | flops 2113930240 | bytes 176160768 | tf_op jit(solution)/shard_map/ab,erbc->erac/dot_general | solution.py:45
  257.3 110.3 %copy.14 = f32[1,3,14336,512]{3,1,2,0:T(4,128)} copy(f32[1,3,14336,512]{3,2,1,0:T(8,128)} %convolution_bitcast_fusion) | data formatting | bytes 176160768
  367.6 0.0 copy-done.2
  367.6 92.6 %gather_fusion = f32[8192,3]{0,1:T(4,128)S(1)} fusion(f32[3,7340032]{1,0:T(4,128)} %bitcast.18, s32[8192]{0:T(1024)S(1)} %copy-done.2), kind=kCustom, calls=%fused_computation | custom fusion | bytes 229376 | tf_op jit(solution)/shard_map/jit(_take)/gather | solution.py:51
  460.2 0.7 broadcast_select_fusion
  460.9 3.4 all-to-all-start
  464.3 7.3 %all-to-all-done = f32[3,8,1024]{2,0,1:T(4,128)S(1)} async-done(((f32[3,8,1024]{2,0,1:T(4,128)}), f32[3,8,1024]{2,0,1:T(4,128)S(1)}, u32[]{:S(2)}, u32[]{:S(2)}) %all-to-all-start) | async-done | bytes 98336 | tf_op jit(solution)/shard_map/all_to_all | solution.py:52
  471.6 0.3 fusion.14
  471.8 30.6 %all_gather.11 = f32[3,8192]{1,0:T(4,128)S(1)} all-gather(f32[3,1024]{1,0:T(4,128)S(1)} %bitcast_multiply_fusion), channel_id=1, replica_groups=mesh['groups'=2,'param'=8,'dp'=2] {'param'}, dimensions={1}, use_global_device_ids=true | all-gather | bytes 110592 | tf_op jit(solution)/shard_map/all_gather | solution.py:59
  502.5 0.7 copy.19
  503.1 0.0 copy-done.1
  (7 shorter events, 0.0 us)
Async XLA Ops:
  6.5 68.8 %copy-start = (bf16[3,128,1792]{2,1,0:T(8,128)(2,1)S(1)}, bf16[3,128,1792]{2,1,0:T(8,128)(2,1)}, u32[]{:S(2)}) copy-start(bf16[3,128,1792]{2,1,0:T(8,128)(2,1)} %param.4) | copy-start | bytes 4128772
  6.5 17.3 %copy-start.4 = (s32[1024]{0:T(1024)S(1)}, s32[1024]{0:T(1024)}, u32[]{:S(2)}) copy-start(s32[1024]{0:T(1024)} %param.7) | copy-start | bytes 12292
  6.5 68.8 %all-gather.2.cloned.1.call-start = ((), (), s32[]{:S(2)}) async-start(), calls=%async_computation.1 | async-start | bytes 3538944 | tf_op jit(solution)/shard_map/all_gather | solution.py:33
  257.2 110.3 %copy-start.2 = (s32[8192]{0:T(1024)S(1)}, s32[8192]{0:T(1024)}, u32[]{:S(2)}) copy-start(s32[8192]{0:T(1024)} %fusion.16) | copy-start | bytes 98308
  257.3 202.9 %copy-start.3 = (pred[8,1024]{1,0:T(8,128)(4,1)S(1)}, pred[8,1024]{1,0:T(8,128)(4,1)}, u32[]{:S(2)}) copy-start(pred[8,1024]{1,0:T(8,128)(4,1)} %broadcast_in_dim.19) | copy-start | bytes 24580
  257.3 245.9 %copy-start.1 = (bf16[3,128,1792]{2,1,0:T(8,128)(2,1)S(1)}, bf16[3,128,1792]{2,1,0:T(8,128)(2,1)}, u32[]{:S(2)}) copy-start(bf16[3,128,1792]{2,1,0:T(8,128)(2,1)} %param.4) | copy-start | bytes 4128772
  460.9 10.7 %all-to-all-start = ((f32[3,8,1024]{2,0,1:T(4,128)}), f32[3,8,1024]{2,0,1:T(4,128)S(1)}, u32[]{:S(2)}, u32[]{:S(2)}) async-start(f32[3,8,1024]{2,0,1:T(4,128)} %broadcast_select_fusion), calls=%async_computation | async-start | bytes 262144 | tf_op jit(solution)/shard_map/all_to_all | solution.py:52
Sparse Core Ops, SparseCore 0:
  9.4 65.8 all-gather.1
where the time goes:
time: 513 us; the launch traced here: 510 us
  local copies, waits for them, and re-layouts  234 us (46%)
  matrix products  153 us (30%)
  blocking collectives  63.3 us (12%)
  waiting for transfers between devices  25.5 us (5%)
  other arithmetic  17.9 us (3%)
  between operations  13.5 us (3%)
    unnamed x13, local copies, waits for them, and re-layouts  141 us
    gather x1, local copies, waits for them, and re-layouts, local(): jnp.take(flattened, all_offsets, axis=1)  92.6 us
    dot_general x1, matrix products, local(): jnp.einsum('ab,erbc->erac', outer_table, section_one, precision=lax.Preci...  81.5 us
    dot_general x1, matrix products, local(): jnp.einsum('erab,bc->erac', tiled, inner_table, preferred_element_type=jn...  47.6 us
    all_gather x1, blocking collectives, local(): all_offsets = lax.all_gather(offsets, 'param', axis=0, tiled=True)  32.7 us
    all_gather x1, blocking collectives, local(): sketch = lax.all_gather(segment, 'param', axis=1, tiled=True)  30.6 us
    dot_general x1, matrix products, local(): jnp.einsum('etr,etd->erd', hidden, lax.all_gather(cotangent, 'param', axi...  23.3 us
    all_gather x1, waiting for transfers between devices, local(): lax.all_gather(cotangent, 'param', axis=2, tiled=True)  17.5 us
  transfers between devices with their start and end apart: 2, of which 2 were waited for; matrix products, arithmetic and copies ran while one was open for 4% of the time, Pallas kernels for 0%

commit v1 on v0

v1 whole, which is shorter than its diff:
```python
import functools
import math

import jax
import jax.numpy as jnp
from jax import lax
from jax.experimental import pallas as pl
from jax.experimental.pallas import tpu as pltpu
from jax.sharding import PartitionSpec as P

I32, F32, BF16 = jnp.int32, jnp.float32, jnp.bfloat16
LANES = 128
HALF = 16
MIB = 2**20


def signed(word):
    return word - 2**32 if word >= 2**31 else word


def parity(bits, count):
    shift = 1
    while shift < count:
        shift *= 2
    while shift > 1:
        shift //= 2
        bits = bits ^ (bits >> shift)
    return bits & 1


def pick_tile(rows, most):
    return max(size for size in range(16, min(rows, most) + 1, 16) if rows % size == 0)


def pack_kernel(flips_ref, words_ref):
    words = None
    for tile in range(flips_ref.shape[1] // LANES):
        bit = tile // 2 + HALF * (tile % 2)
        flips = flips_ref[:, tile * LANES:(tile + 1) * LANES]
        term = (flips >> 1) & 1 if bit == 0 else flips & jnp.int32(signed(1 << bit))
        words = term if words is None else words | term
    words_ref[...] = words


def pack(sign_flips):
    rows, width = sign_flips.shape
    tile = pick_tile(rows, 256)
    return pl.pallas_call(
        pack_kernel,
        grid=(rows // tile,),
        in_specs=[pl.BlockSpec((tile, width), lambda i: (i, 0))],
        out_specs=pl.BlockSpec((tile, LANES), lambda i: (i, 0)),
        out_shape=jax.ShapeDtypeStruct((rows, LANES), I32),
        compiler_params=pltpu.CompilerParams(vmem_limit_bytes=32 * MIB),
        cost_estimate=pl.CostEstimate(flops=2 * rows * width, bytes_accessed=4 * rows * width, transcendentals=0),
        name="pack_signs",
    )(sign_flips)


def hadamard_words(column):
    length = column.shape[1]
    lane = lax.broadcasted_iota(I32, (LANES, length), 0)
    words = -parity(lane & column, 7)

    def where_bit(bit, pattern):
        return -((column >> bit) & 1) & jnp.int32(signed(pattern))

    upper = where_bit(7, 0xFFFF0000)
    for bit, pattern in ((8, 0xAAAA), (9, 0xCCCC), (10, 0xF0F0), (11, 0xFF00)):
        upper = upper ^ where_bit(bit, pattern * 0x10001)
    return words ^ upper


def gather_kernel(rows_ref, offsets_ref, words_ref, hidden_ref, signs_ref, picked_ref, held, *, length, row_shift):
    step = pl.program_id(0)
    offsets = offsets_ref[...]
    unroll = 32

    def copy_rows(group, _):
        for sub in range(unroll):
            at = group * unroll + sub
            held[pl.ds(at, 1), :] = words_ref[pl.ds(rows_ref[step * length + at], 1), :]
        return 0

    lax.fori_loop(0, length // unroll, copy_rows, 0)
    row = lax.broadcasted_iota(I32, (hidden_ref.shape[1], length), 0)
    one_hot = jnp.where(row == (offsets >> row_shift), 1.0, 0.0).astype(BF16)
    picked_ref[...] = jnp.dot(hidden_ref[...], one_hot, preferred_element_type=F32).astype(BF16)
    signs_ref[...] = held[...].T ^ hadamard_words(offsets & ((1 << row_shift) - 1))


def gather(offsets, words, hidden, width):
    count, tokens, length = offsets.shape[0], hidden.shape[0], 1024
    row_shift = width.bit_length() - 1
    return pl.pallas_call(
        functools.partial(gather_kernel, length=length, row_shift=row_shift),
        grid_spec=pltpu.PrefetchScalarGridSpec(
            num_scalar_prefetch=1,
            grid=(count // length,),
            in_specs=[
                pl.BlockSpec((1, length), lambda i, _: (0, i)),
                pl.BlockSpec(words.shape, lambda i, _: (0, 0)),
                pl.BlockSpec(hidden.shape, lambda i, _: (0, 0)),
            ],
            out_specs=[
                pl.BlockSpec((LANES, length), lambda i, _: (0, i)),
                pl.BlockSpec((tokens, length), lambda i, _: (0, i)),
            ],
            scratch_shapes=[pltpu.VMEM((length, LANES), I32)],
        ),
        out_shape=[jax.ShapeDtypeStruct((LANES, count), I32), jax.ShapeDtypeStruct((tokens, count), BF16)],
        compiler_params=pltpu.CompilerParams(vmem_limit_bytes=48 * MIB),
        cost_estimate=pl.CostEstimate(
            flops=2 * hidden.size * count, bytes_accessed=4 * LANES * count + 2 * tokens * count, transcendentals=0
        ),
        name="gather_rows",
    )(offsets >> row_shift, offsets.reshape(1, count), words, hidden)


def project_kernel(scalars, *refs, blocks, has_total, last, length, start, per_shard, parties, scale):
    cotangents = refs[:blocks]
    signs_ref, rest = refs[blocks], refs[blocks + 1:]
    total = None
    if has_total:
        total, rest = rest[0][...], rest[1:]
    words = signs_ref[...]
    halves = cotangents[0].shape[1] // (2 * LANES)
    for at in range(blocks):
        pieces = []
        for half in range(halves):
            bit = scalars[1 + at] * halves + half
            for mask in (jnp.int32(1) << bit, jnp.int32(1) << (bit + HALF)):
                pieces.append(jnp.where((words & mask) != 0, -1.0, 1.0).astype(BF16))
        term = jnp.dot(cotangents[at][...], jnp.concatenate(pieces, axis=0), preferred_element_type=F32)
        total = term if total is None else total + term
    if not last:
        rest[0][...] = total
        return
    picked_ref, out_ref = rest
    examples = out_ref.shape[0]
    position = start + pl.program_id(0) * length + lax.broadcasted_iota(I32, (1, length), 1)
    shard = position // per_shard
    sign = scale * (1 - 2 * parity(shard & scalars[0], parties.bit_length())).astype(F32)
    weighted = (total * picked_ref[...].astype(F32)).reshape(examples, -1, length)
    out_ref[...] = jnp.sum(weighted, axis=1) * sign


def project(scalars, cotangents, signs, total, picked, examples, span, per_shard, parties, scale):
    start, count = span
    tokens, depth = cotangents[0].shape
    length = 1024
    blocks = len(cotangents)
    first = start // length
    last = picked is not None
    shifted = lambda i, _: (0, i + first)
    in_specs = [pl.BlockSpec((tokens, depth), lambda i, _: (0, 0)) for _ in cotangents]
    in_specs.append(pl.BlockSpec((LANES, length), shifted))
    args = list(cotangents) + [signs]
    if total is not None:
        in_specs.append(pl.BlockSpec((tokens, length), shifted))
        args.append(total)
    if last:
        in_specs.append(pl.BlockSpec((tokens, length), shifted))
        args.append(picked)
    rows = examples if last else tokens
    return pl.pallas_call(
        functools.partial(
            project_kernel, blocks=blocks, has_total=total is not None, last=last, length=length, start=start,
            per_shard=per_shard, parties=parties, scale=scale,
        ),
        grid_spec=pltpu.PrefetchScalarGridSpec(
            num_scalar_prefetch=1,
            grid=(count // length,),
            in_specs=in_specs,
            out_specs=pl.BlockSpec((rows, length), lambda i, _: (0, i)),
        ),
        out_shape=jax.ShapeDtypeStruct((rows, count), F32),
        compiler_params=pltpu.CompilerParams(vmem_limit_bytes=56 * MIB),
        cost_estimate=pl.CostEstimate(
            flops=2 * tokens * depth * blocks * count, bytes_accessed=4 * tokens * count, transcendentals=0
        ),
        name="project_blocks",
    )(scalars, *args)


def by_xor(parties, step):
    return [(source, source ^ step) for source in range(parties)]


def exchange_offsets(offsets, own, parties):
    step = 1
    while step < parties:
        other = lax.ppermute(offsets, "param", by_xor(parties, step))
        offsets = jnp.where(
            (own & step) == 0, jnp.concatenate([offsets, other]), jnp.concatenate([other, offsets])
        )
        step *= 2
    return offsets


def sum_shards(values, parties):
    step = 1
    while step < parties:
        values = values + lax.ppermute(values, "param", by_xor(parties, step))
        step *= 2
    return values


def local(hidden, cotangent, sign_flips, offsets):
    examples, tokens, rows = hidden.shape
    width = sign_flips.shape[1]
    parties = lax.axis_size("param")
    own = lax.axis_index("param").astype(I32)
    per_shard = offsets.shape[0]
    count = per_shard * parties
    scale = 1.0 / math.sqrt(parties * width)
    flat = examples * tokens
    depth = cotangent.shape[2]
    held = cotangent.reshape(flat, depth)

    if depth % (2 * LANES) == 0 and parties % 2 == 0:
        order = list(range(0, parties, 2)) + list(range(parties - 1, 0, -2))
        forward = [(order[at], order[(at + 1) % parties]) for at in range(parties)]
        backward = [(target, source) for source, target in forward]
        place = jnp.where(own % 2 == 0, own // 2, parties - 1 - own // 2)

        def shard_at(spot):
            spot = (spot + parties) % parties
            return jnp.where(spot < parties // 2, 2 * spot, 2 * (parties - spot) - 1)

        pieces, numbers = [held], [own]
        ahead = behind = held
        for step in range(1, parties // 2):
            ahead = lax.ppermute(ahead, "param", forward)
            behind = lax.ppermute(behind, "param", backward)
            pieces += [ahead, behind]
            numbers += [shard_at(place - step), shard_at(place + step)]
        middle = flat // 2
        ahead = lax.ppermute(ahead[:middle], "param", forward)
        behind = lax.ppermute(behind[middle:], "param", backward)
        pieces.append(jnp.concatenate([ahead, behind], axis=0))
        numbers.append(shard_at(place + parties // 2))
    else:
        whole = lax.all_gather(cotangent, "param", axis=2, tiled=True).reshape(flat, width)
        span = 4 * LANES
        pieces = [whole[:, at:at + span] for at in range(0, width, span)]
        numbers = [jnp.int32(at) for at in range(len(pieces))]

    all_offsets = exchange_offsets(offsets, own, parties)
    words = pack(sign_flips)
    signs, picked = gather(all_offsets, words, hidden.reshape(flat, rows), width)

    def run(chosen, total, final, span):
        scalars = jnp.stack([own] + [numbers[at] for at in chosen])
        return project(
            scalars, [pieces[at] for at in chosen], signs, total, picked if final else None, examples, span,
            per_shard, parties, scale,
        )

    early = max(1, len(pieces) - 3)
    total = run(range(early), None, False, (0, count))
    late = range(early, len(pieces))
    half = count // 2
    parts = [sum_shards(run(late, total, True, (start, half)), parties) for start in (0, half)]
    return jnp.concatenate(parts, axis=1)


def solution(mesh):
    return jax.shard_map(
        local,
        mesh=mesh,
        in_specs=(
            P(("groups", "dp"), None, "param"),
            P(("groups", "dp"), None, "param"),
            P("param", None),
            P("param"),
        ),
        out_specs=P(("groups", "dp"), None),
        check_vma=False,
    )
```

time: 513 us -> 131 us (0.26)
  local copies, waits for them, and re-layouts: 234 us -> 1.45 us
  matrix products: 153 us -> 0 us
  Pallas kernels: 0 us -> 78 us
  blocking collectives: 63.3 us -> 0 us
  starting transfers between devices: 3.37 us -> 22.9 us
  other arithmetic: 17.9 us -> 3.11 us
  between operations: 13.5 us -> 0.18 us
    dot_general x4 -> x0, matrix products: 153 us -> none  [the longest x1 81.5 us: local(): jnp.einsum('ab,erbc->erac', outer_table, section_one, precision=lax.Preci...]
    unnamed x13 -> x19, local copies, waits for them, and re-layouts: 141 us -> 0.78 us
    gather x1 -> x0, local copies, waits for them, and re-layouts: 92.6 us -> none  [local(): jnp.take(flattened, all_offsets, axis=1)]
    pallas_call x0 -> x5, Pallas kernels: none -> 78 us  [the longest x3 42.1 us: project(): pl.pallas_call(functools.partial(project_kernel, blocks=blocks, has_total...]
    all_gather x2 -> x0, blocking collectives: 63.3 us -> none  [the longest x1 32.7 us: local(): all_offsets = lax.all_gather(offsets, 'param', axis=0, tiled=True)]
    ppermute x0 -> x17, waiting for transfers between devices: none -> 24.4 us  [the longest x3 11 us: exchange_offsets(): other = lax.ppermute(offsets, 'param', by_xor(parties, step))]
    ppermute x0 -> x17, starting transfers between devices: none -> 22.9 us  [the longest x6 8.11 us: sum_shards(): values = values + lax.ppermute(values, 'param', by_xor(parties, step))]
    all_gather x1 -> x0, waiting for transfers between devices: 17.5 us -> none  [local(): lax.all_gather(cotangent, 'param', axis=2, tiled=True)]
  transfers between devices with their start and end apart: 2 -> 17, of which waited for: 2 -> 7; matrix products, arithmetic and copies ran while one was open for 4% -> 2% of each run, Pallas kernels for 0% -> 52%
where the time goes in v1:
time: 131 us; the launch traced here: 130 us
  Pallas kernels  78 us (60%)
  waiting for transfers between devices  24.4 us (19%)
  starting transfers between devices  22.9 us (17%)
  other arithmetic  3.11 us (2%)
  local copies, waits for them, and re-layouts  1.45 us (1%)
    pallas_call x3, Pallas kernels, project(): pl.pallas_call(functools.partial(project_kernel, blocks=blocks, has_total...  42.1 us
    pallas_call x1, Pallas kernels, gather(): pl.pallas_call(functools.partial(gather_kernel, length=length, row_shift=...  25.1 us
    ppermute x3, waiting for transfers between devices, exchange_offsets(): other = lax.ppermute(offsets, 'param', by_xor(parties, step))  11 us
    pallas_call x1, Pallas kernels, pack(): pl.pallas_call(pack_kernel, grid=(rows // tile,), in_specs=[pl.BlockSpec(...  10.8 us
    ppermute x6, starting transfers between devices, sum_shards(): values = values + lax.ppermute(values, 'param', by_xor(parties, step))  8.11 us
    ppermute x3, waiting for transfers between devices, local(): ahead = lax.ppermute(ahead, 'param', forward)  7.19 us
    ppermute x3, starting transfers between devices, local(): ahead = lax.ppermute(ahead, 'param', forward)  7.12 us
    ppermute x6, waiting for transfers between devices, sum_shards(): values = values + lax.ppermute(values, 'param', by_xor(parties, step))  6.19 us
  transfers between devices with their start and end apart: 17, of which 7 were waited for; matrix products, arithmetic and copies ran while one was open for 2% of the time, Pallas kernels for 52%

profile of v1, /device:TPU:0, one launch (start us, length us, event | category | flops | bytes accessed | tf_op | source)
XLA Modules:
  0.0 130.1 jit_solution(4156624904733264047)
XLA Ops:
  0.0 3.0 %collective-permute-start = (bf16[384,512]{1,0:T(8,128)(2,1)}, bf16[384,512]{1,0:T(8,128)(2,1)S(1)}, u32[]{:S(2)}, u32[]{:S(2)}) collective-permute-start(bf16[384,512]{1,0:T(8,128)(2,1)} %bitcast.15), channel_id=1, source_target_pairs={{0,4},{4,8},{8,12},{12,14},{14,10},{10,6},{6,2},{2,0},{1,5},{5,9},... | collective-permute-start | bytes 1179656 | tf_op jit(solution)/shard_map/ppermute | solution.py:234
  3.0 1.9 %collective-permute-start.8 = (s32[1024]{0:T(1024)}, s32[1024]{0:T(1024)S(1)}, u32[]{:S(2)}, u32[]{:S(2)}) collective-permute-start(s32[1024]{0:T(1024)} %param.7), channel_id=1, source_target_pairs={{0,2},{2,0},{4,6},{6,4},{8,10},{10,8},{12,14},{14,12},{1,3},{3,1},... | collective-permute-start | bytes 12296 | tf_op jit(solution)/shard_map/ppermute | solution.py:193
  5.0 7.4 %collective-permute-done.8 = s32[1024]{0:T(1024)S(1)} collective-permute-done((s32[1024]{0:T(1024)}, s32[1024]{0:T(1024)S(1)}, u32[]{:S(2)}, u32[]{:S(2)}) %collective-permute-start.8) | collective-permute-done | bytes 4128 | tf_op jit(solution)/shard_map/ppermute | solution.py:193
  12.3 0.8 add_select_fusion.2
  13.1 3.6 %collective-permute-done.9 = s32[2048]{0:T(1024)S(1)} collective-permute-done((s32[2048]{0:T(1024)S(1)}, s32[2048]{0:T(1024)S(1)}, u32[]{:S(2)}, u32[]{:S(2)}) %collective-permute-start.9) | collective-permute-done | bytes 8224 | tf_op jit(solution)/shard_map/ppermute | solution.py:193
  16.8 3.6 %collective-permute-start.10 = (s32[4096]{0:T(1024)S(1)}, s32[4096]{0:T(1024)S(1)}, u32[]{:S(2)}, u32[]{:S(2)}) collective-permute-start(s32[4096]{0:T(1024)S(1)} %add_select_fusion.1), channel_id=1, source_target_pairs={{0,8},{2,10},{4,12},{6,14},{8,0},{10,2},{12,4},{14,6},{1,9},{3,11}... | collective-permute-start | bytes 49160 | tf_op jit(solution)/shard_map/ppermute | solution.py:193
  21.7 10.8 %pack_signs.1.words_ref = s32[1792,128]{1,0:T(8,128)S(1)} custom-call(s32[1792,4096]{1,0:T(8,128)} %flips_ref.1), custom_call_target="tpu_custom_call" | custom-call | flops 14680064 | bytes 29360128 | tf_op jit(solution)/shard_map/pack_signs/pallas_call | solution.py:48
  32.5 2.1 %collective-permute-start.1 = (bf16[384,512]{1,0:T(8,128)(2,1)S(1)}, bf16[384,512]{1,0:T(8,128)(2,1)S(1)}, u32[]{:S(2)}, u32[]{:S(2)}) collective-permute-start(bf16[384,512]{1,0:T(8,128)(2,1)S(1)} %collective-permute-done.refs_1_), channel_id=1, source_target_pairs={{0,4},{4,8},{8,12},{12,14},{14,10},{10,6},{6,2},{2,0},{1,5},{5,9},... | collective-permute-start | bytes 1179656 | tf_op jit(solution)/shard_map/ppermute | solution.py:234
  34.6 7.2 %collective-permute-done.1.refs_3_ = bf16[384,512]{1,0:T(8,128)(2,1)S(1)} collective-permute-done((bf16[384,512]{1,0:T(8,128)(2,1)S(1)}, bf16[384,512]{1,0:T(8,128)(2,1)S(1)}, u32[]{:S(2)}, u32[]{:S(2)}) %collective-permute-start.1) | collective-permute-done | bytes 393248 | tf_op jit(solution)/shard_map/ppermute | solution.py:234
  41.8 2.0 %collective-permute-start.2 = (bf16[384,512]{1,0:T(8,128)(2,1)S(1)}, bf16[384,512]{1,0:T(8,128)(2,1)S(1)}, u32[]{:S(2)}, u32[]{:S(2)}) collective-permute-start(bf16[384,512]{1,0:T(8,128)(2,1)S(1)} %collective-permute-done.1.refs_3_), channel_id=1, source_target_pairs={{0,4},{4,8},{8,12},{12,14},{14,10},{10,6},{6,2},{2,0},{1,5},{5,9},... | collective-permute-start | bytes 1179656 | tf_op jit(solution)/shard_map/ppermute | solution.py:234
  43.9 25.1 %gather_rows.1 = (s32[128,8192]{1,0:T(8,128)}, bf16[384,8192]{1,0:T(8,128)(2,1)}) custom-call(s32[8192]{0:T(1024)S(1)} %fusion.rows_ref, s32[1,8192]{1,0:T(1,128)S(1)} %broadcast_select_fusion.offsets_ref, s32[1792,128]{1,0:T(8,128)S(1)} %pack_signs.1.words_ref, bf16[384,1792]{1,0:T(8,128)(2,1)S(1)} %bitcast.12), custom_call_target="tpu_custom_call" | custom-call | flops 11274289152 | bytes 10485760 | tf_op jit(solution)/shard_map/gather_rows/pallas_call | solution.py:95
  69.0 2.1 %collective-permute-start.6 = (bf16[192,512]{1,0:T(8,128)(2,1)S(1)}, bf16[192,512]{1,0:T(8,128)(2,1)S(1)}, u32[]{:S(2)}, u32[]{:S(2)}) collective-permute-start(bf16[192,512]{1,0:T(8,128)(2,1)S(1)} %slice.8), channel_id=1, source_target_pairs={{0,4},{4,8},{8,12},{12,14},{14,10},{10,6},{6,2},{2,0},{1,5},{5,9},... | collective-permute-start | bytes 589832 | tf_op jit(solution)/shard_map/ppermute | solution.py:239
  71.2 21.6 %project_blocks.3.refs_4_ = f32[384,8192]{1,0:T(8,128)} custom-call(s32[6]{0:T(128)} %stack.46.scalars, bf16[384,512]{1,0:T(8,128)(2,1)} %bitcast.17, bf16[384,512]{1,0:T(8,128)(2,1)} %copy-done.5, bf16[384,512]{1,0:T(8,128)(2,1)} %copy-done.6, bf16[384,512]{1,0:T(8,128)(2,1)} %copy-done.7, bf16[384,512]{1,0:T(8,128)(2,1)} %copy-done.8, ...), custom_call_target="tpu_custom_call" | custom-call | flops 16106127360 | bytes 12582912 | tf_op jit(solution)/shard_map/project_blocks/pallas_call | solution.py:166
  92.9 0.7 copy-done.3
  93.6 10.2 %project_blocks.4 = f32[3,4096]{1,0:T(4,128)} custom-call(s32[4]{0:T(128)} %pad_add_fusion.scalars, bf16[384,512]{1,0:T(8,128)(2,1)} %copy-done.1, bf16[384,512]{1,0:T(8,128)(2,1)} %copy-done.2, bf16[384,512]{1,0:T(8,128)(2,1)} %copy-done.3, s32[128,8192]{1,0:T(8,128)} %get-tuple-element.7.refs_5_.refs_3_, f32[384,8192]{1,0:T(8,128)} %project_blocks.3.refs_4_, ...), custom_call_target="tpu_custom_call" | custom-call | flops 4831838208 | bytes 6291456 | tf_op jit(solution)/shard_map/project_blocks/pallas_call | solution.py:166
  104.2 10.2 %project_blocks.5 = f32[3,4096]{1,0:T(4,128)} custom-call(s32[4]{0:T(128)} %pad_add_fusion.scalars, bf16[384,512]{1,0:T(8,128)(2,1)} %copy-done.1, bf16[384,512]{1,0:T(8,128)(2,1)} %copy-done.2, bf16[384,512]{1,0:T(8,128)(2,1)} %copy-done.3, s32[128,8192]{1,0:T(8,128)} %get-tuple-element.7.refs_5_.refs_3_, f32[384,8192]{1,0:T(8,128)} %project_blocks.3.refs_4_, ...), custom_call_target="tpu_custom_call" | custom-call | flops 4831838208 | bytes 6291456 | tf_op jit(solution)/shard_map/project_blocks/pallas_call | solution.py:166
  114.4 1.7 %collective-permute-start.14 = (f32[3,4096]{1,0:T(4,128)}, f32[3,4096]{1,0:T(4,128)S(1)}, u32[]{:S(2)}, u32[]{:S(2)}) collective-permute-start(f32[3,4096]{1,0:T(4,128)} %project_blocks.5), channel_id=1, source_target_pairs={{0,2},{2,0},{4,6},{6,4},{8,10},{10,8},{12,14},{14,12},{1,3},{3,1},... | collective-permute-start | bytes 147464 | tf_op jit(solution)/shard_map/ppermute | solution.py:204
  116.2 2.1 %collective-permute-start.12 = (f32[3,4096]{1,0:T(4,128)S(1)}, f32[3,4096]{1,0:T(4,128)S(1)}, u32[]{:S(2)}, u32[]{:S(2)}) collective-permute-start(f32[3,4096]{1,0:T(4,128)S(1)} %add.108), channel_id=1, source_target_pairs={{0,4},{2,6},{4,0},{6,2},{8,12},{10,14},{12,8},{14,10},{1,5},{3,7},... | collective-permute-start | bytes 147464 | tf_op jit(solution)/shard_map/ppermute | solution.py:204
  118.9 0.9 add.111
  119.8 2.0 %collective-permute-start.15 = (f32[3,4096]{1,0:T(4,128)S(1)}, f32[3,4096]{1,0:T(4,128)S(1)}, u32[]{:S(2)}, u32[]{:S(2)}) collective-permute-start(f32[3,4096]{1,0:T(4,128)S(1)} %add.111), channel_id=1, source_target_pairs={{0,4},{2,6},{4,0},{6,2},{8,12},{10,14},{12,8},{14,10},{1,5},{3,7},... | collective-permute-start | bytes 147464 | tf_op jit(solution)/shard_map/ppermute | solution.py:204
  122.3 1.8 %collective-permute-done.15 = f32[3,4096]{1,0:T(4,128)S(1)} collective-permute-done((f32[3,4096]{1,0:T(4,128)S(1)}, f32[3,4096]{1,0:T(4,128)S(1)}, u32[]{:S(2)}, u32[]{:S(2)}) %collective-permute-start.15) | collective-permute-done | bytes 49184 | tf_op jit(solution)/shard_map/ppermute | solution.py:204
  124.1 1.5 %collective-permute-start.16 = (f32[3,4096]{1,0:T(4,128)S(1)}, f32[3,4096]{1,0:T(4,128)S(1)}, u32[]{:S(2)}, u32[]{:S(2)}) collective-permute-start(f32[3,4096]{1,0:T(4,128)S(1)} %add.112), channel_id=1, source_target_pairs={{0,8},{2,10},{4,12},{6,14},{8,0},{10,2},{12,4},{14,6},{1,9},{3,11}... | collective-permute-start | bytes 147464 | tf_op jit(solution)/shard_map/ppermute | solution.py:204
  125.6 2.1 %collective-permute-done.13 = f32[3,4096]{1,0:T(4,128)S(1)} collective-permute-done((f32[3,4096]{1,0:T(4,128)S(1)}, f32[3,4096]{1,0:T(4,128)S(1)}, u32[]{:S(2)}, u32[]{:S(2)}) %collective-permute-start.13) | collective-permute-done | bytes 49184 | tf_op jit(solution)/shard_map/ppermute | solution.py:204
  127.8 1.6 %collective-permute-done.16 = f32[3,4096]{1,0:T(4,128)S(1)} collective-permute-done((f32[3,4096]{1,0:T(4,128)S(1)}, f32[3,4096]{1,0:T(4,128)S(1)}, u32[]{:S(2)}, u32[]{:S(2)}) %collective-permute-start.16) | collective-permute-done | bytes 49184 | tf_op jit(solution)/shard_map/ppermute | solution.py:204
  (50 shorter events, 3.8 us)
Async XLA Ops:
  0.0 32.5 %collective-permute-start = (bf16[384,512]{1,0:T(8,128)(2,1)}, bf16[384,512]{1,0:T(8,128)(2,1)S(1)}, u32[]{:S(2)}, u32[]{:S(2)}) collective-permute-start(bf16[384,512]{1,0:T(8,128)(2,1)} %bitcast.15), channel_id=1, source_target_pairs={{0,4},{4,8},{8,12},{12,14},{14,10},{10,6},{6,2},{2,0},{1,5},{5,9},... | collective-permute-start | bytes 1179656 | tf_op jit(solution)/shard_map/ppermute | solution.py:234
  3.0 31.5 %collective-permute-start.3 = (bf16[384,512]{1,0:T(8,128)(2,1)}, bf16[384,512]{1,0:T(8,128)(2,1)S(1)}, u32[]{:S(2)}, u32[]{:S(2)}) collective-permute-start(bf16[384,512]{1,0:T(8,128)(2,1)} %bitcast.16), channel_id=1, source_target_pairs={{4,0},{8,4},{12,8},{14,12},{10,14},{6,10},{2,6},{0,2},{5,1},{9,5},... | collective-permute-start | bytes 1179656 | tf_op jit(solution)/shard_map/ppermute | solution.py:235
  3.0 9.3 %collective-permute-start.8 = (s32[1024]{0:T(1024)}, s32[1024]{0:T(1024)S(1)}, u32[]{:S(2)}, u32[]{:S(2)}) collective-permute-start(s32[1024]{0:T(1024)} %param.7), channel_id=1, source_target_pairs={{0,2},{2,0},{4,6},{6,4},{8,10},{10,8},{12,14},{14,12},{1,3},{3,1},... | collective-permute-start | bytes 12296 | tf_op jit(solution)/shard_map/ppermute | solution.py:193
  13.1 3.7 %collective-permute-start.9 = (s32[2048]{0:T(1024)S(1)}, s32[2048]{0:T(1024)S(1)}, u32[]{:S(2)}, u32[]{:S(2)}) collective-permute-start(s32[2048]{0:T(1024)S(1)} %add_select_fusion.2), channel_id=1, source_target_pairs={{0,4},{2,6},{4,0},{6,2},{8,12},{10,14},{12,8},{14,10},{1,5},{3,7},... | collective-permute-start | bytes 24584 | tf_op jit(solution)/shard_map/ppermute | solution.py:193
  16.8 17.8 %collective-permute-start.10 = (s32[4096]{0:T(1024)S(1)}, s32[4096]{0:T(1024)S(1)}, u32[]{:S(2)}, u32[]{:S(2)}) collective-permute-start(s32[4096]{0:T(1024)S(1)} %add_select_fusion.1), channel_id=1, source_target_pairs={{0,8},{2,10},{4,12},{6,14},{8,0},{10,2},{12,4},{14,6},{1,9},{3,11}... | collective-permute-start | bytes 49160 | tf_op jit(solution)/shard_map/ppermute | solution.py:193
  21.7 22.2 %copy-start = (bf16[3,128,1792]{2,1,0:T(8,128)(2,1)S(1)}, bf16[3,128,1792]{2,1,0:T(8,128)(2,1)}, u32[]{:S(2)}) copy-start(bf16[3,128,1792]{2,1,0:T(8,128)(2,1)} %param.4) | copy-start | bytes 4128772
  32.5 36.5 %copy-start.5 = (bf16[384,512]{1,0:T(8,128)(2,1)}, bf16[384,512]{1,0:T(8,128)(2,1)S(1)}, u32[]{:S(2)}) copy-start(bf16[384,512]{1,0:T(8,128)(2,1)S(1)} %collective-permute-done.refs_1_) | copy-start | bytes 1179652
  32.5 9.3 %collective-permute-start.1 = (bf16[384,512]{1,0:T(8,128)(2,1)S(1)}, bf16[384,512]{1,0:T(8,128)(2,1)S(1)}, u32[]{:S(2)}, u32[]{:S(2)}) collective-permute-start(bf16[384,512]{1,0:T(8,128)(2,1)S(1)} %collective-permute-done.refs_1_), channel_id=1, source_target_pairs={{0,4},{4,8},{8,12},{12,14},{14,10},{10,6},{6,2},{2,0},{1,5},{5,9},... | collective-permute-start | bytes 1179656 | tf_op jit(solution)/shard_map/ppermute | solution.py:234
  34.6 34.4 %copy-start.6 = (bf16[384,512]{1,0:T(8,128)(2,1)}, bf16[384,512]{1,0:T(8,128)(2,1)S(1)}, u32[]{:S(2)}) copy-start(bf16[384,512]{1,0:T(8,128)(2,1)S(1)} %collective-permute-done.3.refs_2_) | copy-start | bytes 1179652
  34.6 9.3 %collective-permute-start.4 = (bf16[384,512]{1,0:T(8,128)(2,1)S(1)}, bf16[384,512]{1,0:T(8,128)(2,1)S(1)}, u32[]{:S(2)}, u32[]{:S(2)}) collective-permute-start(bf16[384,512]{1,0:T(8,128)(2,1)S(1)} %collective-permute-done.3.refs_2_), channel_id=1, source_target_pairs={{4,0},{8,4},{12,8},{14,12},{10,14},{6,10},{2,6},{0,2},{5,1},{9,5},... | collective-permute-start | bytes 1179656 | tf_op jit(solution)/shard_map/ppermute | solution.py:235
  41.8 27.2 %copy-start.7 = (bf16[384,512]{1,0:T(8,128)(2,1)}, bf16[384,512]{1,0:T(8,128)(2,1)S(1)}, u32[]{:S(2)}) copy-start(bf16[384,512]{1,0:T(8,128)(2,1)S(1)} %collective-permute-done.1.refs_3_) | copy-start | bytes 1179652
  41.8 27.2 %collective-permute-start.2 = (bf16[384,512]{1,0:T(8,128)(2,1)S(1)}, bf16[384,512]{1,0:T(8,128)(2,1)S(1)}, u32[]{:S(2)}, u32[]{:S(2)}) collective-permute-start(bf16[384,512]{1,0:T(8,128)(2,1)S(1)} %collective-permute-done.1.refs_3_), channel_id=1, source_target_pairs={{0,4},{4,8},{8,12},{12,14},{14,10},{10,6},{6,2},{2,0},{1,5},{5,9},... | collective-permute-start | bytes 1179656 | tf_op jit(solution)/shard_map/ppermute | solution.py:234
  43.8 25.1 %copy-start.8 = (bf16[384,512]{1,0:T(8,128)(2,1)}, bf16[384,512]{1,0:T(8,128)(2,1)S(1)}, u32[]{:S(2)}) copy-start(bf16[384,512]{1,0:T(8,128)(2,1)S(1)} %collective-permute-done.4.refs_4_) | copy-start | bytes 1179652
  43.8 27.2 %collective-permute-start.5 = (bf16[384,512]{1,0:T(8,128)(2,1)S(1)}, bf16[384,512]{1,0:T(8,128)(2,1)S(1)}, u32[]{:S(2)}, u32[]{:S(2)}) collective-permute-start(bf16[384,512]{1,0:T(8,128)(2,1)S(1)} %collective-permute-done.4.refs_4_), channel_id=1, source_target_pairs={{4,0},{8,4},{12,8},{14,12},{10,14},{6,10},{2,6},{0,2},{5,1},{9,5},... | collective-permute-start | bytes 1179656 | tf_op jit(solution)/shard_map/ppermute | solution.py:235
  69.0 23.8 %copy-start.1 = (bf16[384,512]{1,0:T(8,128)(2,1)}, bf16[384,512]{1,0:T(8,128)(2,1)S(1)}, u32[]{:S(2)}) copy-start(bf16[384,512]{1,0:T(8,128)(2,1)S(1)} %collective-permute-done.2.refs_0_) | copy-start | bytes 1179652
  69.0 23.8 %collective-permute-start.6 = (bf16[192,512]{1,0:T(8,128)(2,1)S(1)}, bf16[192,512]{1,0:T(8,128)(2,1)S(1)}, u32[]{:S(2)}, u32[]{:S(2)}) collective-permute-start(bf16[192,512]{1,0:T(8,128)(2,1)S(1)} %slice.8), channel_id=1, source_target_pairs={{0,4},{4,8},{8,12},{12,14},{14,10},{10,6},{6,2},{2,0},{1,5},{5,9},... | collective-permute-start | bytes 589832 | tf_op jit(solution)/shard_map/ppermute | solution.py:239
  71.1 21.7 %copy-start.2 = (bf16[384,512]{1,0:T(8,128)(2,1)}, bf16[384,512]{1,0:T(8,128)(2,1)S(1)}, u32[]{:S(2)}) copy-start(bf16[384,512]{1,0:T(8,128)(2,1)S(1)} %collective-permute-done.5.refs_1_) | copy-start | bytes 1179652
  71.1 21.7 %collective-permute-start.7 = (bf16[192,512]{1,0:T(8,128)(2,1)S(1)}, bf16[192,512]{1,0:T(8,128)(2,1)S(1)}, u32[]{:S(2)}, u32[]{:S(2)}) collective-permute-start(bf16[192,512]{1,0:T(8,128)(2,1)S(1)} %slice.9), channel_id=1, source_target_pairs={{4,0},{8,4},{12,8},{14,12},{10,14},{6,10},{2,6},{0,2},{5,1},{9,5},... | collective-permute-start | bytes 589832 | tf_op jit(solution)/shard_map/ppermute | solution.py:240
  103.8 12.3 %collective-permute-start.11 = (f32[3,4096]{1,0:T(4,128)}, f32[3,4096]{1,0:T(4,128)S(1)}, u32[]{:S(2)}, u32[]{:S(2)}) collective-permute-start(f32[3,4096]{1,0:T(4,128)} %project_blocks.4), channel_id=1, source_target_pairs={{0,2},{2,0},{4,6},{6,4},{8,10},{10,8},{12,14},{14,12},{1,3},{3,1},... | collective-permute-start | bytes 147464 | tf_op jit(solution)/shard_map/ppermute | solution.py:204
  114.4 4.5 %collective-permute-start.14 = (f32[3,4096]{1,0:T(4,128)}, f32[3,4096]{1,0:T(4,128)S(1)}, u32[]{:S(2)}, u32[]{:S(2)}) collective-permute-start(f32[3,4096]{1,0:T(4,128)} %project_blocks.5), channel_id=1, source_target_pairs={{0,2},{2,0},{4,6},{6,4},{8,10},{10,8},{12,14},{14,12},{1,3},{3,1},... | collective-permute-start | bytes 147464 | tf_op jit(solution)/shard_map/ppermute | solution.py:204
  116.2 5.6 %collective-permute-start.12 = (f32[3,4096]{1,0:T(4,128)S(1)}, f32[3,4096]{1,0:T(4,128)S(1)}, u32[]{:S(2)}, u32[]{:S(2)}) collective-permute-start(f32[3,4096]{1,0:T(4,128)S(1)} %add.108), channel_id=1, source_target_pairs={{0,4},{2,6},{4,0},{6,2},{8,12},{10,14},{12,8},{14,10},{1,5},{3,7},... | collective-permute-start | bytes 147464 | tf_op jit(solution)/shard_map/ppermute | solution.py:204
  119.8 4.3 %collective-permute-start.15 = (f32[3,4096]{1,0:T(4,128)S(1)}, f32[3,4096]{1,0:T(4,128)S(1)}, u32[]{:S(2)}, u32[]{:S(2)}) collective-permute-start(f32[3,4096]{1,0:T(4,128)S(1)} %add.111), channel_id=1, source_target_pairs={{0,4},{2,6},{4,0},{6,2},{8,12},{10,14},{12,8},{14,10},{1,5},{3,7},... | collective-permute-start | bytes 147464 | tf_op jit(solution)/shard_map/ppermute | solution.py:204
  121.8 5.9 %collective-permute-start.13 = (f32[3,4096]{1,0:T(4,128)S(1)}, f32[3,4096]{1,0:T(4,128)S(1)}, u32[]{:S(2)}, u32[]{:S(2)}) collective-permute-start(f32[3,4096]{1,0:T(4,128)S(1)} %add.109), channel_id=1, source_target_pairs={{0,8},{2,10},{4,12},{6,14},{8,0},{10,2},{12,4},{14,6},{1,9},{3,11}... | collective-permute-start | bytes 147464 | tf_op jit(solution)/shard_map/ppermute | solution.py:204
  124.1 5.2 %collective-permute-start.16 = (f32[3,4096]{1,0:T(4,128)S(1)}, f32[3,4096]{1,0:T(4,128)S(1)}, u32[]{:S(2)}, u32[]{:S(2)}) collective-permute-start(f32[3,4096]{1,0:T(4,128)S(1)} %add.112), channel_id=1, source_target_pairs={{0,8},{2,10},{4,12},{6,14},{8,0},{10,2},{12,4},{14,6},{1,9},{3,11}... | collective-permute-start | bytes 147464 | tf_op jit(solution)/shard_map/ppermute | solution.py:204
  (2 other events, 13.0 us)

commit v2 on v0

v2 whole, which is shorter than its diff:
```python
import functools
import math

import jax
import jax.numpy as jnp
from jax import lax
from jax.experimental import pallas as pl
from jax.experimental.pallas import tpu as pltpu
from jax.sharding import PartitionSpec as P

I32, F32, BF16 = jnp.int32, jnp.float32, jnp.bfloat16
LANES = 128
HALF = 16
GROUP = 8
STRIDE = 9
CHUNK = 512
MIB = 2**20
LAST_DIMS = (((1,), (1,)), ((), ()))


def signed(word):
    return word - 2**32 if word >= 2**31 else word


def parity(bits, count):
    shift = 1
    while shift < count:
        shift *= 2
    while shift > 1:
        shift //= 2
        bits = bits ^ (bits >> shift)
    return bits & 1


def table_kernel(flips_ref, hidden_ref, *refs, examples):
    table_ref = refs[-1]
    tile = flips_ref.shape[0]
    words = [None, None]
    for column in range(flips_ref.shape[1] // LANES):
        bit, part = column // 2, column % 2
        flips = flips_ref[:, column * LANES:(column + 1) * LANES]
        term = (flips >> 1) & 1 if bit == 0 else flips & jnp.int32(1 << bit)
        words[part] = term if words[part] is None else words[part] | term
    for part in range(2):
        table_ref[pl.ds(examples + part, tile, stride=GROUP), :] = words[part].astype(F32)
    tokens = hidden_ref.shape[0] // examples
    for example in range(examples):
        block = hidden_ref[example * tokens:(example + 1) * tokens, :].astype(F32).T
        table_ref[pl.ds(example, tile, stride=GROUP), :] = block[:tile]


def build_table(sign_flips, hidden, table, examples, tile, span):
    rows, width = sign_flips.shape
    first, count = span
    lanes = -(-tile // LANES) * LANES
    in_specs = [
        pl.BlockSpec((tile, width), lambda i: (i + first, 0)),
        pl.BlockSpec((hidden.shape[0], lanes), lambda i: (0, i + first)),
    ]
    args = [sign_flips, hidden]
    aliases = {}
    if table is not None:
        in_specs.append(pl.BlockSpec(memory_space=pl.ANY))
        args.append(table)
        aliases = {2: 0}
    return pl.pallas_call(
        functools.partial(table_kernel, examples=examples),
        grid=(count,),
        in_specs=in_specs,
        out_specs=pl.BlockSpec((tile * GROUP, LANES), lambda i: (i + first, 0)),
        out_shape=jax.ShapeDtypeStruct((rows * GROUP, LANES), F32),
        input_output_aliases=aliases,
        compiler_params=pltpu.CompilerParams(vmem_limit_bytes=60 * MIB),
        cost_estimate=pl.CostEstimate(
            flops=2 * tile * count * width, bytes_accessed=4 * tile * count * width, transcendentals=0
        ),
        name="build_table",
    )(*args)


def hadamard_words(column):
    length = column.shape[1]
    lane = lax.broadcasted_iota(I32, (LANES, length), 0)
    words = -parity(lane & column, 7)

    def where_bit(bit, pattern):
        return -((column >> bit) & 1) & jnp.int32(signed(pattern))

    upper = where_bit(7, 0xFFFF0000)
    for bit, pattern in ((8, 0xAAAA), (9, 0xCCCC), (10, 0xF0F0), (11, 0xFF00)):
        upper = upper ^ where_bit(bit, pattern * 0x10001)
    return words ^ upper


def sign_columns(words, bits):
    pieces = []
    for bit in bits:
        for mask in (jnp.int32(1) << bit, jnp.int32(1) << (bit + HALF)):
            pieces.append(jnp.where((words & mask) != 0, -1.0, 1.0).astype(BF16))
    return jnp.concatenate(pieces, axis=1)


def project(scalars, cotangents, words, total):
    halves = cotangents[0].shape[1] // (2 * LANES)
    for at, cotangent in enumerate(cotangents):
        first = scalars[1 + at] * halves
        columns = sign_columns(words, [first + half for half in range(halves)])
        term = lax.dot_general(cotangent[...], columns, LAST_DIMS, preferred_element_type=F32)
        total = term if total is None else total + term
    return total


def sample_kernel(
    scalars, rows_ref, offsets_ref, table_ref, *refs, blocks, examples, length, sub, first, low_mask
):
    cotangents, (signs_ref, picked_ref, total_ref, held) = refs[:blocks], refs[blocks:]
    step = pl.program_id(0)
    slot = lax.rem(step, 2)

    def copy_row(chunk, at, target):
        row = pl.multiple_of(rows_ref[first + chunk * length + at], GROUP)
        held[target, pl.ds(at * STRIDE, GROUP), :] = table_ref[pl.ds(row, GROUP), :]

    @pl.when(step == 0)
    def _():
        unroll = 32

        def copy_group(group, _):
            for at in range(unroll):
                copy_row(0, group * unroll + at, 0)
            return 0

        lax.fori_loop(0, length // unroll, copy_group, 0)

    def column(row):
        return held[slot, pl.ds(row, length, stride=STRIDE), :]

    low, high = column(examples).astype(I32), column(examples + 1).astype(I32)
    words = (low | (high << HALF)) ^ hadamard_words(offsets_ref[...] & low_mask).T
    signs_ref[...] = words
    tokens = picked_ref.shape[0] // examples
    for example in range(examples):
        picked_ref[example * tokens:(example + 1) * tokens, :] = column(example).astype(BF16).T
    following = jnp.minimum(step + 1, pl.num_programs(0) - 1)
    for start in range(0, length, sub):
        for at in range(start, start + sub):
            copy_row(following, at, 1 - slot)
        total_ref[:, start:start + sub] = project(scalars, cotangents, words[start:start + sub], None)


def sample(scalars, rows, offsets, table, cotangents, examples, span, width):
    start, count = span
    tokens, depth = cotangents[0].shape
    length = CHUNK
    first = start // length
    whole = lambda i, *_: (0, 0)
    return pl.pallas_call(
        functools.partial(
            sample_kernel, blocks=len(cotangents), examples=examples, length=length, sub=length, first=start,
            low_mask=width - 1,
        ),
        grid_spec=pltpu.PrefetchScalarGridSpec(
            num_scalar_prefetch=2,
            grid=(count // length,),
            in_specs=[pl.BlockSpec((1, length), lambda i, *_: (0, i + first)), pl.BlockSpec(table.shape, whole)]
            + [pl.BlockSpec(piece.shape, whole) for piece in cotangents],
            out_specs=[
                pl.BlockSpec((length, LANES), lambda i, *_: (i, 0)),
                pl.BlockSpec((tokens, length), lambda i, *_: (0, i)),
                pl.BlockSpec((tokens, length), lambda i, *_: (0, i)),
            ],
            scratch_shapes=[pltpu.VMEM((2, length * STRIDE, LANES), F32)],
        ),
        out_shape=[
            jax.ShapeDtypeStruct((count, LANES), I32),
            jax.ShapeDtypeStruct((tokens, count), BF16),
            jax.ShapeDtypeStruct((tokens, count), F32),
        ],
        compiler_params=pltpu.CompilerParams(vmem_limit_bytes=48 * MIB),
        cost_estimate=pl.CostEstimate(
            flops=2 * tokens * depth * len(cotangents) * count, bytes_accessed=6 * tokens * count, transcendentals=0
        ),
        name="sample_rows",
    )(scalars, rows, offsets, table, *cotangents)


def finish_kernel(
    scalars, *refs, blocks, examples, length, sub, start, per_shard, parties, scale
):
    cotangents, (signs_ref, picked_ref, total_ref, out_ref) = refs[:blocks], refs[blocks:]
    for at in range(0, length, sub):
        spot = slice(at, at + sub)
        total = project(scalars, cotangents, signs_ref[spot, :], total_ref[:, spot])
        position = start + pl.program_id(0) * length + at + lax.broadcasted_iota(I32, (1, sub), 1)
        shard = position // per_shard
        sign = scale * (1 - 2 * parity(shard & scalars[0], parties.bit_length())).astype(F32)
        weighted = (total * picked_ref[:, spot].astype(F32)).reshape(examples, -1, sub)
        out_ref[:, spot] = jnp.sum(weighted, axis=1) * sign


def finish(scalars, cotangents, signs, picked, total, examples, start, per_shard, parties, scale):
    tokens, depth = cotangents[0].shape
    count = signs.shape[0]
    sub = CHUNK // 2
    length = count // 2 if count % (2 * sub) == 0 else count
    across = lambda i, _: (0, i)
    return pl.pallas_call(
        functools.partial(
            finish_kernel, blocks=len(cotangents), examples=examples, length=length, sub=sub, start=start,
            per_shard=per_shard, parties=parties, scale=scale,
        ),
        grid_spec=pltpu.PrefetchScalarGridSpec(
            num_scalar_prefetch=1,
            grid=(count // length,),
            in_specs=[pl.BlockSpec(piece.shape, lambda i, _: (0, 0)) for piece in cotangents]
            + [
                pl.BlockSpec((length, LANES), lambda i, _: (i, 0)),
                pl.BlockSpec((tokens, length), across),
                pl.BlockSpec((tokens, length), across),
            ],
            out_specs=pl.BlockSpec((examples, length), across),
        ),
        out_shape=jax.ShapeDtypeStruct((examples, count), F32),
        compiler_params=pltpu.CompilerParams(vmem_limit_bytes=48 * MIB),
        cost_estimate=pl.CostEstimate(
            flops=2 * tokens * depth * len(cotangents) * count, bytes_accessed=6 * tokens * count, transcendentals=0
        ),
        name="finish_blocks",
    )(scalars, *cotangents, signs, picked, total)


def by_xor(parties, step):
    return [(source, source ^ step) for source in range(parties)]


def sum_shards(values, parties):
    step = 1
    while step < parties:
        values = values + lax.ppermute(values, "param", by_xor(parties, step))
        step *= 2
    return values


def local(hidden, cotangent, sign_flips, offsets):
    examples, tokens, rows = hidden.shape
    width = sign_flips.shape[1]
    parties = lax.axis_size("param")
    own = lax.axis_index("param").astype(I32)
    per_shard = offsets.shape[0]
    count = per_shard * parties
    scale = 1.0 / math.sqrt(parties * width)
    flat = examples * tokens
    depth = cotangent.shape[2]
    held = cotangent.reshape(flat, depth)

    units = hidden.reshape(flat, rows)
    if rows % LANES:
        units = jnp.pad(units, ((0, 0), (0, -rows % LANES)))
    tile = 2 * LANES if rows % (2 * LANES) == 0 else LANES if rows % LANES == 0 else rows
    tiles = rows // tile
    table, built, step = None, 0, 1
    ringed = depth % (2 * LANES) == 0 and parties % 2 == 0
    steps = parties.bit_length() - 1
    for at in range(steps):
        other = lax.ppermute(offsets, "param", by_xor(parties, step))
        until = -(-tiles * (at + 1) // steps)
        if until > built:
            table = build_table(sign_flips, units, table, examples, tile, (built, until - built))
            built = until
            table, other = lax.optimization_barrier((table, other))
        if at == 0:
            held, other = lax.optimization_barrier((held, other))
        offsets = jnp.where(
            (own & step) == 0, jnp.concatenate([offsets, other]), jnp.concatenate([other, offsets])
        )
        step *= 2

    row_shift = width.bit_length() - 1
    unit_rows = (offsets >> row_shift) * GROUP
    line = offsets.reshape(1, count)
    chunks = count // CHUNK
    bounds = [at * chunks // 3 * CHUNK for at in range(4)]
    spans = [(start, end - start) for start, end in zip(bounds, bounds[1:])]
    pieces, numbers, sampled = [held], [own], []

    def scalars(first, last):
        return jnp.stack([own] + numbers[first:last])

    def sample_next():
        return sample(
            scalars(0, len(pieces)), unit_rows, line, table, pieces, examples, spans[len(sampled)], width
        ), len(pieces)

    if ringed:
        order = list(range(0, parties, 2)) + list(range(parties - 1, 0, -2))
        forward = [(order[at], order[(at + 1) % parties]) for at in range(parties)]
        backward = [(target, source) for source, target in forward]
        place = jnp.where(own % 2 == 0, own // 2, parties - 1 - own // 2)

        def shard_at(spot):
            spot = (spot + parties) % parties
            return jnp.where(spot < parties // 2, 2 * spot, 2 * (parties - spot) - 1)

        ahead = behind = held
        for step in range(1, parties // 2):
            ahead = lax.ppermute(ahead, "param", forward)
            behind = lax.ppermute(behind, "param", backward)
            if step > 1 and len(sampled) < 3:
                sampled.append(sample_next())
                (signs, picked, total), used = sampled[-1]
                ahead, behind, signs = lax.optimization_barrier((ahead, behind, signs))
                sampled[-1] = (signs, picked, total), used
            pieces += [ahead, behind]
            numbers += [shard_at(place - step), shard_at(place + step)]
        middle = flat // 2
        ahead = lax.ppermute(ahead[:middle], "param", forward)
        behind = lax.ppermute(behind[middle:], "param", backward)
        last = jnp.concatenate([ahead, behind], axis=0)
        last_number = shard_at(place + parties // 2)
    else:
        whole = lax.all_gather(cotangent, "param", axis=2, tiled=True).reshape(flat, width)
        span = 4 * LANES
        pieces = [whole[:, at:at + span] for at in range(0, width - span, span)]
        numbers = [jnp.int32(at) for at in range(len(pieces))]
        last, last_number = whole[:, width - span:], jnp.int32(len(pieces))

    while len(sampled) < 3:
        sampled.append(sample_next())
    pieces.append(last)
    numbers.append(last_number)
    values = [
        finish(
            scalars(used, len(pieces)), pieces[used:], signs, picked, total, examples, start, per_shard, parties, scale
        )
        for ((signs, picked, total), used), (start, _) in zip(sampled, spans)
    ]
    parts = [values[0], jnp.concatenate(values[1:], axis=1)]
    return jnp.concatenate([sum_shards(part, parties) for part in parts], axis=1)


def solution(mesh):
    return jax.shard_map(
        local,
        mesh=mesh,
        in_specs=(
            P(("groups", "dp"), None, "param"),
            P(("groups", "dp"), None, "param"),
            P("param", None),
            P("param"),
        ),
        out_specs=P(("groups", "dp"), None),
        check_vma=False,
    )
```

time: 513 us -> 123 us (0.24)
  local copies, waits for them, and re-layouts: 234 us -> 4.47 us
  matrix products: 153 us -> 0 us
  Pallas kernels: 0 us -> 79.9 us
  blocking collectives: 63.3 us -> 0 us
  other arithmetic: 17.9 us -> 1.1 us
  starting transfers between devices: 3.37 us -> 19.1 us
  between operations: 13.5 us -> 0.18 us
  waiting for transfers between devices: 25.5 us -> 17.7 us
    dot_general x4 -> x0, matrix products: 153 us -> none  [the longest x1 81.5 us: local(): jnp.einsum('ab,erbc->erac', outer_table, section_one, precision=lax.Preci...]
    unnamed x13 -> x15, local copies, waits for them, and re-layouts: 141 us -> 4.17 us
    gather x1 -> x0, local copies, waits for them, and re-layouts: 92.6 us -> none  [local(): jnp.take(flattened, all_offsets, axis=1)]
    pallas_call x0 -> x9, Pallas kernels: none -> 79.9 us  [the longest x3 43.8 us: sample(): pl.pallas_call(functools.partial(sample_kernel, blocks=len(cotangents), e...]
    all_gather x2 -> x0, blocking collectives: 63.3 us -> none  [the longest x1 32.7 us: local(): all_offsets = lax.all_gather(offsets, 'param', axis=0, tiled=True)]
    ppermute x0 -> x17, starting transfers between devices: none -> 19.1 us  [the longest x3 7.23 us: local(): other = lax.ppermute(offsets, 'param', by_xor(parties, step))]
    ppermute x0 -> x17, waiting for transfers between devices: none -> 17.7 us  [the longest x6 14.6 us: sum_shards(): values = values + lax.ppermute(values, 'param', by_xor(parties, step))]
    all_gather x1 -> x0, waiting for transfers between devices: 17.5 us -> none  [local(): lax.all_gather(cotangent, 'param', axis=2, tiled=True)]
  transfers between devices with their start and end apart: 2 -> 17, of which waited for: 2 -> 5; matrix products, arithmetic and copies ran while one was open for 4% -> 0% of each run, Pallas kernels for 0% -> 57%
where the time goes in v2:
time: 123 us; the launch traced here: 122 us
  Pallas kernels  79.9 us (65%)
  starting transfers between devices  19.1 us (16%)
  waiting for transfers between devices  17.7 us (14%)
  local copies, waits for them, and re-layouts  4.47 us (4%)
    pallas_call x3, Pallas kernels, sample(): pl.pallas_call(functools.partial(sample_kernel, blocks=len(cotangents), e...  43.8 us
    pallas_call x3, Pallas kernels, finish(): pl.pallas_call(functools.partial(finish_kernel, blocks=len(cotangents), e...  18.3 us
    pallas_call x3, Pallas kernels, build_table(): pl.pallas_call(functools.partial(table_kernel, examples=examples), grid=(...  17.8 us
    ppermute x6, waiting for transfers between devices, sum_shards(): values = values + lax.ppermute(values, 'param', by_xor(parties, step))  14.6 us
    ppermute x3, starting transfers between devices, local(): other = lax.ppermute(offsets, 'param', by_xor(parties, step))  7.23 us
    unnamed x15, local copies, waits for them, and re-layouts  4.17 us
    ppermute x3, starting transfers between devices, local(): ahead = lax.ppermute(ahead, 'param', forward)  3.84 us
    ppermute x6, starting transfers between devices, sum_shards(): values = values + lax.ppermute(values, 'param', by_xor(parties, step))  3.63 us
  transfers between devices with their start and end apart: 17, of which 5 were waited for; matrix products, arithmetic and copies ran while one was open for 0% of the time, Pallas kernels for 57%

profile of v2, /device:TPU:0, one launch (start us, length us, event | category | flops | bytes accessed | tf_op | source)
XLA Modules:
  0.0 122.4 jit_solution(13328842933639517978)
XLA Ops:
  0.0 2.9 %collective-permute-start = (s32[1024]{0:T(1024)}, s32[1024]{0:T(1024)S(1)}, u32[]{:S(2)}, u32[]{:S(2)}) collective-permute-start(s32[1024]{0:T(1024)} %param.7), channel_id=1, source_target_pairs={{0,2},{2,0},{4,6},{6,4},{8,10},{10,8},{12,14},{14,12},{1,3},{3,1},... | collective-permute-start | bytes 12296 | tf_op jit(solution)/shard_map/ppermute | solution.py:265
  3.0 7.5 %build_table.3.refs_0_ = f32[14336,128]{1,0:T(8,128)} custom-call(s32[1792,4096]{1,0:T(8,128)} %flips_ref.5, bf16[384,1792]{1,0:T(8,128)(2,1)} %bitcast.17), custom_call_target="tpu_custom_call" | custom-call | flops 6291456 | bytes 12582912 | tf_op jit(solution)/shard_map/build_table/pallas_call | solution.py:66
  10.6 1.6 %collective-permute-start.5 = (s32[2048]{0:T(1024)S(1)}, s32[2048]{0:T(1024)S(1)}, u32[]{:S(2)}, u32[]{:S(2)}) collective-permute-start(s32[2048]{0:T(1024)S(1)} %add_select_fusion.2), channel_id=1, source_target_pairs={{0,4},{2,6},{4,0},{6,2},{8,12},{10,14},{12,8},{14,10},{1,5},{3,7},... | collective-permute-start | bytes 24584 | tf_op jit(solution)/shard_map/ppermute | solution.py:265
  12.3 5.2 %build_table.4.refs_0_ = f32[14336,128]{1,0:T(8,128)} custom-call(s32[1792,4096]{1,0:T(8,128)} %flips_ref.5, bf16[384,1792]{1,0:T(8,128)(2,1)} %bitcast.18, f32[14336,128]{1,0:T(8,128)} %build_table.3.refs_0_), custom_call_target="tpu_custom_call", output_to_operand_aliasing={{}: (2, {})} | custom-call | flops 4194304 | bytes 8388608 | tf_op jit(solution)/shard_map/build_table/pallas_call | solution.py:66
  17.5 2.7 %collective-permute-start.6 = (s32[4096]{0:T(1024)S(1)}, s32[4096]{0:T(1024)S(1)}, u32[]{:S(2)}, u32[]{:S(2)}) collective-permute-start(s32[4096]{0:T(1024)S(1)} %add_select_fusion.1), channel_id=1, source_target_pairs={{0,8},{2,10},{4,12},{6,14},{8,0},{10,2},{12,4},{14,6},{1,9},{3,11}... | collective-permute-start | bytes 49160 | tf_op jit(solution)/shard_map/ppermute | solution.py:265
  20.9 1.5 %collective-permute-start.1 = (bf16[384,512]{1,0:T(8,128)(2,1)S(1)}, bf16[384,512]{1,0:T(8,128)(2,1)S(1)}, u32[]{:S(2)}, u32[]{:S(2)}) collective-permute-start(bf16[384,512]{1,0:T(8,128)(2,1)S(1)} %bitcast.13), channel_id=1, source_target_pairs={{0,4},{4,8},{8,12},{12,14},{14,10},{10,6},{6,2},{2,0},{1,5},{5,9},... | collective-permute-start | bytes 1179656 | tf_op jit(solution)/shard_map/ppermute | solution.py:306
  22.4 5.1 %build_table.5.table_ref = f32[14336,128]{1,0:T(8,128)} custom-call(s32[1792,4096]{1,0:T(8,128)} %flips_ref.5, bf16[384,1792]{1,0:T(8,128)(2,1)} %bitcast.19, f32[14336,128]{1,0:T(8,128)} %build_table.4.refs_0_), custom_call_target="tpu_custom_call", output_to_operand_aliasing={{}: (2, {})} | custom-call | flops 4194304 | bytes 8388608 | tf_op jit(solution)/shard_map/build_table/pallas_call | solution.py:66
  27.5 3.0 %collective-permute-done.3.refs_2_ = bf16[384,512]{1,0:T(8,128)(2,1)S(1)} collective-permute-done((bf16[384,512]{1,0:T(8,128)(2,1)S(1)}, bf16[384,512]{1,0:T(8,128)(2,1)S(1)}, u32[]{:S(2)}, u32[]{:S(2)}) %collective-permute-start.3) | collective-permute-done | bytes 393248 | tf_op jit(solution)/shard_map/ppermute | solution.py:307
  31.0 1.7 %collective-permute-start.2 = (bf16[384,512]{1,0:T(8,128)(2,1)S(1)}, bf16[384,512]{1,0:T(8,128)(2,1)S(1)}, u32[]{:S(2)}, u32[]{:S(2)}) collective-permute-start(bf16[384,512]{1,0:T(8,128)(2,1)S(1)} %collective-permute-done.1.refs_1_), channel_id=1, source_target_pairs={{0,4},{4,8},{8,12},{12,14},{14,10},{10,6},{6,2},{2,0},{1,5},{5,9},... | collective-permute-start | bytes 1179656 | tf_op jit(solution)/shard_map/ppermute | solution.py:306
  32.6 11.9 %sample_rows.3 = (s32[2560,128]{1,0:T(8,128)S(1)}, bf16[384,2560]{1,0:T(8,128)(2,1)S(1)}, f32[384,2560]{1,0:T(8,128)}) custom-call(s32[4]{0:T(128)S(1)} %pad_add_fusion.scalars, s32[8192]{0:T(1024)S(1)} %fusion.1.rows_ref, s32[1,8192]{1,0:T(1,128)S(1)} %broadcast_select_fusion.offsets_ref, f32[14336,128]{1,0:T(8,128)} %build_table.5.table_ref, ...), custom_call_target="tpu_custom_call" | custom-call | flops 3019898880 | bytes 5898240 | tf_op jit(solution)/shard_map/sample_rows/pallas_call | solution.py:157
  46.5 1.4 %collective-permute-start.8 = (bf16[384,512]{1,0:T(8,128)(2,1)S(1)}, bf16[384,512]{1,0:T(8,128)(2,1)S(1)}, u32[]{:S(2)}, u32[]{:S(2)}) collective-permute-start(bf16[384,512]{1,0:T(8,128)(2,1)S(1)} %collective-permute-done.4.refs_4_.refs_1_), channel_id=1, source_target_pairs={{4,0},{8,4},{12,8},{14,12},{10,14},{6,10},{2,6},{0,2},{5,1},{9,5},... | collective-permute-start | bytes 1179656 | tf_op jit(solution)/shard_map/ppermute | solution.py:307
  47.9 13.9 %sample_rows.4 = (s32[2560,128]{1,0:T(8,128)S(1)}, bf16[384,2560]{1,0:T(8,128)(2,1)S(1)}, f32[384,2560]{1,0:T(8,128)}) custom-call(s32[6]{0:T(128)S(1)} %stack.74.scalars, s32[8192]{0:T(1024)S(1)} %fusion.1.rows_ref, s32[1,8192]{1,0:T(1,128)S(1)} %broadcast_select_fusion.offsets_ref, f32[14336,128]{1,0:T(8,128)} %build_table.5.table_ref, ...), custom_call_target="tpu_custom_call" | custom-call | flops 5033164800 | bytes 5898240 | tf_op jit(solution)/shard_map/sample_rows/pallas_call | solution.py:157
  62.3 1.7 %collective-permute-start.9 = (bf16[192,512]{1,0:T(8,128)(2,1)S(1)}, bf16[192,512]{1,0:T(8,128)(2,1)S(1)}, u32[]{:S(2)}, u32[]{:S(2)}) collective-permute-start(bf16[192,512]{1,0:T(8,128)(2,1)S(1)} %slice.6), channel_id=1, source_target_pairs={{0,4},{4,8},{8,12},{12,14},{14,10},{10,6},{6,2},{2,0},{1,5},{5,9},... | collective-permute-start | bytes 589832 | tf_op jit(solution)/shard_map/ppermute | solution.py:316
  63.9 18.0 %sample_rows.5 = (s32[3072,128]{1,0:T(8,128)S(1)}, bf16[384,3072]{1,0:T(8,128)(2,1)}, f32[384,3072]{1,0:T(8,128)}) custom-call(s32[8]{0:T(128)S(1)} %stack.77.scalars, s32[8192]{0:T(1024)S(1)} %fusion.1.rows_ref, s32[1,8192]{1,0:T(1,128)S(1)} %broadcast_select_fusion.offsets_ref, f32[14336,128]{1,0:T(8,128)} %build_table.5.table_ref, ...), custom_call_target="tpu_custom_call" | custom-call | flops 8455716864 | bytes 7077888 | tf_op jit(solution)/shard_map/sample_rows/pallas_call | solution.py:157
  82.0 6.0 %finish_blocks.4 = f32[3,2560]{1,0:T(4,128)S(1)} custom-call(s32[4]{0:T(128)S(1)} %pad_add_fusion.1.scalars, bf16[384,512]{1,0:T(8,128)(2,1)S(1)} %collective-permute-done.7.refs_2_.refs_0_.refs_5_, bf16[384,512]{1,0:T(8,128)(2,1)S(1)} %collective-permute-done.8.refs_3_.refs_1_.refs_6_, ...), custom_call_target="tpu_custom_call" | custom-call | flops 3019898880 | bytes 5898240 | tf_op jit(solution)/shard_map/finish_blocks/pallas_call | solution.py:207
  88.1 4.3 %finish_blocks.5 = f32[3,3072]{1,0:T(4,128)S(1)} custom-call(s32[2]{0:T(128)S(1)} %pad_add_fusion.2.scalars, bf16[384,512]{1,0:T(8,128)(2,1)S(1)} %constant_dynamic-update-slice_fusion.refs_4_.refs_2_.refs_0_, s32[3072,128]{1,0:T(8,128)S(1)} %get-tuple-element.48.refs_1_, bf16[384,3072]{1,0:T(8,128)(2,1)S(1)} %copy-done, f32[384,3072]{1,0:T(8,128)} %get-tuple-element.50.refs_3_), custom_call_target="tpu_custom_call" | custom-call | flops 1207959552 | bytes 7077888 | tf_op jit(solution)/shard_map/finish_blocks/pallas_call | solution.py:207
  92.9 4.1 %collective-permute-done.14 = f32[3,5632]{1,0:T(4,128)S(1)} collective-permute-done((f32[3,5632]{1,0:T(4,128)S(1)}, f32[3,5632]{1,0:T(4,128)S(1)}, u32[]{:S(2)}, u32[]{:S(2)}) %collective-permute-start.14) | collective-permute-done | bytes 67616 | tf_op jit(solution)/shard_map/ppermute | solution.py:239
  97.7 1.5 %copy-done.3 = bf16[384,2560]{1,0:T(8,128)(2,1)S(1)} copy-done((bf16[384,2560]{1,0:T(8,128)(2,1)S(1)}, bf16[384,2560]{1,0:T(8,128)(2,1)}, u32[]{:S(2)}) %copy-start.3) | copy-done | bytes 1966104
  99.3 1.3 %copy-done.5 = s32[2560,128]{1,0:T(8,128)S(1)} copy-done((s32[2560,128]{1,0:T(8,128)S(1)}, s32[2560,128]{1,0:T(8,128)}, u32[]{:S(2)}) %copy-start.5) | copy-done | bytes 1310744
  100.6 7.9 %finish_blocks.3 = f32[3,2560]{1,0:T(4,128)S(1)} custom-call(s32[6]{0:T(128)S(1)} %stack.34.scalars, bf16[384,512]{1,0:T(8,128)(2,1)S(1)} %collective-permute-done.2.refs_3_.refs_0_, bf16[384,512]{1,0:T(8,128)(2,1)S(1)} %collective-permute-done.4.refs_4_.refs_1_, bf16[384,512]{1,0:T(8,128)(2,1)S(1)} %collective-permute-done.7.refs_2_.refs_0_.refs_5_, ...), custom_call_target="tpu_custom_call" | custom-call | flops 5033164800 | bytes 5898240 | tf_op jit(solution)/shard_map/finish_blocks/pallas_call | solution.py:207
  109.6 3.1 %collective-permute-done.11 = f32[3,2560]{1,0:T(4,128)S(1)} collective-permute-done((f32[3,2560]{1,0:T(4,128)S(1)}, f32[3,2560]{1,0:T(4,128)S(1)}, u32[]{:S(2)}, u32[]{:S(2)}) %collective-permute-start.11) | collective-permute-done | bytes 30752 | tf_op jit(solution)/shard_map/ppermute | solution.py:239
  112.6 1.5 %collective-permute-start.12 = (f32[3,2560]{1,0:T(4,128)S(1)}, f32[3,2560]{1,0:T(4,128)S(1)}, u32[]{:S(2)}, u32[]{:S(2)}) collective-permute-start(f32[3,2560]{1,0:T(4,128)S(1)} %add.108), channel_id=1, source_target_pairs={{0,4},{2,6},{4,0},{6,2},{8,12},{10,14},{12,8},{14,10},{1,5},{3,7},... | collective-permute-start | bytes 92168 | tf_op jit(solution)/shard_map/ppermute | solution.py:239
  114.1 2.6 %collective-permute-done.12 = f32[3,2560]{1,0:T(4,128)S(1)} collective-permute-done((f32[3,2560]{1,0:T(4,128)S(1)}, f32[3,2560]{1,0:T(4,128)S(1)}, u32[]{:S(2)}, u32[]{:S(2)}) %collective-permute-start.12) | collective-permute-done | bytes 30752 | tf_op jit(solution)/shard_map/ppermute | solution.py:239
  116.8 4.9 %collective-permute-done.13 = f32[3,2560]{1,0:T(4,128)S(1)} collective-permute-done((f32[3,2560]{1,0:T(4,128)S(1)}, f32[3,2560]{1,0:T(4,128)S(1)}, u32[]{:S(2)}, u32[]{:S(2)}) %collective-permute-start.13) | collective-permute-done | bytes 30752 | tf_op jit(solution)/shard_map/ppermute | solution.py:239
  (55 shorter events, 6.9 us)
Async XLA Ops:
  0.0 10.5 %collective-permute-start = (s32[1024]{0:T(1024)}, s32[1024]{0:T(1024)S(1)}, u32[]{:S(2)}, u32[]{:S(2)}) collective-permute-start(s32[1024]{0:T(1024)} %param.7), channel_id=1, source_target_pairs={{0,2},{2,0},{4,6},{6,4},{8,10},{10,8},{12,14},{14,12},{1,3},{3,1},... | collective-permute-start | bytes 12296 | tf_op jit(solution)/shard_map/ppermute | solution.py:265
  3.0 7.5 %copy-start.6 = (s32[1024]{0:T(1024)S(1)}, s32[1024]{0:T(1024)}, u32[]{:S(2)}) copy-start(s32[1024]{0:T(1024)} %param.7) | copy-start | bytes 12292
  10.6 6.9 %collective-permute-start.5 = (s32[2048]{0:T(1024)S(1)}, s32[2048]{0:T(1024)S(1)}, u32[]{:S(2)}, u32[]{:S(2)}) collective-permute-start(s32[2048]{0:T(1024)S(1)} %add_select_fusion.2), channel_id=1, source_target_pairs={{0,4},{2,6},{4,0},{6,2},{8,12},{10,14},{12,8},{14,10},{1,5},{3,7},... | collective-permute-start | bytes 24584 | tf_op jit(solution)/shard_map/ppermute | solution.py:265
  12.3 8.1 %copy-start.1 = (bf16[3,128,512]{2,1,0:T(8,128)(2,1)S(1)}, bf16[3,128,512]{2,1,0:T(8,128)(2,1)}, u32[]{:S(2)}) copy-start(bf16[3,128,512]{2,1,0:T(8,128)(2,1)} %param.5) | copy-start | bytes 1179652
  17.5 10.0 %collective-permute-start.6 = (s32[4096]{0:T(1024)S(1)}, s32[4096]{0:T(1024)S(1)}, u32[]{:S(2)}, u32[]{:S(2)}) collective-permute-start(s32[4096]{0:T(1024)S(1)} %add_select_fusion.1), channel_id=1, source_target_pairs={{0,8},{2,10},{4,12},{6,14},{8,0},{10,2},{12,4},{14,6},{1,9},{3,11}... | collective-permute-start | bytes 49160 | tf_op jit(solution)/shard_map/ppermute | solution.py:265
  20.4 10.2 %collective-permute-start.3 = (bf16[384,512]{1,0:T(8,128)(2,1)S(1)}, bf16[384,512]{1,0:T(8,128)(2,1)S(1)}, u32[]{:S(2)}, u32[]{:S(2)}) collective-permute-start(bf16[384,512]{1,0:T(8,128)(2,1)S(1)} %bitcast.12), channel_id=1, source_target_pairs={{4,0},{8,4},{12,8},{14,12},{10,14},{6,10},{2,6},{0,2},{5,1},{9,5},... | collective-permute-start | bytes 1179656 | tf_op jit(solution)/shard_map/ppermute | solution.py:307
  20.9 10.0 %collective-permute-start.1 = (bf16[384,512]{1,0:T(8,128)(2,1)S(1)}, bf16[384,512]{1,0:T(8,128)(2,1)S(1)}, u32[]{:S(2)}, u32[]{:S(2)}) collective-permute-start(bf16[384,512]{1,0:T(8,128)(2,1)S(1)} %bitcast.13), channel_id=1, source_target_pairs={{0,4},{4,8},{8,12},{12,14},{14,10},{10,6},{6,2},{2,0},{1,5},{5,9},... | collective-permute-start | bytes 1179656 | tf_op jit(solution)/shard_map/ppermute | solution.py:306
  30.6 15.2 %collective-permute-start.4 = (bf16[384,512]{1,0:T(8,128)(2,1)S(1)}, bf16[384,512]{1,0:T(8,128)(2,1)S(1)}, u32[]{:S(2)}, u32[]{:S(2)}) collective-permute-start(bf16[384,512]{1,0:T(8,128)(2,1)S(1)} %collective-permute-done.3.refs_2_), channel_id=1, source_target_pairs={{4,0},{8,4},{12,8},{14,12},{10,14},{6,10},{2,6},{0,2},{5,1},{9,5},... | collective-permute-start | bytes 1179656 | tf_op jit(solution)/shard_map/ppermute | solution.py:307
  31.0 14.9 %collective-permute-start.2 = (bf16[384,512]{1,0:T(8,128)(2,1)S(1)}, bf16[384,512]{1,0:T(8,128)(2,1)S(1)}, u32[]{:S(2)}, u32[]{:S(2)}) collective-permute-start(bf16[384,512]{1,0:T(8,128)(2,1)S(1)} %collective-permute-done.1.refs_1_), channel_id=1, source_target_pairs={{0,4},{4,8},{8,12},{12,14},{14,10},{10,6},{6,2},{2,0},{1,5},{5,9},... | collective-permute-start | bytes 1179656 | tf_op jit(solution)/shard_map/ppermute | solution.py:306
  44.5 1.3 %copy-start.2 = (bf16[384,2560]{1,0:T(8,128)(2,1)}, bf16[384,2560]{1,0:T(8,128)(2,1)S(1)}, u32[]{:S(2)}) copy-start(bf16[384,2560]{1,0:T(8,128)(2,1)S(1)} %get-tuple-element.43.refs_6_) | copy-start | bytes 5898244
  45.8 16.0 %copy-start.4 = (s32[2560,128]{1,0:T(8,128)}, s32[2560,128]{1,0:T(8,128)S(1)}, u32[]{:S(2)}) copy-start(s32[2560,128]{1,0:T(8,128)S(1)} %get-tuple-element.42.refs_5_) | copy-start | bytes 3932164
  45.8 16.0 %collective-permute-start.7 = (bf16[384,512]{1,0:T(8,128)(2,1)S(1)}, bf16[384,512]{1,0:T(8,128)(2,1)S(1)}, u32[]{:S(2)}, u32[]{:S(2)}) collective-permute-start(bf16[384,512]{1,0:T(8,128)(2,1)S(1)} %collective-permute-done.2.refs_3_.refs_0_), channel_id=1, source_target_pairs={{0,4},{4,8},{8,12},{12,14},{14,10},{10,6},{6,2},{2,0},{1,5},{5,9},... | collective-permute-start | bytes 1179656 | tf_op jit(solution)/shard_map/ppermute | solution.py:306
  46.5 15.3 %collective-permute-start.8 = (bf16[384,512]{1,0:T(8,128)(2,1)S(1)}, bf16[384,512]{1,0:T(8,128)(2,1)S(1)}, u32[]{:S(2)}, u32[]{:S(2)}) collective-permute-start(bf16[384,512]{1,0:T(8,128)(2,1)S(1)} %collective-permute-done.4.refs_4_.refs_1_), channel_id=1, source_target_pairs={{4,0},{8,4},{12,8},{14,12},{10,14},{6,10},{2,6},{0,2},{5,1},{9,5},... | collective-permute-start | bytes 1179656 | tf_op jit(solution)/shard_map/ppermute | solution.py:307
  61.9 20.1 %collective-permute-start.10 = (bf16[192,512]{1,0:T(8,128)(2,1)S(1)}, bf16[192,512]{1,0:T(8,128)(2,1)S(1)}, u32[]{:S(2)}, u32[]{:S(2)}) collective-permute-start(bf16[192,512]{1,0:T(8,128)(2,1)S(1)} %slice.7), channel_id=1, source_target_pairs={{4,0},{8,4},{12,8},{14,12},{10,14},{6,10},{2,6},{0,2},{5,1},{9,5},... | collective-permute-start | bytes 589832 | tf_op jit(solution)/shard_map/ppermute | solution.py:317
  62.3 19.7 %collective-permute-start.9 = (bf16[192,512]{1,0:T(8,128)(2,1)S(1)}, bf16[192,512]{1,0:T(8,128)(2,1)S(1)}, u32[]{:S(2)}, u32[]{:S(2)}) collective-permute-start(bf16[192,512]{1,0:T(8,128)(2,1)S(1)} %slice.6), channel_id=1, source_target_pairs={{0,4},{4,8},{8,12},{12,14},{14,10},{10,6},{6,2},{2,0},{1,5},{5,9},... | collective-permute-start | bytes 589832 | tf_op jit(solution)/shard_map/ppermute | solution.py:316
  82.0 6.0 %copy-start = (bf16[384,3072]{1,0:T(8,128)(2,1)S(1)}, bf16[384,3072]{1,0:T(8,128)(2,1)}, u32[]{:S(2)}) copy-start(bf16[384,3072]{1,0:T(8,128)(2,1)} %get-tuple-element.49.refs_2_) | copy-start | bytes 7077892
  92.4 4.6 %collective-permute-start.14 = (f32[3,5632]{1,0:T(4,128)S(1)}, f32[3,5632]{1,0:T(4,128)S(1)}, u32[]{:S(2)}, u32[]{:S(2)}) collective-permute-start(f32[3,5632]{1,0:T(4,128)S(1)} %pad_maximum_fusion.1), channel_id=1, source_target_pairs={{0,2},{2,0},{4,6},{6,4},{8,10},{10,8},{12,14},{14,12},{1,3},{3,1},... | collective-permute-start | bytes 202760 | tf_op jit(solution)/shard_map/ppermute | solution.py:239
  97.1 11.9 %collective-permute-start.15 = (f32[3,5632]{1,0:T(4,128)S(1)}, f32[3,5632]{1,0:T(4,128)S(1)}, u32[]{:S(2)}, u32[]{:S(2)}) collective-permute-start(f32[3,5632]{1,0:T(4,128)S(1)} %fusion.2), channel_id=1, source_target_pairs={{0,4},{2,6},{4,0},{6,2},{8,12},{10,14},{12,8},{14,10},{1,5},{3,7},... | collective-permute-start | bytes 202760 | tf_op jit(solution)/shard_map/ppermute | solution.py:239
  97.7 1.5 %copy-start.3 = (bf16[384,2560]{1,0:T(8,128)(2,1)S(1)}, bf16[384,2560]{1,0:T(8,128)(2,1)}, u32[]{:S(2)}) copy-start(bf16[384,2560]{1,0:T(8,128)(2,1)} %copy-done.2) | copy-start | bytes 5898244
  99.3 1.3 %copy-start.5 = (s32[2560,128]{1,0:T(8,128)S(1)}, s32[2560,128]{1,0:T(8,128)}, u32[]{:S(2)}) copy-start(s32[2560,128]{1,0:T(8,128)} %copy-done.4) | copy-start | bytes 3932164
  108.6 4.1 %collective-permute-start.11 = (f32[3,2560]{1,0:T(4,128)S(1)}, f32[3,2560]{1,0:T(4,128)S(1)}, u32[]{:S(2)}, u32[]{:S(2)}) collective-permute-start(f32[3,2560]{1,0:T(4,128)S(1)} %finish_blocks.3), channel_id=1, source_target_pairs={{0,2},{2,0},{4,6},{6,4},{8,10},{10,8},{12,14},{14,12},{1,3},{3,1},... | collective-permute-start | bytes 92168 | tf_op jit(solution)/shard_map/ppermute | solution.py:239
  109.0 12.7 %collective-permute-start.16 = (f32[3,5632]{1,0:T(4,128)S(1)}, f32[3,5632]{1,0:T(4,128)S(1)}, u32[]{:S(2)}, u32[]{:S(2)}) collective-permute-start(f32[3,5632]{1,0:T(4,128)S(1)} %add.112), channel_id=1, source_target_pairs={{0,8},{2,10},{4,12},{6,14},{8,0},{10,2},{12,4},{14,6},{1,9},{3,11}... | collective-permute-start | bytes 202760 | tf_op jit(solution)/shard_map/ppermute | solution.py:239
  112.6 4.1 %collective-permute-start.12 = (f32[3,2560]{1,0:T(4,128)S(1)}, f32[3,2560]{1,0:T(4,128)S(1)}, u32[]{:S(2)}, u32[]{:S(2)}) collective-permute-start(f32[3,2560]{1,0:T(4,128)S(1)} %add.108), channel_id=1, source_target_pairs={{0,4},{2,6},{4,0},{6,2},{8,12},{10,14},{12,8},{14,10},{1,5},{3,7},... | collective-permute-start | bytes 92168 | tf_op jit(solution)/shard_map/ppermute | solution.py:239
  116.7 5.0 %collective-permute-start.13 = (f32[3,2560]{1,0:T(4,128)S(1)}, f32[3,2560]{1,0:T(4,128)S(1)}, u32[]{:S(2)}, u32[]{:S(2)}) collective-permute-start(f32[3,2560]{1,0:T(4,128)S(1)} %add.109), channel_id=1, source_target_pairs={{0,8},{2,10},{4,12},{6,14},{8,0},{10,2},{12,4},{14,6},{1,9},{3,11}... | collective-permute-start | bytes 92168 | tf_op jit(solution)/shard_map/ppermute | solution.py:239

commit v3 on v2

v3 whole, which is shorter than its diff:
```python
import functools
import math

import jax
import jax.numpy as jnp
from jax import lax
from jax.experimental import pallas as pl
from jax.experimental.pallas import tpu as pltpu
from jax.sharding import PartitionSpec as P

I32, F32, BF16 = jnp.int32, jnp.float32, jnp.bfloat16
LANES = 128
HALF = 16
SIGN_ROWS = 2
EARLY = ()
CHUNK = 512
MIB = 2**20
LAST_DIMS = (((1,), (1,)), ((), ()))


def signed(word):
    return word - 2**32 if word >= 2**31 else word


def parity(bits, count):
    shift = 1
    while shift < count:
        shift *= 2
    while shift > 1:
        shift //= 2
        bits = bits ^ (bits >> shift)
    return bits & 1


def table_kernel(flips_ref, hidden_ref, *refs, examples):
    table_ref = refs[-1]
    tile = flips_ref.shape[0]
    group = examples + SIGN_ROWS
    words = [None, None]
    for column in range(flips_ref.shape[1] // LANES):
        bit, part = column // 2, column % 2
        flips = flips_ref[:, column * LANES:(column + 1) * LANES]
        term = (flips >> 1) & 1 if bit == 0 else flips & jnp.int32(1 << bit)
        words[part] = term if words[part] is None else words[part] | term
    for part in range(2):
        table_ref[pl.ds(examples + part, tile, stride=group), :] = words[part].astype(F32)
    tokens = hidden_ref.shape[0] // examples
    for example in range(examples):
        block = hidden_ref[example * tokens:(example + 1) * tokens, :].astype(F32).T
        table_ref[pl.ds(example, tile, stride=group), :] = block[:tile]


def build_table(sign_flips, hidden, table, examples, tile, span):
    rows, width = sign_flips.shape
    first, count = span
    group = examples + SIGN_ROWS
    lanes = -(-tile // LANES) * LANES
    in_specs = [
        pl.BlockSpec((tile, width), lambda i: (i + first, 0)),
        pl.BlockSpec((hidden.shape[0], lanes), lambda i: (0, i + first)),
    ]
    args = [sign_flips, hidden]
    aliases = {}
    if table is not None:
        in_specs.append(pl.BlockSpec(memory_space=pl.ANY))
        args.append(table)
        aliases = {2: 0}
    return pl.pallas_call(
        functools.partial(table_kernel, examples=examples),
        grid=(count,),
        in_specs=in_specs,
        out_specs=pl.BlockSpec((tile * group, LANES), lambda i: (i + first, 0)),
        out_shape=jax.ShapeDtypeStruct((rows * group, LANES), F32),
        input_output_aliases=aliases,
        compiler_params=pltpu.CompilerParams(vmem_limit_bytes=40 * MIB),
        cost_estimate=pl.CostEstimate(
            flops=2 * tile * count * width, bytes_accessed=4 * tile * count * width, transcendentals=0
        ),
        name="build_table",
    )(*args)


def hadamard_words(column):
    length = column.shape[1]
    lane = lax.broadcasted_iota(I32, (LANES, length), 0)
    words = -parity(lane & column, 7)

    def where_bit(bit, pattern):
        return -((column >> bit) & 1) & jnp.int32(signed(pattern))

    upper = where_bit(7, 0xFFFF0000)
    for bit, pattern in ((8, 0xAAAA), (9, 0xCCCC), (10, 0xF0F0), (11, 0xFF00)):
        upper = upper ^ where_bit(bit, pattern * 0x10001)
    return words ^ upper


def sign_columns(words, bits):
    pieces = []
    for bit in bits:
        for mask in (jnp.int32(1) << bit, jnp.int32(1) << (bit + HALF)):
            pieces.append(jnp.where((words & mask) != 0, -1.0, 1.0).astype(BF16))
    return jnp.concatenate(pieces, axis=1)


def join(cotangents, joined):
    depth = cotangents[0].shape[1]
    for at, cotangent in enumerate(cotangents):
        joined[:, at * depth:(at + 1) * depth] = cotangent[...]


def project(scalars, joined, words, depth):
    halves = depth // (2 * LANES)
    bits = [scalars[1 + at] * halves + half for at in range(joined.shape[1] // depth) for half in range(halves)]
    return lax.dot_general(joined[...], sign_columns(words, bits), LAST_DIMS, preferred_element_type=F32)


def weigh(total, picked, scalars, position, examples, per_shard, parties, scale):
    shard = position // per_shard
    sign = scale * (1 - 2 * parity(shard & scalars[0], parties.bit_length())).astype(F32)
    weighted = (total * picked.astype(F32)).reshape(examples, -1, total.shape[1])
    return jnp.sum(weighted, axis=1) * sign


def sample_kernel(
    scalars, rows_ref, offsets_ref, table_ref, *refs, blocks, examples, length, first, low_mask, whole, per_shard,
    parties, scale
):
    cotangents, outs, (held, made, joined) = refs[:blocks], refs[blocks:-3], refs[-3:]
    step, steps = pl.program_id(0), pl.num_programs(0)
    group = examples + SIGN_ROWS

    def copy_row(chunk, at, slot):
        row = rows_ref[first + chunk * length + at]
        held[slot, pl.ds(at * group, group), :] = table_ref[pl.ds(row, group), :]

    def copy_chunk(chunk):
        unroll = 32
        slot = lax.rem(chunk, 3)

        def copy_group(block, _):
            for at in range(unroll):
                copy_row(chunk, block * unroll + at, slot)
            return 0

        lax.fori_loop(0, length // unroll, copy_group, 0)

    def make_words(chunk):
        slot = lax.rem(chunk, 3)
        low, high = [held[slot, pl.ds(examples + part, length, stride=group), :].astype(I32) for part in range(2)]
        start = first + jnp.minimum(chunk, steps - 1) * length
        column = offsets_ref[:, pl.ds(pl.multiple_of(start, LANES), length)] & low_mask
        made[lax.rem(chunk, 2)] = (low | (high << HALF)) ^ hadamard_words(column).T

    @pl.when(step == 0)
    def _():
        join(cotangents, joined)
        copy_chunk(0)
        copy_chunk(jnp.minimum(1, steps - 1))
        make_words(0)

    words = made[lax.rem(step, 2)]
    third = jnp.minimum(step + 2, steps - 1)
    target = lax.rem(step + 2, 3)
    for at in range(length):
        copy_row(third, at, target)
    total = project(scalars, joined, words, cotangents[0].shape[1])
    picked = [
        held[lax.rem(step, 3), pl.ds(example, length, stride=group), :].astype(BF16).T for example in range(examples)
    ]
    if whole:
        position = first + step * length + lax.broadcasted_iota(I32, (1, length), 1)
        outs[0][...] = weigh(
            total, jnp.concatenate(picked, axis=0), scalars, position, examples, per_shard, parties, scale
        )
    else:
        signs_ref, picked_ref, total_ref = outs
        total_ref[...] = total
        signs_ref[...] = words
        tokens = picked_ref.shape[0] // examples
        for example in range(examples):
            picked_ref[example * tokens:(example + 1) * tokens, :] = picked[example]
    make_words(step + 1)


def sample(scalars, rows, offsets, table, cotangents, examples, span, width, whole, per_shard, parties, scale):
    start, count = span
    tokens, depth = cotangents[0].shape
    length = CHUNK
    fixed = lambda i, *_: (0, 0)
    across = lambda i, *_: (0, i)
    if whole:
        out_specs = pl.BlockSpec((examples, length), across)
        out_shape = jax.ShapeDtypeStruct((examples, count), F32)
    else:
        out_specs = [
            pl.BlockSpec((length, LANES), lambda i, *_: (i, 0)),
            pl.BlockSpec((tokens, length), across),
            pl.BlockSpec((tokens, length), across),
        ]
        out_shape = [
            jax.ShapeDtypeStruct((count, LANES), I32),
            jax.ShapeDtypeStruct((tokens, count), BF16),
            jax.ShapeDtypeStruct((tokens, count), F32),
        ]
    return pl.pallas_call(
        functools.partial(
            sample_kernel, blocks=len(cotangents), examples=examples, length=length, first=start,
            low_mask=width - 1, whole=whole, per_shard=per_shard, parties=parties, scale=scale,
        ),
        grid_spec=pltpu.PrefetchScalarGridSpec(
            num_scalar_prefetch=2,
            grid=(count // length,),
            in_specs=[pl.BlockSpec(offsets.shape, fixed), pl.BlockSpec(table.shape, fixed)]
            + [pl.BlockSpec(piece.shape, fixed) for piece in cotangents],
            out_specs=out_specs,
            scratch_shapes=[
                pltpu.VMEM((3, length * (examples + SIGN_ROWS), LANES), F32),
                pltpu.VMEM((2, length, LANES), I32),
                pltpu.VMEM((tokens, depth * len(cotangents)), BF16),
            ],
        ),
        out_shape=out_shape,
        compiler_params=pltpu.CompilerParams(vmem_limit_bytes=40 * MIB),
        cost_estimate=pl.CostEstimate(
            flops=2 * tokens * depth * len(cotangents) * count, bytes_accessed=6 * tokens * count, transcendentals=0
        ),
        name="sample_whole" if whole else "sample_rows",
    )(scalars, rows, offsets, table, *cotangents)


def finish_kernel(
    scalars, *refs, blocks, examples, length, sub, start, per_shard, parties, scale
):
    cotangents, (signs_ref, picked_ref, total_ref, out_ref, joined) = refs[:blocks], refs[blocks:]

    @pl.when(pl.program_id(0) == 0)
    def _():
        join(cotangents, joined)

    for at in range(0, length, sub):
        spot = slice(at, at + sub)
        total = project(scalars, joined, signs_ref[spot, :], cotangents[0].shape[1]) + total_ref[:, spot]
        position = start + pl.program_id(0) * length + at + lax.broadcasted_iota(I32, (1, sub), 1)
        out_ref[:, spot] = weigh(
            total, picked_ref[:, spot], scalars, position, examples, per_shard, parties, scale
        )


def finish(scalars, cotangents, signs, picked, total, examples, start, per_shard, parties, scale):
    tokens, depth = cotangents[0].shape
    count = signs.shape[0]
    sub = CHUNK // 2
    length = count // 2 if count % (2 * sub) == 0 else count
    across = lambda i, _: (0, i)
    return pl.pallas_call(
        functools.partial(
            finish_kernel, blocks=len(cotangents), examples=examples, length=length, sub=sub, start=start,
            per_shard=per_shard, parties=parties, scale=scale,
        ),
        grid_spec=pltpu.PrefetchScalarGridSpec(
            num_scalar_prefetch=1,
            grid=(count // length,),
            in_specs=[pl.BlockSpec(piece.shape, lambda i, _: (0, 0)) for piece in cotangents]
            + [
                pl.BlockSpec((length, LANES), lambda i, _: (i, 0)),
                pl.BlockSpec((tokens, length), across),
                pl.BlockSpec((tokens, length), across),
            ],
            out_specs=pl.BlockSpec((examples, length), across),
            scratch_shapes=[pltpu.VMEM((tokens, depth * len(cotangents)), BF16)],
        ),
        out_shape=jax.ShapeDtypeStruct((examples, count), F32),
        compiler_params=pltpu.CompilerParams(vmem_limit_bytes=48 * MIB),
        cost_estimate=pl.CostEstimate(
            flops=2 * tokens * depth * len(cotangents) * count, bytes_accessed=6 * tokens * count, transcendentals=0
        ),
        name="finish_blocks",
    )(scalars, *cotangents, signs, picked, total)


def by_xor(parties, step):
    return [(source, source ^ step) for source in range(parties)]


def sum_shards(values, parties):
    step = 1
    while step < parties:
        values = values + lax.ppermute(values, "param", by_xor(parties, step))
        step *= 2
    return values


def local(hidden, cotangent, sign_flips, offsets):
    examples, tokens, rows = hidden.shape
    width = sign_flips.shape[1]
    parties = lax.axis_size("param")
    own = lax.axis_index("param").astype(I32)
    per_shard = offsets.shape[0]
    count = per_shard * parties
    scale = 1.0 / math.sqrt(parties * width)
    flat = examples * tokens
    depth = cotangent.shape[2]
    held = cotangent.reshape(flat, depth)

    ringed = depth % (2 * LANES) == 0 and parties % 2 == 0
    pieces, numbers = [held], [own]
    if ringed:
        order = list(range(0, parties, 2)) + list(range(parties - 1, 0, -2))
        forward = [(order[at], order[(at + 1) % parties]) for at in range(parties)]
        backward = [(target, source) for source, target in forward]
        place = jnp.where(own % 2 == 0, own // 2, parties - 1 - own // 2)

        def shard_at(spot):
            spot = (spot + parties) % parties
            return jnp.where(spot < parties // 2, 2 * spot, 2 * (parties - spot) - 1)

        def pass_on(ahead, behind):
            return lax.ppermute(ahead, "param", forward), lax.ppermute(behind, "param", backward)

    units = hidden.reshape(flat, rows)
    if rows % LANES:
        units = jnp.pad(units, ((0, 0), (0, -rows % LANES)))
    tile = 2 * LANES if rows % (2 * LANES) == 0 else LANES if rows % LANES == 0 else rows
    tiles = rows // tile
    table, built, step = None, 0, 1
    steps = parties.bit_length() - 1
    for at in range(steps):
        other = lax.ppermute(offsets, "param", by_xor(parties, step))
        until = tiles - (tiles - 1) * (steps - 1 - at) // max(steps - 1, 1)
        if until > built:
            table = build_table(sign_flips, units, table, examples, tile, (built, until - built))
            built = until
            table, other = lax.optimization_barrier((table, other))
        if ringed and at == 0:
            held, other = lax.optimization_barrier((held, other))
            ahead, behind = pass_on(held, held)
        if ringed and at == 1:
            table, ahead, behind = lax.optimization_barrier((table, ahead, behind))
        offsets = jnp.where(
            (own & step) == 0, jnp.concatenate([offsets, other]), jnp.concatenate([other, offsets])
        )
        step *= 2

    row_shift = width.bit_length() - 1
    unit_rows = (offsets >> row_shift) * (examples + SIGN_ROWS)
    line = offsets.reshape(1, count)
    eighth = count // 8
    sizes = [part * eighth for part in EARLY] if ringed else []
    sizes.append(count - sum(sizes))
    spans = [(sum(sizes[:at]), size) for at, size in enumerate(sizes)]
    sampled = []

    def scalars(first, last):
        return jnp.stack([own] + numbers[first:last])

    def sample_next(whole):
        return sample(
            scalars(0, len(pieces)), unit_rows, line, table, pieces, examples, spans[len(sampled)], width, whole,
            per_shard, parties, scale,
        )

    if ringed:
        for step in range(1, parties // 2):
            pieces += [ahead, behind]
            numbers += [shard_at(place - step), shard_at(place + step)]
            if step + 1 < parties // 2:
                ahead, behind = pass_on(ahead, behind)
            else:
                middle = flat // 2
                ahead, behind = pass_on(ahead[:middle], behind[middle:])
            if step > 1 and len(sampled) < len(EARLY):
                signs, picked, total = sample_next(False)
                ahead, behind, signs = lax.optimization_barrier((ahead, behind, signs))
                sampled.append((signs, picked, total, len(pieces)))
        pieces.append(jnp.concatenate([ahead, behind], axis=0))
        numbers.append(shard_at(place + parties // 2))
    else:
        gathered = lax.all_gather(cotangent, "param", axis=2, tiled=True).reshape(flat, width)
        span = 4 * LANES
        pieces = [gathered[:, at:at + span] for at in range(0, width, span)]
        numbers = [jnp.int32(at) for at in range(len(pieces))]
    whole = sample_next(True)
    parts = [whole]
    if sampled:
        parts = [
            finish(
                scalars(used, len(pieces)), pieces[used:], signs, picked, total, examples, start, per_shard, parties,
                scale,
            )
            for (signs, picked, total, used), (start, _) in zip(sampled, spans)
        ]
        parts = [jnp.concatenate(parts, axis=1), whole]
    return jnp.concatenate([sum_shards(part, parties) for part in parts], axis=1)


def solution(mesh):
    return jax.shard_map(
        local,
        mesh=mesh,
        in_specs=(
            P(("groups", "dp"), None, "param"),
            P(("groups", "dp"), None, "param"),
            P("param", None),
            P("param"),
        ),
        out_specs=P(("groups", "dp"), None),
        check_vma=False,
    )
```

time: 123 us -> 113 us (0.919)
  Pallas kernels: 79.9 us -> 51.7 us
  local copies, waits for them, and re-layouts: 4.47 us -> 14.6 us
  waiting for transfers between devices: 17.7 us -> 26.5 us
    pallas_call x3 -> x0, Pallas kernels: 18.3 us -> none  [finish(): pl.pallas_call(functools.partial(finish_kernel, blocks=len(cotangents), e...]
    unnamed x15 -> x20, local copies, waits for them, and re-layouts: 4.17 us -> 14.5 us
    ppermute x8, waiting for transfers between devices: 3.06 us -> 12 us  [the longest x4 11.3 us: pass_on(): lax.ppermute(behind, 'param', backward)]
    pallas_call x3 -> x1, Pallas kernels: 43.8 us -> 37.4 us  [sample(): pl.pallas_call(functools.partial(sample_kernel, blocks=len(cotangents), e...]
    pallas_call x3, Pallas kernels: 17.8 us -> 14.3 us  [build_table(): pl.pallas_call(functools.partial(table_kernel, examples=examples), grid=(...]
    ppermute x6 -> x3, starting transfers between devices: 3.63 us -> 3.19 us  [sum_shards(): values = values + lax.ppermute(values, 'param', by_xor(parties, step))]
    ppermute x6 -> x3, waiting for transfers between devices: 14.6 us -> 14.6 us  [sum_shards(): values = values + lax.ppermute(values, 'param', by_xor(parties, step))]
  transfers between devices with their start and end apart: 17 -> 14, of which waited for: 5 -> 6; matrix products, arithmetic and copies ran while one was open for 0% -> 0% of each run, Pallas kernels for 57% -> 13%
where the time goes in v3:
time: 113 us; the launch traced here: 112 us
  Pallas kernels  51.7 us (46%)
  waiting for transfers between devices  26.5 us (23%)
  starting transfers between devices  18.6 us (16%)
  local copies, waits for them, and re-layouts  14.6 us (13%)
    pallas_call x1, Pallas kernels, sample(): pl.pallas_call(functools.partial(sample_kernel, blocks=len(cotangents), e...  37.4 us
    ppermute x3, waiting for transfers between devices, sum_shards(): values = values + lax.ppermute(values, 'param', by_xor(parties, step))  14.6 us
    unnamed x20, local copies, waits for them, and re-layouts  14.5 us
    pallas_call x3, Pallas kernels, build_table(): pl.pallas_call(functools.partial(table_kernel, examples=examples), grid=(...  14.3 us
    ppermute x4, waiting for transfers between devices, pass_on(): lax.ppermute(behind, 'param', backward)  11.3 us
    ppermute x3, starting transfers between devices, local(): other = lax.ppermute(offsets, 'param', by_xor(parties, step))  7.1 us
    ppermute x4, starting transfers between devices, pass_on(): lax.ppermute(ahead, 'param', forward)  6.1 us
    ppermute x3, starting transfers between devices, sum_shards(): values = values + lax.ppermute(values, 'param', by_xor(parties, step))  3.19 us
  transfers between devices with their start and end apart: 14, of which 6 were waited for; matrix products, arithmetic and copies ran while one was open for 0% of the time, Pallas kernels for 13%

profile of v3, /device:TPU:0, one launch (start us, length us, event | category | flops | bytes accessed | tf_op | source)
XLA Modules:
  0.0 112.3 jit_solution(321642195205993317)
XLA Ops:
  0.0 2.9 %collective-permute-start = (s32[1024]{0:T(1024)}, s32[1024]{0:T(1024)S(1)}, u32[]{:S(2)}, u32[]{:S(2)}) collective-permute-start(s32[1024]{0:T(1024)} %param.7), channel_id=1, source_target_pairs={{0,2},{2,0},{4,6},{6,4},{8,10},{10,8},{12,14},{14,12},{1,3},{3,1},... | collective-permute-start | bytes 12296 | tf_op jit(solution)/shard_map/ppermute | solution.py:328
  2.9 1.3 %copy-done.6 = bf16[3,128,1792]{2,1,0:T(8,128)(2,1)S(1)} copy-done((bf16[3,128,1792]{2,1,0:T(8,128)(2,1)S(1)}, bf16[3,128,1792]{2,1,0:T(8,128)(2,1)}, u32[]{:S(2)}) %copy-start.6) | copy-done | bytes 1376280
  4.3 2.8 %build_table.3.refs_0_ = f32[8960,128]{1,0:T(8,128)S(1)} custom-call(s32[1792,4096]{1,0:T(8,128)} %flips_ref.5, bf16[384,1792]{1,0:T(8,128)(2,1)S(1)} %bitcast.12), custom_call_target="tpu_custom_call" | custom-call | flops 2097152 | bytes 4194304 | tf_op jit(solution)/shard_map/build_table/pallas_call | solution.py:68
  7.1 2.1 %copy-done = f32[8960,128]{1,0:T(8,128)} copy-done((f32[8960,128]{1,0:T(8,128)}, f32[8960,128]{1,0:T(8,128)S(1)}, u32[]{:S(2)}) %copy-start) | copy-done | bytes 4587544
  9.2 1.6 %collective-permute-start.2 = (bf16[384,512]{1,0:T(8,128)(2,1)S(1)}, bf16[384,512]{1,0:T(8,128)(2,1)S(1)}, u32[]{:S(2)}, u32[]{:S(2)}) collective-permute-start(bf16[384,512]{1,0:T(8,128)(2,1)S(1)} %bitcast.15), channel_id=1, source_target_pairs={{0,4},{4,8},{8,12},{12,14},{14,10},{10,6},{6,2},{2,0},{1,5},{5,9},... | collective-permute-start | bytes 1179656 | tf_op jit(solution)/shard_map/ppermute | solution.py:318
  11.2 1.6 %collective-permute-start.1 = (s32[2048]{0:T(1024)S(1)}, s32[2048]{0:T(1024)S(1)}, u32[]{:S(2)}, u32[]{:S(2)}) collective-permute-start(s32[2048]{0:T(1024)S(1)} %add_select_fusion.2), channel_id=1, source_target_pairs={{0,4},{2,6},{4,0},{6,2},{8,12},{10,14},{12,8},{14,10},{1,5},{3,7},... | collective-permute-start | bytes 24584 | tf_op jit(solution)/shard_map/ppermute | solution.py:328
  12.8 2.3 %copy-done.1 = f32[8960,128]{1,0:T(8,128)S(1)} copy-done((f32[8960,128]{1,0:T(8,128)S(1)}, f32[8960,128]{1,0:T(8,128)}, u32[]{:S(2)}) %copy-start.1) | copy-done | bytes 4587544
  15.1 5.7 %build_table.4.refs_0_ = f32[8960,128]{1,0:T(8,128)S(1)} custom-call(s32[1792,4096]{1,0:T(8,128)} %flips_ref.5, bf16[384,1792]{1,0:T(8,128)(2,1)S(1)} %bitcast.13, f32[8960,128]{1,0:T(8,128)S(1)} %copy-done.1), custom_call_target="tpu_custom_call", output_to_operand_aliasing={{}: (2, {})} | custom-call | flops 6291456 | bytes 12582912 | tf_op jit(solution)/shard_map/build_table/pallas_call | solution.py:68
  20.9 2.1 %copy-done.2 = f32[8960,128]{1,0:T(8,128)} copy-done((f32[8960,128]{1,0:T(8,128)}, f32[8960,128]{1,0:T(8,128)S(1)}, u32[]{:S(2)}) %copy-start.2) | copy-done | bytes 4587544
  23.5 1.5 %collective-permute-start.5 = (bf16[384,512]{1,0:T(8,128)(2,1)S(1)}, bf16[384,512]{1,0:T(8,128)(2,1)}, u32[]{:S(2)}, u32[]{:S(2)}) collective-permute-start(bf16[384,512]{1,0:T(8,128)(2,1)S(1)} %collective-permute-done.2.refs_1_), channel_id=1, source_target_pairs={{0,4},{4,8},{8,12},{12,14},{14,10},{10,6},{6,2},{2,0},{1,5},{5,9},... | collective-permute-start | bytes 1179656 | tf_op jit(solution)/shard_map/ppermute | solution.py:318
  25.0 7.8 %collective-permute-done.6.refs_4_ = bf16[384,512]{1,0:T(8,128)(2,1)} collective-permute-done((bf16[384,512]{1,0:T(8,128)(2,1)S(1)}, bf16[384,512]{1,0:T(8,128)(2,1)}, u32[]{:S(2)}, u32[]{:S(2)}) %collective-permute-start.6) | collective-permute-done | bytes 393248 | tf_op jit(solution)/shard_map/ppermute | solution.py:318
  33.4 1.5 %collective-permute-start.7 = (bf16[384,512]{1,0:T(8,128)(2,1)}, bf16[384,512]{1,0:T(8,128)(2,1)S(1)}, u32[]{:S(2)}, u32[]{:S(2)}) collective-permute-start(bf16[384,512]{1,0:T(8,128)(2,1)} %collective-permute-done.5.refs_3_), channel_id=1, source_target_pairs={{0,4},{4,8},{8,12},{12,14},{14,10},{10,6},{6,2},{2,0},{1,5},{5,9},... | collective-permute-start | bytes 1179656 | tf_op jit(solution)/shard_map/ppermute | solution.py:318
  34.9 2.6 %collective-permute-start.4 = (s32[4096]{0:T(1024)S(1)}, s32[4096]{0:T(1024)S(1)}, u32[]{:S(2)}, u32[]{:S(2)}) collective-permute-start(s32[4096]{0:T(1024)S(1)} %add_select_fusion.1), channel_id=1, source_target_pairs={{0,8},{2,10},{4,12},{6,14},{8,0},{10,2},{12,4},{14,6},{1,9},{3,11}... | collective-permute-start | bytes 49160 | tf_op jit(solution)/shard_map/ppermute | solution.py:328
  37.5 2.3 %copy-done.3 = f32[8960,128]{1,0:T(8,128)S(1)} copy-done((f32[8960,128]{1,0:T(8,128)S(1)}, f32[8960,128]{1,0:T(8,128)}, u32[]{:S(2)}) %copy-start.3) | copy-done | bytes 4587544
  39.8 5.7 %build_table.5.table_ref = f32[8960,128]{1,0:T(8,128)S(1)} custom-call(s32[1792,4096]{1,0:T(8,128)} %flips_ref.5, bf16[384,1792]{1,0:T(8,128)(2,1)S(1)} %bitcast.14, f32[8960,128]{1,0:T(8,128)S(1)} %copy-done.3), custom_call_target="tpu_custom_call", output_to_operand_aliasing={{}: (2, {})} | custom-call | flops 6291456 | bytes 12582912 | tf_op jit(solution)/shard_map/build_table/pallas_call | solution.py:68
  45.6 2.1 %copy-done.4 = f32[8960,128]{1,0:T(8,128)} copy-done((f32[8960,128]{1,0:T(8,128)}, f32[8960,128]{1,0:T(8,128)S(1)}, u32[]{:S(2)}) %copy-start.4) | copy-done | bytes 4587544
  48.3 1.5 %collective-permute-start.9 = (bf16[192,512]{1,0:T(8,128)(2,1)S(1)}, bf16[192,512]{1,0:T(8,128)(2,1)S(1)}, u32[]{:S(2)}, u32[]{:S(2)}) collective-permute-start(bf16[192,512]{1,0:T(8,128)(2,1)S(1)} %slice.8), channel_id=1, source_target_pairs={{0,4},{4,8},{8,12},{12,14},{14,10},{10,6},{6,2},{2,0},{1,5},{5,9},... | collective-permute-start | bytes 589832 | tf_op jit(solution)/shard_map/ppermute | solution.py:318
  49.9 3.5 %collective-permute-done.10 = bf16[192,512]{1,0:T(8,128)(2,1)S(1)} collective-permute-done((bf16[192,512]{1,0:T(8,128)(2,1)S(1)}, bf16[192,512]{1,0:T(8,128)(2,1)S(1)}, u32[]{:S(2)}, u32[]{:S(2)}) %collective-permute-start.10) | collective-permute-done | bytes 196640 | tf_op jit(solution)/shard_map/ppermute | solution.py:318
  54.1 2.3 %copy-done.5 = f32[8960,128]{1,0:T(8,128)S(1)} copy-done((f32[8960,128]{1,0:T(8,128)S(1)}, f32[8960,128]{1,0:T(8,128)}, u32[]{:S(2)}) %copy-start.5) | copy-done | bytes 4587544
  56.4 37.4 %sample_whole.1 = f32[3,8192]{1,0:T(4,128)S(1)} custom-call(s32[9]{0:T(128)S(1)} %stack.36.scalars, s32[8192]{0:T(1024)S(1)} %fusion.1.rows_ref, s32[1,8192]{1,0:T(1,128)S(1)} %broadcast_select_fusion.offsets_ref, f32[8960,128]{1,0:T(8,128)S(1)} %copy-done.5, bf16[384,512]{1,0:T(8,128)(2,1)S(1)} %bitcast.17, ...), custom_call_target="tpu_custom_call" | custom-call | flops 25769803776 | bytes 18874368 | tf_op jit(solution)/shard_map/sample_whole/pallas_call | solution.py:205
  94.3 4.5 %collective-permute-done.11 = f32[3,8192]{1,0:T(4,128)S(1)} collective-permute-done((f32[3,8192]{1,0:T(4,128)S(1)}, f32[3,8192]{1,0:T(4,128)S(1)}, u32[]{:S(2)}, u32[]{:S(2)}) %collective-permute-start.11) | collective-permute-done | bytes 98336 | tf_op jit(solution)/shard_map/ppermute | solution.py:288
  98.8 1.6 %collective-permute-start.12 = (f32[3,8192]{1,0:T(4,128)S(1)}, f32[3,8192]{1,0:T(4,128)S(1)}, u32[]{:S(2)}, u32[]{:S(2)}) collective-permute-start(f32[3,8192]{1,0:T(4,128)S(1)} %add.99), channel_id=1, source_target_pairs={{0,4},{2,6},{4,0},{6,2},{8,12},{10,14},{12,8},{14,10},{1,5},{3,7},... | collective-permute-start | bytes 294920 | tf_op jit(solution)/shard_map/ppermute | solution.py:288
  100.4 3.8 %collective-permute-done.12 = f32[3,8192]{1,0:T(4,128)S(1)} collective-permute-done((f32[3,8192]{1,0:T(4,128)S(1)}, f32[3,8192]{1,0:T(4,128)S(1)}, u32[]{:S(2)}, u32[]{:S(2)}) %collective-permute-start.12) | collective-permute-done | bytes 98336 | tf_op jit(solution)/shard_map/ppermute | solution.py:288
  105.3 6.2 %collective-permute-done.13 = f32[3,8192]{1,0:T(4,128)S(1)} collective-permute-done((f32[3,8192]{1,0:T(4,128)S(1)}, f32[3,8192]{1,0:T(4,128)S(1)}, u32[]{:S(2)}, u32[]{:S(2)}) %collective-permute-start.13) | collective-permute-done | bytes 98336 | tf_op jit(solution)/shard_map/ppermute | solution.py:288
  (39 shorter events, 5.4 us)
Async XLA Ops:
  0.0 9.2 %collective-permute-start = (s32[1024]{0:T(1024)}, s32[1024]{0:T(1024)S(1)}, u32[]{:S(2)}, u32[]{:S(2)}) collective-permute-start(s32[1024]{0:T(1024)} %param.7), channel_id=1, source_target_pairs={{0,2},{2,0},{4,6},{6,4},{8,10},{10,8},{12,14},{14,12},{1,3},{3,1},... | collective-permute-start | bytes 12296 | tf_op jit(solution)/shard_map/ppermute | solution.py:328
  2.9 1.3 %copy-start.6 = (bf16[3,128,1792]{2,1,0:T(8,128)(2,1)S(1)}, bf16[3,128,1792]{2,1,0:T(8,128)(2,1)}, u32[]{:S(2)}) copy-start(bf16[3,128,1792]{2,1,0:T(8,128)(2,1)} %param.4) | copy-start | bytes 4128772
  4.3 4.9 %copy-start.8 = (bf16[3,128,512]{2,1,0:T(8,128)(2,1)S(1)}, bf16[3,128,512]{2,1,0:T(8,128)(2,1)}, u32[]{:S(2)}) copy-start(bf16[3,128,512]{2,1,0:T(8,128)(2,1)} %param.5) | copy-start | bytes 1179652
  4.3 6.9 %copy-start.9 = (s32[1024]{0:T(1024)S(1)}, s32[1024]{0:T(1024)}, u32[]{:S(2)}) copy-start(s32[1024]{0:T(1024)} %param.7) | copy-start | bytes 12292
  4.3 8.5 %copy-start.7 = (bf16[3,128,1792]{2,1,0:T(8,128)(2,1)S(1)}, bf16[3,128,1792]{2,1,0:T(8,128)(2,1)}, u32[]{:S(2)}) copy-start(bf16[3,128,1792]{2,1,0:T(8,128)(2,1)} %param.4) | copy-start | bytes 4128772
  7.1 2.1 %copy-start = (f32[8960,128]{1,0:T(8,128)}, f32[8960,128]{1,0:T(8,128)S(1)}, u32[]{:S(2)}) copy-start(f32[8960,128]{1,0:T(8,128)S(1)} %build_table.3.refs_0_) | copy-start | bytes 13762564
  9.2 13.8 %collective-permute-start.2 = (bf16[384,512]{1,0:T(8,128)(2,1)S(1)}, bf16[384,512]{1,0:T(8,128)(2,1)S(1)}, u32[]{:S(2)}, u32[]{:S(2)}) collective-permute-start(bf16[384,512]{1,0:T(8,128)(2,1)S(1)} %bitcast.15), channel_id=1, source_target_pairs={{0,4},{4,8},{8,12},{12,14},{14,10},{10,6},{6,2},{2,0},{1,5},{5,9},... | collective-permute-start | bytes 1179656 | tf_op jit(solution)/shard_map/ppermute | solution.py:318
  10.8 12.2 %collective-permute-start.3 = (bf16[384,512]{1,0:T(8,128)(2,1)S(1)}, bf16[384,512]{1,0:T(8,128)(2,1)S(1)}, u32[]{:S(2)}, u32[]{:S(2)}) collective-permute-start(bf16[384,512]{1,0:T(8,128)(2,1)S(1)} %bitcast.16), channel_id=1, source_target_pairs={{4,0},{8,4},{12,8},{14,12},{10,14},{6,10},{2,6},{0,2},{5,1},{9,5},... | collective-permute-start | bytes 1179656 | tf_op jit(solution)/shard_map/ppermute | solution.py:318
  11.2 11.7 %collective-permute-start.1 = (s32[2048]{0:T(1024)S(1)}, s32[2048]{0:T(1024)S(1)}, u32[]{:S(2)}, u32[]{:S(2)}) collective-permute-start(s32[2048]{0:T(1024)S(1)} %add_select_fusion.2), channel_id=1, source_target_pairs={{0,4},{2,6},{4,0},{6,2},{8,12},{10,14},{12,8},{14,10},{1,5},{3,7},... | collective-permute-start | bytes 24584 | tf_op jit(solution)/shard_map/ppermute | solution.py:328
  12.8 2.3 %copy-start.1 = (f32[8960,128]{1,0:T(8,128)S(1)}, f32[8960,128]{1,0:T(8,128)}, u32[]{:S(2)}) copy-start(f32[8960,128]{1,0:T(8,128)} %copy-done) | copy-start | bytes 13762564
  20.8 2.1 %copy-start.2 = (f32[8960,128]{1,0:T(8,128)}, f32[8960,128]{1,0:T(8,128)S(1)}, u32[]{:S(2)}) copy-start(f32[8960,128]{1,0:T(8,128)S(1)} %build_table.4.refs_0_) | copy-start | bytes 13762564
  22.9 9.9 %collective-permute-start.6 = (bf16[384,512]{1,0:T(8,128)(2,1)S(1)}, bf16[384,512]{1,0:T(8,128)(2,1)}, u32[]{:S(2)}, u32[]{:S(2)}) collective-permute-start(bf16[384,512]{1,0:T(8,128)(2,1)S(1)} %collective-permute-done.3.refs_2_), channel_id=1, source_target_pairs={{4,0},{8,4},{12,8},{14,12},{10,14},{6,10},{2,6},{0,2},{5,1},{9,5},... | collective-permute-start | bytes 1179656 | tf_op jit(solution)/shard_map/ppermute | solution.py:318
  23.5 9.8 %collective-permute-start.5 = (bf16[384,512]{1,0:T(8,128)(2,1)S(1)}, bf16[384,512]{1,0:T(8,128)(2,1)}, u32[]{:S(2)}, u32[]{:S(2)}) collective-permute-start(bf16[384,512]{1,0:T(8,128)(2,1)S(1)} %collective-permute-done.2.refs_1_), channel_id=1, source_target_pairs={{0,4},{4,8},{8,12},{12,14},{14,10},{10,6},{6,2},{2,0},{1,5},{5,9},... | collective-permute-start | bytes 1179656 | tf_op jit(solution)/shard_map/ppermute | solution.py:318
  32.8 14.9 %collective-permute-start.8 = (bf16[384,512]{1,0:T(8,128)(2,1)}, bf16[384,512]{1,0:T(8,128)(2,1)S(1)}, u32[]{:S(2)}, u32[]{:S(2)}) collective-permute-start(bf16[384,512]{1,0:T(8,128)(2,1)} %collective-permute-done.6.refs_4_), channel_id=1, source_target_pairs={{4,0},{8,4},{12,8},{14,12},{10,14},{6,10},{2,6},{0,2},{5,1},{9,5},... | collective-permute-start | bytes 1179656 | tf_op jit(solution)/shard_map/ppermute | solution.py:318
  33.4 14.9 %collective-permute-start.7 = (bf16[384,512]{1,0:T(8,128)(2,1)}, bf16[384,512]{1,0:T(8,128)(2,1)S(1)}, u32[]{:S(2)}, u32[]{:S(2)}) collective-permute-start(bf16[384,512]{1,0:T(8,128)(2,1)} %collective-permute-done.5.refs_3_), channel_id=1, source_target_pairs={{0,4},{4,8},{8,12},{12,14},{14,10},{10,6},{6,2},{2,0},{1,5},{5,9},... | collective-permute-start | bytes 1179656 | tf_op jit(solution)/shard_map/ppermute | solution.py:318
  34.9 12.8 %collective-permute-start.4 = (s32[4096]{0:T(1024)S(1)}, s32[4096]{0:T(1024)S(1)}, u32[]{:S(2)}, u32[]{:S(2)}) collective-permute-start(s32[4096]{0:T(1024)S(1)} %add_select_fusion.1), channel_id=1, source_target_pairs={{0,8},{2,10},{4,12},{6,14},{8,0},{10,2},{12,4},{14,6},{1,9},{3,11}... | collective-permute-start | bytes 49160 | tf_op jit(solution)/shard_map/ppermute | solution.py:328
  37.5 2.3 %copy-start.3 = (f32[8960,128]{1,0:T(8,128)S(1)}, f32[8960,128]{1,0:T(8,128)}, u32[]{:S(2)}) copy-start(f32[8960,128]{1,0:T(8,128)} %copy-done.2) | copy-start | bytes 13762564
  45.6 2.1 %copy-start.4 = (f32[8960,128]{1,0:T(8,128)}, f32[8960,128]{1,0:T(8,128)S(1)}, u32[]{:S(2)}) copy-start(f32[8960,128]{1,0:T(8,128)S(1)} %build_table.5.table_ref) | copy-start | bytes 13762564
  47.7 5.7 %collective-permute-start.10 = (bf16[192,512]{1,0:T(8,128)(2,1)S(1)}, bf16[192,512]{1,0:T(8,128)(2,1)S(1)}, u32[]{:S(2)}, u32[]{:S(2)}) collective-permute-start(bf16[192,512]{1,0:T(8,128)(2,1)S(1)} %slice.9), channel_id=1, source_target_pairs={{4,0},{8,4},{12,8},{14,12},{10,14},{6,10},{2,6},{0,2},{5,1},{9,5},... | collective-permute-start | bytes 589832 | tf_op jit(solution)/shard_map/ppermute | solution.py:318
  48.3 5.7 %collective-permute-start.9 = (bf16[192,512]{1,0:T(8,128)(2,1)S(1)}, bf16[192,512]{1,0:T(8,128)(2,1)S(1)}, u32[]{:S(2)}, u32[]{:S(2)}) collective-permute-start(bf16[192,512]{1,0:T(8,128)(2,1)S(1)} %slice.8), channel_id=1, source_target_pairs={{0,4},{4,8},{8,12},{12,14},{14,10},{10,6},{6,2},{2,0},{1,5},{5,9},... | collective-permute-start | bytes 589832 | tf_op jit(solution)/shard_map/ppermute | solution.py:318
  54.1 2.3 %copy-start.5 = (f32[8960,128]{1,0:T(8,128)S(1)}, f32[8960,128]{1,0:T(8,128)}, u32[]{:S(2)}) copy-start(f32[8960,128]{1,0:T(8,128)} %copy-done.4) | copy-start | bytes 13762564
  93.8 5.0 %collective-permute-start.11 = (f32[3,8192]{1,0:T(4,128)S(1)}, f32[3,8192]{1,0:T(4,128)S(1)}, u32[]{:S(2)}, u32[]{:S(2)}) collective-permute-start(f32[3,8192]{1,0:T(4,128)S(1)} %sample_whole.1), channel_id=1, source_target_pairs={{0,2},{2,0},{4,6},{6,4},{8,10},{10,8},{12,14},{14,12},{1,3},{3,1},... | collective-permute-start | bytes 294920 | tf_op jit(solution)/shard_map/ppermute | solution.py:288
  98.8 5.4 %collective-permute-start.12 = (f32[3,8192]{1,0:T(4,128)S(1)}, f32[3,8192]{1,0:T(4,128)S(1)}, u32[]{:S(2)}, u32[]{:S(2)}) collective-permute-start(f32[3,8192]{1,0:T(4,128)S(1)} %add.99), channel_id=1, source_target_pairs={{0,4},{2,6},{4,0},{6,2},{8,12},{10,14},{12,8},{14,10},{1,5},{3,7},... | collective-permute-start | bytes 294920 | tf_op jit(solution)/shard_map/ppermute | solution.py:288
  104.3 7.3 %collective-permute-start.13 = (f32[3,8192]{1,0:T(4,128)S(1)}, f32[3,8192]{1,0:T(4,128)S(1)}, u32[]{:S(2)}, u32[]{:S(2)}) collective-permute-start(f32[3,8192]{1,0:T(4,128)S(1)} %add.100), channel_id=1, source_target_pairs={{0,8},{2,10},{4,12},{6,14},{8,0},{10,2},{12,4},{14,6},{1,9},{3,11}... | collective-permute-start | bytes 294920 | tf_op jit(solution)/shard_map/ppermute | solution.py:288

commit v4 on v3

--- a/solution.py
+++ b/solution.py
@@ -72,7 +72,7 @@
         out_specs=pl.BlockSpec((tile * group, LANES), lambda i: (i + first, 0)),
         out_shape=jax.ShapeDtypeStruct((rows * group, LANES), F32),
         input_output_aliases=aliases,
-        compiler_params=pltpu.CompilerParams(vmem_limit_bytes=40 * MIB),
+        compiler_params=pltpu.CompilerParams(vmem_limit_bytes=60 * MIB),
         cost_estimate=pl.CostEstimate(
             flops=2 * tile * count * width, bytes_accessed=4 * tile * count * width, transcendentals=0
         ),
@@ -220,7 +220,7 @@
             ],
         ),
         out_shape=out_shape,
-        compiler_params=pltpu.CompilerParams(vmem_limit_bytes=40 * MIB),
+        compiler_params=pltpu.CompilerParams(vmem_limit_bytes=56 * MIB),
         cost_estimate=pl.CostEstimate(
             flops=2 * tokens * depth * len(cotangents) * count, bytes_accessed=6 * tokens * count, transcendentals=0
         ),
@@ -317,6 +317,8 @@
         def pass_on(ahead, behind):
             return lax.ppermute(ahead, "param", forward), lax.ppermute(behind, "param", backward)
 
+        ahead, behind = pass_on(held, held)
+
     units = hidden.reshape(flat, rows)
     if rows % LANES:
         units = jnp.pad(units, ((0, 0), (0, -rows % LANES)))
@@ -326,14 +328,11 @@
     steps = parties.bit_length() - 1
     for at in range(steps):
         other = lax.ppermute(offsets, "param", by_xor(parties, step))
-        until = tiles - (tiles - 1) * (steps - 1 - at) // max(steps - 1, 1)
+        until = -(-tiles * (at + 1) // steps)
         if until > built:
             table = build_table(sign_flips, units, table, examples, tile, (built, until - built))
             built = until
             table, other = lax.optimization_barrier((table, other))
-        if ringed and at == 0:
-            held, other = lax.optimization_barrier((held, other))
-            ahead, behind = pass_on(held, held)
         if ringed and at == 1:
             table, ahead, behind = lax.optimization_barrier((table, ahead, behind))
         offsets = jnp.where(
@@ -363,6 +362,8 @@
         for step in range(1, parties // 2):
             pieces += [ahead, behind]
             numbers += [shard_at(place - step), shard_at(place + step)]
+            if step == 2:
+                ahead, behind, table = lax.optimization_barrier((ahead, behind, table))
             if step + 1 < parties // 2:
                 ahead, behind = pass_on(ahead, behind)
             else:
@@ -380,7 +381,7 @@
         pieces = [gathered[:, at:at + span] for at in range(0, width, span)]
         numbers = [jnp.int32(at) for at in range(len(pieces))]
     whole = sample_next(True)
-    parts = [whole]
+    parts = [whole[:, :count // 2], whole[:, count // 2:]]
     if sampled:
         parts = [
             finish(

time: 113 us -> 111 us (0.982)
  local copies, waits for them, and re-layouts: 14.6 us -> 1.58 us
  Pallas kernels: 51.7 us -> 57.5 us
  starting transfers between devices: 18.6 us -> 23.7 us
  other arithmetic: 0.83 us -> 3.68 us
  waiting for transfers between devices: 26.5 us -> 24 us
    unnamed x20 -> x14, local copies, waits for them, and re-layouts: 14.5 us -> 0.03 us
    ppermute x3 -> x6, waiting for transfers between devices: 14.6 us -> 10.6 us  [sum_shards(): values = values + lax.ppermute(values, 'param', by_xor(parties, step))]
    ppermute x3, waiting for transfers between devices: 0.01 us -> 3.83 us  [local(): other = lax.ppermute(offsets, 'param', by_xor(parties, step))]
    ppermute x3 -> x6, starting transfers between devices: 3.19 us -> 6.83 us  [sum_shards(): values = values + lax.ppermute(values, 'param', by_xor(parties, step))]
    pallas_call x1, Pallas kernels: 37.4 us -> 40.8 us  [sample(): pl.pallas_call(functools.partial(sample_kernel, blocks=len(cotangents), e...]
    pallas_call x3, Pallas kernels: 14.3 us -> 16.7 us  [build_table(): pl.pallas_call(functools.partial(table_kernel, examples=examples), grid=(...]
    ppermute x4, waiting for transfers between devices: 11.3 us -> 9.5 us  [pass_on(): lax.ppermute(behind, 'param', backward)]
    ppermute x4, starting transfers between devices: 6.1 us -> 7.94 us  [pass_on(): lax.ppermute(ahead, 'param', forward)]
  transfers between devices with their start and end apart: 14 -> 17, of which waited for: 6 -> 11; matrix products, arithmetic and copies ran while one was open for 0% -> 2% of each run, Pallas kernels for 13% -> 15%
where the time goes in v4:
time: 111 us
  Pallas kernels  57.5 us (52%)
  waiting for transfers between devices  24 us (22%)
  starting transfers between devices  23.7 us (21%)
  other arithmetic  3.68 us (3%)
  local copies, waits for them, and re-layouts  1.58 us (1%)
    pallas_call x1, Pallas kernels, sample(): pl.pallas_call(functools.partial(sample_kernel, blocks=len(cotangents), e...  40.8 us
    pallas_call x3, Pallas kernels, build_table(): pl.pallas_call(functools.partial(table_kernel, examples=examples), grid=(...  16.7 us
    ppermute x6, waiting for transfers between devices, sum_shards(): values = values + lax.ppermute(values, 'param', by_xor(parties, step))  10.6 us
    ppermute x4, waiting for transfers between devices, pass_on(): lax.ppermute(behind, 'param', backward)  9.5 us
    ppermute x4, starting transfers between devices, pass_on(): lax.ppermute(ahead, 'param', forward)  7.94 us
    ppermute x3, starting transfers between devices, local(): other = lax.ppermute(offsets, 'param', by_xor(parties, step))  7.57 us
    ppermute x6, starting transfers between devices, sum_shards(): values = values + lax.ppermute(values, 'param', by_xor(parties, step))  6.83 us
    ppermute x3, waiting for transfers between devices, local(): other = lax.ppermute(offsets, 'param', by_xor(parties, step))  3.83 us
  transfers between devices with their start and end apart: 17, of which 11 were waited for; matrix products, arithmetic and copies ran while one was open for 2% of the time, Pallas kernels for 15%

profile of v4, /device:TPU:0, one launch (start us, length us, event | category | flops | bytes accessed | tf_op | source)
XLA Modules:
  0.0 110.5 jit_solution(2584210722727804749)
XLA Ops:
  0.0 3.0 %collective-permute-start.2 = (bf16[384,512]{1,0:T(8,128)(2,1)}, bf16[384,512]{1,0:T(8,128)(2,1)S(1)}, u32[]{:S(2)}, u32[]{:S(2)}) collective-permute-start(bf16[384,512]{1,0:T(8,128)(2,1)} %bitcast.17), channel_id=1, source_target_pairs={{0,4},{4,8},{8,12},{12,14},{14,10},{10,6},{6,2},{2,0},{1,5},{5,9},... | collective-permute-start | bytes 1179656 | tf_op jit(solution)/shard_map/ppermute | solution.py:318
  3.0 1.9 %collective-permute-start = (s32[1024]{0:T(1024)}, s32[1024]{0:T(1024)S(1)}, u32[]{:S(2)}, u32[]{:S(2)}) collective-permute-start(s32[1024]{0:T(1024)} %param.7), channel_id=1, source_target_pairs={{0,2},{2,0},{4,6},{6,4},{8,10},{10,8},{12,14},{14,12},{1,3},{3,1},... | collective-permute-start | bytes 12296 | tf_op jit(solution)/shard_map/ppermute | solution.py:330
  5.0 6.9 %build_table.3.refs_0_ = f32[8960,128]{1,0:T(8,128)} custom-call(s32[1792,4096]{1,0:T(8,128)} %flips_ref.5, bf16[384,1792]{1,0:T(8,128)(2,1)} %bitcast.12), custom_call_target="tpu_custom_call" | custom-call | flops 6291456 | bytes 12582912 | tf_op jit(solution)/shard_map/build_table/pallas_call | solution.py:68
  12.4 1.2 %collective-permute-start.1 = (s32[2048]{0:T(1024)S(1)}, s32[2048]{0:T(1024)S(1)}, u32[]{:S(2)}, u32[]{:S(2)}) collective-permute-start(s32[2048]{0:T(1024)S(1)} %add_select_fusion.2), channel_id=1, source_target_pairs={{0,4},{2,6},{4,0},{6,2},{8,12},{10,14},{12,8},{14,10},{1,5},{3,7},... | collective-permute-start | bytes 24584 | tf_op jit(solution)/shard_map/ppermute | solution.py:330
  13.6 4.9 %build_table.4.refs_0_ = f32[8960,128]{1,0:T(8,128)} custom-call(s32[1792,4096]{1,0:T(8,128)} %flips_ref.5, bf16[384,1792]{1,0:T(8,128)(2,1)} %bitcast.13, f32[8960,128]{1,0:T(8,128)} %build_table.3.refs_0_), custom_call_target="tpu_custom_call", output_to_operand_aliasing={{}: (2, {})} | custom-call | flops 4194304 | bytes 8388608 | tf_op jit(solution)/shard_map/build_table/pallas_call | solution.py:68
  19.4 1.2 %collective-permute-start.6 = (bf16[384,512]{1,0:T(8,128)(2,1)S(1)}, bf16[384,512]{1,0:T(8,128)(2,1)S(1)}, u32[]{:S(2)}, u32[]{:S(2)}) collective-permute-start(bf16[384,512]{1,0:T(8,128)(2,1)S(1)} %collective-permute-done.3.refs_2_), channel_id=1, source_target_pairs={{4,0},{8,4},{12,8},{14,12},{10,14},{6,10},{2,6},{0,2},{5,1},{9,5},... | collective-permute-start | bytes 1179656 | tf_op jit(solution)/shard_map/ppermute | solution.py:318
  20.6 4.4 %collective-permute-start.4 = (s32[4096]{0:T(1024)S(1)}, s32[4096]{0:T(1024)S(1)}, u32[]{:S(2)}, u32[]{:S(2)}) collective-permute-start(s32[4096]{0:T(1024)S(1)} %add_select_fusion.1), channel_id=1, source_target_pairs={{0,8},{2,10},{4,12},{6,14},{8,0},{10,2},{12,4},{14,6},{1,9},{3,11}... | collective-permute-start | bytes 49160 | tf_op jit(solution)/shard_map/ppermute | solution.py:330
  25.0 4.9 %build_table.5.table_ref = f32[8960,128]{1,0:T(8,128)} custom-call(s32[1792,4096]{1,0:T(8,128)} %flips_ref.5, bf16[384,1792]{1,0:T(8,128)(2,1)} %bitcast.14, f32[8960,128]{1,0:T(8,128)} %build_table.4.refs_0_), custom_call_target="tpu_custom_call", output_to_operand_aliasing={{}: (2, {})} | custom-call | flops 4194304 | bytes 8388608 | tf_op jit(solution)/shard_map/build_table/pallas_call | solution.py:68
  29.9 3.4 %collective-permute-done.4 = s32[4096]{0:T(1024)S(1)} collective-permute-done((s32[4096]{0:T(1024)S(1)}, s32[4096]{0:T(1024)S(1)}, u32[]{:S(2)}, u32[]{:S(2)}) %collective-permute-start.4) | collective-permute-done | bytes 16416 | tf_op jit(solution)/shard_map/ppermute | solution.py:330
  33.4 2.0 %collective-permute-start.7 = (bf16[384,512]{1,0:T(8,128)(2,1)S(1)}, bf16[384,512]{1,0:T(8,128)(2,1)S(1)}, u32[]{:S(2)}, u32[]{:S(2)}) collective-permute-start(bf16[384,512]{1,0:T(8,128)(2,1)S(1)} %collective-permute-done.5.refs_3_), channel_id=1, source_target_pairs={{0,4},{4,8},{8,12},{12,14},{14,10},{10,6},{6,2},{2,0},{1,5},{5,9},... | collective-permute-start | bytes 1179656 | tf_op jit(solution)/shard_map/ppermute | solution.py:318
  36.0 7.2 %collective-permute-done.8.refs_6_ = bf16[384,512]{1,0:T(8,128)(2,1)S(1)} collective-permute-done((bf16[384,512]{1,0:T(8,128)(2,1)S(1)}, bf16[384,512]{1,0:T(8,128)(2,1)S(1)}, u32[]{:S(2)}, u32[]{:S(2)}) %collective-permute-start.8) | collective-permute-done | bytes 393248 | tf_op jit(solution)/shard_map/ppermute | solution.py:318
  43.3 2.0 %collective-permute-start.9 = (bf16[192,512]{1,0:T(8,128)(2,1)S(1)}, bf16[192,512]{1,0:T(8,128)(2,1)S(1)}, u32[]{:S(2)}, u32[]{:S(2)}) collective-permute-start(bf16[192,512]{1,0:T(8,128)(2,1)S(1)} %slice.16), channel_id=1, source_target_pairs={{0,4},{4,8},{8,12},{12,14},{14,10},{10,6},{6,2},{2,0},{1,5},{5,9},... | collective-permute-start | bytes 589832 | tf_op jit(solution)/shard_map/ppermute | solution.py:318
  46.6 2.3 %collective-permute-done.10 = bf16[192,512]{1,0:T(8,128)(2,1)S(1)} collective-permute-done((bf16[192,512]{1,0:T(8,128)(2,1)S(1)}, bf16[192,512]{1,0:T(8,128)(2,1)S(1)}, u32[]{:S(2)}, u32[]{:S(2)}) %collective-permute-start.10) | collective-permute-done | bytes 196640 | tf_op jit(solution)/shard_map/ppermute | solution.py:318
  49.8 40.8 %sample_whole.1 = f32[3,8192]{1,0:T(4,128)} custom-call(s32[9]{0:T(128)} %stack.36.scalars, s32[8192]{0:T(1024)} %fusion.1.rows_ref, s32[1,8192]{1,0:T(1,128)} %broadcast_select_fusion.offsets_ref, f32[8960,128]{1,0:T(8,128)} %build_table.5.table_ref, bf16[384,512]{1,0:T(8,128)(2,1)} %bitcast.19, bf16[384,512]{1,0:T(8,128)(2,1)} %copy-done.3, ...), custom_call_target="tpu_custom_call" | custom-call | flops 25769803776 | bytes 18874368 | tf_op jit(solution)/shard_map/sample_whole/pallas_call | solution.py:205
  90.6 0.9 fusion.2
  91.5 2.0 %collective-permute-start.14 = (f32[3,4096]{1,0:T(4,128)S(1)}, f32[3,4096]{1,0:T(4,128)S(1)}, u32[]{:S(2)}, u32[]{:S(2)}) collective-permute-start(f32[3,4096]{1,0:T(4,128)S(1)} %get-tuple-element.32), channel_id=1, source_target_pairs={{0,2},{2,0},{4,6},{6,4},{8,10},{10,8},{12,14},{14,12},{1,3},{3,1},... | collective-permute-start | bytes 147464 | tf_op jit(solution)/shard_map/ppermute | solution.py:288
  93.5 2.2 %collective-permute-done.11 = f32[3,4096]{1,0:T(4,128)S(1)} collective-permute-done((f32[3,4096]{1,0:T(4,128)S(1)}, f32[3,4096]{1,0:T(4,128)S(1)}, u32[]{:S(2)}, u32[]{:S(2)}) %collective-permute-start.11) | collective-permute-done | bytes 49184 | tf_op jit(solution)/shard_map/ppermute | solution.py:288
  96.5 0.9 slice_add_fusion.1
  97.4 2.1 %collective-permute-start.15 = (f32[3,4096]{1,0:T(4,128)S(1)}, f32[3,4096]{1,0:T(4,128)S(1)}, u32[]{:S(2)}, u32[]{:S(2)}) collective-permute-start(f32[3,4096]{1,0:T(4,128)S(1)} %get-tuple-element.30), channel_id=1, source_target_pairs={{0,4},{2,6},{4,0},{6,2},{8,12},{10,14},{12,8},{14,10},{1,5},{3,7},... | collective-permute-start | bytes 147464 | tf_op jit(solution)/shard_map/ppermute | solution.py:288
  99.6 2.2 %collective-permute-done.15 = f32[3,4096]{1,0:T(4,128)S(1)} collective-permute-done((f32[3,4096]{1,0:T(4,128)S(1)}, f32[3,4096]{1,0:T(4,128)S(1)}, u32[]{:S(2)}, u32[]{:S(2)}) %collective-permute-start.15) | collective-permute-done | bytes 49184 | tf_op jit(solution)/shard_map/ppermute | solution.py:288
  101.8 1.5 %collective-permute-start.16 = (f32[3,4096]{1,0:T(4,128)S(1)}, f32[3,4096]{1,0:T(4,128)S(1)}, u32[]{:S(2)}, u32[]{:S(2)}) collective-permute-start(f32[3,4096]{1,0:T(4,128)S(1)} %add.112), channel_id=1, source_target_pairs={{0,8},{2,10},{4,12},{6,14},{8,0},{10,2},{12,4},{14,6},{1,9},{3,11}... | collective-permute-start | bytes 147464 | tf_op jit(solution)/shard_map/ppermute | solution.py:288
  103.8 1.1 collective-permute-start.13
  104.8 2.1 %collective-permute-done.16 = f32[3,4096]{1,0:T(4,128)S(1)} collective-permute-done((f32[3,4096]{1,0:T(4,128)S(1)}, f32[3,4096]{1,0:T(4,128)S(1)}, u32[]{:S(2)}, u32[]{:S(2)}) %collective-permute-start.16) | collective-permute-done | bytes 49184 | tf_op jit(solution)/shard_map/ppermute | solution.py:288
  107.0 2.8 %collective-permute-done.13 = f32[3,4096]{1,0:T(4,128)S(1)} collective-permute-done((f32[3,4096]{1,0:T(4,128)S(1)}, f32[3,4096]{1,0:T(4,128)S(1)}, u32[]{:S(2)}, u32[]{:S(2)}) %collective-permute-start.13) | collective-permute-done | bytes 49184 | tf_op jit(solution)/shard_map/ppermute | solution.py:288
  (43 shorter events, 6.3 us)
Async XLA Ops:
  0.0 18.5 %collective-permute-start.2 = (bf16[384,512]{1,0:T(8,128)(2,1)}, bf16[384,512]{1,0:T(8,128)(2,1)S(1)}, u32[]{:S(2)}, u32[]{:S(2)}) collective-permute-start(bf16[384,512]{1,0:T(8,128)(2,1)} %bitcast.17), channel_id=1, source_target_pairs={{0,4},{4,8},{8,12},{12,14},{14,10},{10,6},{6,2},{2,0},{1,5},{5,9},... | collective-permute-start | bytes 1179656 | tf_op jit(solution)/shard_map/ppermute | solution.py:318
  3.0 15.5 %collective-permute-start.3 = (bf16[384,512]{1,0:T(8,128)(2,1)}, bf16[384,512]{1,0:T(8,128)(2,1)S(1)}, u32[]{:S(2)}, u32[]{:S(2)}) collective-permute-start(bf16[384,512]{1,0:T(8,128)(2,1)} %bitcast.18), channel_id=1, source_target_pairs={{4,0},{8,4},{12,8},{14,12},{10,14},{6,10},{2,6},{0,2},{5,1},{9,5},... | collective-permute-start | bytes 1179656 | tf_op jit(solution)/shard_map/ppermute | solution.py:318
  3.0 9.3 %collective-permute-start = (s32[1024]{0:T(1024)}, s32[1024]{0:T(1024)S(1)}, u32[]{:S(2)}, u32[]{:S(2)}) collective-permute-start(s32[1024]{0:T(1024)} %param.7), channel_id=1, source_target_pairs={{0,2},{2,0},{4,6},{6,4},{8,10},{10,8},{12,14},{14,12},{1,3},{3,1},... | collective-permute-start | bytes 12296 | tf_op jit(solution)/shard_map/ppermute | solution.py:330
  5.0 7.4 %copy-start.2 = (s32[1024]{0:T(1024)S(1)}, s32[1024]{0:T(1024)}, u32[]{:S(2)}) copy-start(s32[1024]{0:T(1024)} %param.7) | copy-start | bytes 12292
  12.4 6.1 %collective-permute-start.1 = (s32[2048]{0:T(1024)S(1)}, s32[2048]{0:T(1024)S(1)}, u32[]{:S(2)}, u32[]{:S(2)}) collective-permute-start(s32[2048]{0:T(1024)S(1)} %add_select_fusion.2), channel_id=1, source_target_pairs={{0,4},{2,6},{4,0},{6,2},{8,12},{10,14},{12,8},{14,10},{1,5},{3,7},... | collective-permute-start | bytes 24584 | tf_op jit(solution)/shard_map/ppermute | solution.py:330
  18.5 11.4 %copy-start.3 = (bf16[384,512]{1,0:T(8,128)(2,1)}, bf16[384,512]{1,0:T(8,128)(2,1)S(1)}, u32[]{:S(2)}) copy-start(bf16[384,512]{1,0:T(8,128)(2,1)S(1)} %collective-permute-done.2.refs_1_) | copy-start | bytes 1179652
  18.5 11.4 %copy-start.4 = (bf16[384,512]{1,0:T(8,128)(2,1)}, bf16[384,512]{1,0:T(8,128)(2,1)S(1)}, u32[]{:S(2)}) copy-start(bf16[384,512]{1,0:T(8,128)(2,1)S(1)} %collective-permute-done.3.refs_2_) | copy-start | bytes 1179652
  18.5 14.8 %collective-permute-start.5 = (bf16[384,512]{1,0:T(8,128)(2,1)S(1)}, bf16[384,512]{1,0:T(8,128)(2,1)S(1)}, u32[]{:S(2)}, u32[]{:S(2)}) collective-permute-start(bf16[384,512]{1,0:T(8,128)(2,1)S(1)} %collective-permute-done.2.refs_1_), channel_id=1, source_target_pairs={{0,4},{4,8},{8,12},{12,14},{14,10},{10,6},{6,2},{2,0},{1,5},{5,9},... | collective-permute-start | bytes 1179656 | tf_op jit(solution)/shard_map/ppermute | solution.py:318
  19.4 13.9 %collective-permute-start.6 = (bf16[384,512]{1,0:T(8,128)(2,1)S(1)}, bf16[384,512]{1,0:T(8,128)(2,1)S(1)}, u32[]{:S(2)}, u32[]{:S(2)}) collective-permute-start(bf16[384,512]{1,0:T(8,128)(2,1)S(1)} %collective-permute-done.3.refs_2_), channel_id=1, source_target_pairs={{4,0},{8,4},{12,8},{14,12},{10,14},{6,10},{2,6},{0,2},{5,1},{9,5},... | collective-permute-start | bytes 1179656 | tf_op jit(solution)/shard_map/ppermute | solution.py:318
  20.6 12.7 %collective-permute-start.4 = (s32[4096]{0:T(1024)S(1)}, s32[4096]{0:T(1024)S(1)}, u32[]{:S(2)}, u32[]{:S(2)}) collective-permute-start(s32[4096]{0:T(1024)S(1)} %add_select_fusion.1), channel_id=1, source_target_pairs={{0,8},{2,10},{4,12},{6,14},{8,0},{10,2},{12,4},{14,6},{1,9},{3,11}... | collective-permute-start | bytes 49160 | tf_op jit(solution)/shard_map/ppermute | solution.py:330
  33.3 16.5 %copy-start.5 = (bf16[384,512]{1,0:T(8,128)(2,1)}, bf16[384,512]{1,0:T(8,128)(2,1)S(1)}, u32[]{:S(2)}) copy-start(bf16[384,512]{1,0:T(8,128)(2,1)S(1)} %collective-permute-done.5.refs_3_) | copy-start | bytes 1179652
  33.3 16.5 %copy-start.6 = (bf16[384,512]{1,0:T(8,128)(2,1)}, bf16[384,512]{1,0:T(8,128)(2,1)S(1)}, u32[]{:S(2)}) copy-start(bf16[384,512]{1,0:T(8,128)(2,1)S(1)} %collective-permute-done.6.refs_4_) | copy-start | bytes 1179652
  33.3 9.9 %collective-permute-start.8 = (bf16[384,512]{1,0:T(8,128)(2,1)S(1)}, bf16[384,512]{1,0:T(8,128)(2,1)S(1)}, u32[]{:S(2)}, u32[]{:S(2)}) collective-permute-start(bf16[384,512]{1,0:T(8,128)(2,1)S(1)} %collective-permute-done.6.refs_4_), channel_id=1, source_target_pairs={{4,0},{8,4},{12,8},{14,12},{10,14},{6,10},{2,6},{0,2},{5,1},{9,5},... | collective-permute-start | bytes 1179656 | tf_op jit(solution)/shard_map/ppermute | solution.py:318
  33.4 9.9 %collective-permute-start.7 = (bf16[384,512]{1,0:T(8,128)(2,1)S(1)}, bf16[384,512]{1,0:T(8,128)(2,1)S(1)}, u32[]{:S(2)}, u32[]{:S(2)}) collective-permute-start(bf16[384,512]{1,0:T(8,128)(2,1)S(1)} %collective-permute-done.5.refs_3_), channel_id=1, source_target_pairs={{0,4},{4,8},{8,12},{12,14},{14,10},{10,6},{6,2},{2,0},{1,5},{5,9},... | collective-permute-start | bytes 1179656 | tf_op jit(solution)/shard_map/ppermute | solution.py:318
  43.2 6.6 %copy-start = (bf16[384,512]{1,0:T(8,128)(2,1)}, bf16[384,512]{1,0:T(8,128)(2,1)S(1)}, u32[]{:S(2)}) copy-start(bf16[384,512]{1,0:T(8,128)(2,1)S(1)} %collective-permute-done.8.refs_6_) | copy-start | bytes 1179652
  43.2 5.7 %collective-permute-start.10 = (bf16[192,512]{1,0:T(8,128)(2,1)S(1)}, bf16[192,512]{1,0:T(8,128)(2,1)S(1)}, u32[]{:S(2)}, u32[]{:S(2)}) collective-permute-start(bf16[192,512]{1,0:T(8,128)(2,1)S(1)} %slice.17), channel_id=1, source_target_pairs={{4,0},{8,4},{12,8},{14,12},{10,14},{6,10},{2,6},{0,2},{5,1},{9,5},... | collective-permute-start | bytes 589832 | tf_op jit(solution)/shard_map/ppermute | solution.py:318
  43.3 6.5 %copy-start.1 = (bf16[384,512]{1,0:T(8,128)(2,1)}, bf16[384,512]{1,0:T(8,128)(2,1)S(1)}, u32[]{:S(2)}) copy-start(bf16[384,512]{1,0:T(8,128)(2,1)S(1)} %collective-permute-done.7.refs_5_) | copy-start | bytes 1179652
  43.3 5.7 %collective-permute-start.9 = (bf16[192,512]{1,0:T(8,128)(2,1)S(1)}, bf16[192,512]{1,0:T(8,128)(2,1)S(1)}, u32[]{:S(2)}, u32[]{:S(2)}) collective-permute-start(bf16[192,512]{1,0:T(8,128)(2,1)S(1)} %slice.16), channel_id=1, source_target_pairs={{0,4},{4,8},{8,12},{12,14},{14,10},{10,6},{6,2},{2,0},{1,5},{5,9},... | collective-permute-start | bytes 589832 | tf_op jit(solution)/shard_map/ppermute | solution.py:318
  91.5 4.3 %collective-permute-start.11 = (f32[3,4096]{1,0:T(4,128)S(1)}, f32[3,4096]{1,0:T(4,128)S(1)}, u32[]{:S(2)}, u32[]{:S(2)}) collective-permute-start(f32[3,4096]{1,0:T(4,128)S(1)} %get-tuple-element.31), channel_id=1, source_target_pairs={{0,2},{2,0},{4,6},{6,4},{8,10},{10,8},{12,14},{14,12},{1,3},{3,1},... | collective-permute-start | bytes 147464 | tf_op jit(solution)/shard_map/ppermute | solution.py:288
  91.5 5.0 %collective-permute-start.14 = (f32[3,4096]{1,0:T(4,128)S(1)}, f32[3,4096]{1,0:T(4,128)S(1)}, u32[]{:S(2)}, u32[]{:S(2)}) collective-permute-start(f32[3,4096]{1,0:T(4,128)S(1)} %get-tuple-element.32), channel_id=1, source_target_pairs={{0,2},{2,0},{4,6},{6,4},{8,10},{10,8},{12,14},{14,12},{1,3},{3,1},... | collective-permute-start | bytes 147464 | tf_op jit(solution)/shard_map/ppermute | solution.py:288
  97.4 4.3 %collective-permute-start.15 = (f32[3,4096]{1,0:T(4,128)S(1)}, f32[3,4096]{1,0:T(4,128)S(1)}, u32[]{:S(2)}, u32[]{:S(2)}) collective-permute-start(f32[3,4096]{1,0:T(4,128)S(1)} %get-tuple-element.30), channel_id=1, source_target_pairs={{0,4},{2,6},{4,0},{6,2},{8,12},{10,14},{12,8},{14,10},{1,5},{3,7},... | collective-permute-start | bytes 147464 | tf_op jit(solution)/shard_map/ppermute | solution.py:288
  99.5 4.3 %collective-permute-start.12 = (f32[3,4096]{1,0:T(4,128)S(1)}, f32[3,4096]{1,0:T(4,128)S(1)}, u32[]{:S(2)}, u32[]{:S(2)}) collective-permute-start(f32[3,4096]{1,0:T(4,128)S(1)} %get-tuple-element.29), channel_id=1, source_target_pairs={{0,4},{2,6},{4,0},{6,2},{8,12},{10,14},{12,8},{14,10},{1,5},{3,7},... | collective-permute-start | bytes 147464 | tf_op jit(solution)/shard_map/ppermute | solution.py:288
  101.8 5.2 %collective-permute-start.16 = (f32[3,4096]{1,0:T(4,128)S(1)}, f32[3,4096]{1,0:T(4,128)S(1)}, u32[]{:S(2)}, u32[]{:S(2)}) collective-permute-start(f32[3,4096]{1,0:T(4,128)S(1)} %add.112), channel_id=1, source_target_pairs={{0,8},{2,10},{4,12},{6,14},{8,0},{10,2},{12,4},{14,6},{1,9},{3,11}... | collective-permute-start | bytes 147464 | tf_op jit(solution)/shard_map/ppermute | solution.py:288
  103.8 6.1 %collective-permute-start.13 = (f32[3,4096]{1,0:T(4,128)S(1)}, f32[3,4096]{1,0:T(4,128)S(1)}, u32[]{:S(2)}, u32[]{:S(2)}) collective-permute-start(f32[3,4096]{1,0:T(4,128)S(1)} %add.109), channel_id=1, source_target_pairs={{0,8},{2,10},{4,12},{6,14},{8,0},{10,2},{12,4},{14,6},{1,9},{3,11}... | collective-permute-start | bytes 147464 | tf_op jit(solution)/shard_map/ppermute | solution.py:288

commit v5 on v4

--- a/solution.py
+++ b/solution.py
@@ -220,7 +220,7 @@
             ],
         ),
         out_shape=out_shape,
-        compiler_params=pltpu.CompilerParams(vmem_limit_bytes=56 * MIB),
+        compiler_params=pltpu.CompilerParams(vmem_limit_bytes=44 * MIB),
         cost_estimate=pl.CostEstimate(
             flops=2 * tokens * depth * len(cotangents) * count, bytes_accessed=6 * tokens * count, transcendentals=0
         ),
@@ -283,10 +283,10 @@
 
 
 def sum_shards(values, parties):
-    step = 1
-    while step < parties:
+    step = parties // 2
+    while step > 0:
         values = values + lax.ppermute(values, "param", by_xor(parties, step))
-        step *= 2
+        step //= 2
     return values
 
 
@@ -318,6 +318,7 @@
             return lax.ppermute(ahead, "param", forward), lax.ppermute(behind, "param", backward)
 
         ahead, behind = pass_on(held, held)
+        arrived = []
 
     units = hidden.reshape(flat, rows)
     if rows % LANES:
@@ -333,8 +334,10 @@
             table = build_table(sign_flips, units, table, examples, tile, (built, until - built))
             built = until
             table, other = lax.optimization_barrier((table, other))
-        if ringed and at == 1:
+        if ringed and at + 1 < min(steps, parties // 2):
             table, ahead, behind = lax.optimization_barrier((table, ahead, behind))
+            arrived += [ahead, behind]
+            ahead, behind = pass_on(ahead, behind)
         offsets = jnp.where(
             (own & step) == 0, jnp.concatenate([offsets, other]), jnp.concatenate([other, offsets])
         )
@@ -360,15 +363,15 @@
 
     if ringed:
         for step in range(1, parties // 2):
-            pieces += [ahead, behind]
+            if len(arrived) < 2 * step:
+                arrived += [ahead, behind]
+                if step + 1 < parties // 2:
+                    ahead, behind = pass_on(ahead, behind)
+                else:
+                    middle = flat // 2
+                    ahead, behind = pass_on(ahead[:middle], behind[middle:])
+            pieces += arrived[2 * step - 2:2 * step]
             numbers += [shard_at(place - step), shard_at(place + step)]
-            if step == 2:
-                ahead, behind, table = lax.optimization_barrier((ahead, behind, table))
-            if step + 1 < parties // 2:
-                ahead, behind = pass_on(ahead, behind)
-            else:
-                middle = flat // 2
-                ahead, behind = pass_on(ahead[:middle], behind[middle:])
             if step > 1 and len(sampled) < len(EARLY):
                 signs, picked, total = sample_next(False)
                 ahead, behind, signs = lax.optimization_barrier((ahead, behind, signs))

time: 111 us -> 99.2 us (0.89)
  Pallas kernels: 57.5 us -> 52.9 us
  waiting for transfers between devices: 24 us -> 20.1 us
  other arithmetic: 3.68 us -> 0.86 us
    pallas_call x1, Pallas kernels: 40.8 us -> 36.2 us  [sample(): pl.pallas_call(functools.partial(sample_kernel, blocks=len(cotangents), e...]
    ppermute x4, waiting for transfers between devices: 9.5 us -> 4.97 us  [pass_on(): lax.ppermute(behind, 'param', backward)]
    unnamed x14 -> x6, local copies, waits for them, and re-layouts: 0.03 us -> 2.3 us
    ppermute x3, starting transfers between devices: 7.57 us -> 6.11 us  [local(): other = lax.ppermute(offsets, 'param', by_xor(parties, step))]
  transfers between devices with their start and end apart: 17 -> 17, of which waited for: 11 -> 12; matrix products, arithmetic and copies ran while one was open for 2% -> 0% of each run, Pallas kernels for 15% -> 17%
where the time goes in v5:
time: 99.2 us; the launch traced here: 99 us
  Pallas kernels  52.9 us (53%)
  starting transfers between devices  22.6 us (23%)
  waiting for transfers between devices  20.1 us (20%)
  local copies, waits for them, and re-layouts  2.44 us (2%)
    pallas_call x1, Pallas kernels, sample(): pl.pallas_call(functools.partial(sample_kernel, blocks=len(cotangents), e...  36.2 us
    pallas_call x3, Pallas kernels, build_table(): pl.pallas_call(functools.partial(table_kernel, examples=examples), grid=(...  16.7 us
    ppermute x6, waiting for transfers between devices, sum_shards(): values = values + lax.ppermute(values, 'param', by_xor(parties, step))  11.1 us
    ppermute x4, starting transfers between devices, pass_on(): lax.ppermute(ahead, 'param', forward)  7.89 us
    ppermute x6, starting transfers between devices, sum_shards(): values = values + lax.ppermute(values, 'param', by_xor(parties, step))  6.69 us
    ppermute x3, starting transfers between devices, local(): other = lax.ppermute(offsets, 'param', by_xor(parties, step))  6.11 us
    ppermute x4, waiting for transfers between devices, pass_on(): lax.ppermute(behind, 'param', backward)  4.97 us
    ppermute x3, waiting for transfers between devices, local(): other = lax.ppermute(offsets, 'param', by_xor(parties, step))  3.41 us
  transfers between devices with their start and end apart: 17, of which 12 were waited for; matrix products, arithmetic and copies ran while one was open for 0% of the time, Pallas kernels for 17%

profile of v5, /device:TPU:0, one launch (start us, length us, event | category | flops | bytes accessed | tf_op | source)
XLA Modules:
  0.0 99.0 jit_solution(14872489873658727057)
XLA Ops:
  0.0 3.0 %collective-permute-start.1 = (bf16[384,512]{1,0:T(8,128)(2,1)}, bf16[384,512]{1,0:T(8,128)(2,1)S(1)}, u32[]{:S(2)}, u32[]{:S(2)}) collective-permute-start(bf16[384,512]{1,0:T(8,128)(2,1)} %bitcast.12), channel_id=1, source_target_pairs={{0,4},{4,8},{8,12},{12,14},{14,10},{10,6},{6,2},{2,0},{1,5},{5,9},... | collective-permute-start | bytes 1179656 | tf_op jit(solution)/shard_map/ppermute | solution.py:318
  3.0 1.9 %collective-permute-start = (s32[1024]{0:T(1024)}, s32[1024]{0:T(1024)S(1)}, u32[]{:S(2)}, u32[]{:S(2)}) collective-permute-start(s32[1024]{0:T(1024)} %param.7), channel_id=1, source_target_pairs={{0,2},{2,0},{4,6},{6,4},{8,10},{10,8},{12,14},{14,12},{1,3},{3,1},... | collective-permute-start | bytes 12296 | tf_op jit(solution)/shard_map/ppermute | solution.py:331
  5.0 6.9 %build_table.3.refs_0_ = f32[8960,128]{1,0:T(8,128)} custom-call(s32[1792,4096]{1,0:T(8,128)} %flips_ref.5, bf16[384,1792]{1,0:T(8,128)(2,1)} %bitcast.15), custom_call_target="tpu_custom_call" | custom-call | flops 6291456 | bytes 12582912 | tf_op jit(solution)/shard_map/build_table/pallas_call | solution.py:68
  12.4 1.5 %collective-permute-done.2.refs_2_ = bf16[384,512]{1,0:T(8,128)(2,1)S(1)} collective-permute-done((bf16[384,512]{1,0:T(8,128)(2,1)}, bf16[384,512]{1,0:T(8,128)(2,1)S(1)}, u32[]{:S(2)}, u32[]{:S(2)}) %collective-permute-start.2) | collective-permute-done | bytes 393248 | tf_op jit(solution)/shard_map/ppermute | solution.py:318
  13.8 1.6 %collective-permute-start.4 = (bf16[384,512]{1,0:T(8,128)(2,1)S(1)}, bf16[384,512]{1,0:T(8,128)(2,1)S(1)}, u32[]{:S(2)}, u32[]{:S(2)}) collective-permute-start(bf16[384,512]{1,0:T(8,128)(2,1)S(1)} %collective-permute-done.1.refs_1_), channel_id=1, source_target_pairs={{0,4},{4,8},{8,12},{12,14},{14,10},{10,6},{6,2},{2,0},{1,5},{5,9},... | collective-permute-start | bytes 1179656 | tf_op jit(solution)/shard_map/ppermute | solution.py:318
  15.8 1.6 %collective-permute-start.3 = (s32[2048]{0:T(1024)S(1)}, s32[2048]{0:T(1024)S(1)}, u32[]{:S(2)}, u32[]{:S(2)}) collective-permute-start(s32[2048]{0:T(1024)S(1)} %add_select_fusion.2), channel_id=1, source_target_pairs={{0,4},{2,6},{4,0},{6,2},{8,12},{10,14},{12,8},{14,10},{1,5},{3,7},... | collective-permute-start | bytes 24584 | tf_op jit(solution)/shard_map/ppermute | solution.py:331
  17.4 4.9 %build_table.4.refs_0_ = f32[8960,128]{1,0:T(8,128)} custom-call(s32[1792,4096]{1,0:T(8,128)} %flips_ref.5, bf16[384,1792]{1,0:T(8,128)(2,1)} %bitcast.16, f32[8960,128]{1,0:T(8,128)} %build_table.3.refs_0_), custom_call_target="tpu_custom_call", output_to_operand_aliasing={{}: (2, {})} | custom-call | flops 4194304 | bytes 8388608 | tf_op jit(solution)/shard_map/build_table/pallas_call | solution.py:68
  22.3 2.6 %collective-permute-done.3 = s32[2048]{0:T(1024)S(1)} collective-permute-done((s32[2048]{0:T(1024)S(1)}, s32[2048]{0:T(1024)S(1)}, u32[]{:S(2)}, u32[]{:S(2)}) %collective-permute-start.3) | collective-permute-done | bytes 8224 | tf_op jit(solution)/shard_map/ppermute | solution.py:331
  25.2 1.8 %collective-permute-start.7 = (bf16[384,512]{1,0:T(8,128)(2,1)S(1)}, bf16[384,512]{1,0:T(8,128)(2,1)S(1)}, u32[]{:S(2)}, u32[]{:S(2)}) collective-permute-start(bf16[384,512]{1,0:T(8,128)(2,1)S(1)} %collective-permute-done.4.refs_3_), channel_id=1, source_target_pairs={{0,4},{4,8},{8,12},{12,14},{14,10},{10,6},{6,2},{2,0},{1,5},{5,9},... | collective-permute-start | bytes 1179656 | tf_op jit(solution)/shard_map/ppermute | solution.py:318
  27.0 2.6 %collective-permute-start.6 = (s32[4096]{0:T(1024)S(1)}, s32[4096]{0:T(1024)S(1)}, u32[]{:S(2)}, u32[]{:S(2)}) collective-permute-start(s32[4096]{0:T(1024)S(1)} %add_select_fusion.1), channel_id=1, source_target_pairs={{0,8},{2,10},{4,12},{6,14},{8,0},{10,2},{12,4},{14,6},{1,9},{3,11}... | collective-permute-start | bytes 49160 | tf_op jit(solution)/shard_map/ppermute | solution.py:331
  29.7 4.9 %build_table.5.table_ref = f32[8960,128]{1,0:T(8,128)} custom-call(s32[1792,4096]{1,0:T(8,128)} %flips_ref.5, bf16[384,1792]{1,0:T(8,128)(2,1)} %bitcast.17, f32[8960,128]{1,0:T(8,128)} %build_table.4.refs_0_), custom_call_target="tpu_custom_call", output_to_operand_aliasing={{}: (2, {})} | custom-call | flops 4194304 | bytes 8388608 | tf_op jit(solution)/shard_map/build_table/pallas_call | solution.py:68
  34.9 1.2 %collective-permute-start.10 = (bf16[192,512]{1,0:T(8,128)(2,1)S(1)}, bf16[192,512]{1,0:T(8,128)(2,1)S(1)}, u32[]{:S(2)}, u32[]{:S(2)}) collective-permute-start(bf16[192,512]{1,0:T(8,128)(2,1)S(1)} %slice.17), channel_id=1, source_target_pairs={{4,0},{8,4},{12,8},{14,12},{10,14},{6,10},{2,6},{0,2},{5,1},{9,5},... | collective-permute-start | bytes 589832 | tf_op jit(solution)/shard_map/ppermute | solution.py:318
  36.1 1.5 %collective-permute-start.9 = (bf16[192,512]{1,0:T(8,128)(2,1)S(1)}, bf16[192,512]{1,0:T(8,128)(2,1)S(1)}, u32[]{:S(2)}, u32[]{:S(2)}) collective-permute-start(bf16[192,512]{1,0:T(8,128)(2,1)S(1)} %slice.16), channel_id=1, source_target_pairs={{0,4},{4,8},{8,12},{12,14},{14,10},{10,6},{6,2},{2,0},{1,5},{5,9},... | collective-permute-start | bytes 589832 | tf_op jit(solution)/shard_map/ppermute | solution.py:318
  37.7 3.5 %collective-permute-done.10 = bf16[192,512]{1,0:T(8,128)(2,1)S(1)} collective-permute-done((bf16[192,512]{1,0:T(8,128)(2,1)S(1)}, bf16[192,512]{1,0:T(8,128)(2,1)S(1)}, u32[]{:S(2)}, u32[]{:S(2)}) %collective-permute-start.10) | collective-permute-done | bytes 196640 | tf_op jit(solution)/shard_map/ppermute | solution.py:318
  41.9 2.3 %copy-done = f32[8960,128]{1,0:T(8,128)S(1)} copy-done((f32[8960,128]{1,0:T(8,128)S(1)}, f32[8960,128]{1,0:T(8,128)}, u32[]{:S(2)}) %copy-start) | copy-done | bytes 4587544
  44.2 36.2 %sample_whole.1 = f32[3,8192]{1,0:T(4,128)S(1)} custom-call(s32[9]{0:T(128)S(1)} %stack.36.scalars, s32[8192]{0:T(1024)S(1)} %fusion.1.rows_ref, s32[1,8192]{1,0:T(1,128)S(1)} %broadcast_select_fusion.offsets_ref, f32[8960,128]{1,0:T(8,128)S(1)} %copy-done, bf16[384,512]{1,0:T(8,128)(2,1)S(1)} %bitcast.14, ...), custom_call_target="tpu_custom_call" | custom-call | flops 25769803776 | bytes 18874368 | tf_op jit(solution)/shard_map/sample_whole/pallas_call | solution.py:205
  80.4 3.0 %collective-permute-start.11 = (f32[3,4096]{1,0:T(4,128)S(1)}, f32[3,4096]{1,0:T(4,128)S(1)}, u32[]{:S(2)}, u32[]{:S(2)}) collective-permute-start(f32[3,4096]{1,0:T(4,128)S(1)} %get-tuple-element.31), channel_id=1, source_target_pairs={{0,8},{2,10},{4,12},{6,14},{8,0},{10,2},{12,4},{14,6},{1,9},{3,11}... | collective-permute-start | bytes 147464 | tf_op jit(solution)/shard_map/ppermute | solution.py:288
  83.4 2.3 %collective-permute-done.11 = f32[3,4096]{1,0:T(4,128)S(1)} collective-permute-done((f32[3,4096]{1,0:T(4,128)S(1)}, f32[3,4096]{1,0:T(4,128)S(1)}, u32[]{:S(2)}, u32[]{:S(2)}) %collective-permute-start.11) | collective-permute-done | bytes 49184 | tf_op jit(solution)/shard_map/ppermute | solution.py:288
  85.7 3.2 %collective-permute-done.14 = f32[3,4096]{1,0:T(4,128)S(1)} collective-permute-done((f32[3,4096]{1,0:T(4,128)S(1)}, f32[3,4096]{1,0:T(4,128)S(1)}, u32[]{:S(2)}, u32[]{:S(2)}) %collective-permute-start.14) | collective-permute-done | bytes 49184 | tf_op jit(solution)/shard_map/ppermute | solution.py:288
  89.0 2.0 %collective-permute-start.15 = (f32[3,4096]{1,0:T(4,128)S(1)}, f32[3,4096]{1,0:T(4,128)S(1)}, u32[]{:S(2)}, u32[]{:S(2)}) collective-permute-start(f32[3,4096]{1,0:T(4,128)S(1)} %get-tuple-element.30), channel_id=1, source_target_pairs={{0,4},{2,6},{4,0},{6,2},{8,12},{10,14},{12,8},{14,10},{1,5},{3,7},... | collective-permute-start | bytes 147464 | tf_op jit(solution)/shard_map/ppermute | solution.py:288
  91.0 2.2 %collective-permute-done.12 = f32[3,4096]{1,0:T(4,128)S(1)} collective-permute-done((f32[3,4096]{1,0:T(4,128)S(1)}, f32[3,4096]{1,0:T(4,128)S(1)}, u32[]{:S(2)}, u32[]{:S(2)}) %collective-permute-start.12) | collective-permute-done | bytes 49184 | tf_op jit(solution)/shard_map/ppermute | solution.py:288
  94.0 1.5 %collective-permute-start.16 = (f32[3,4096]{1,0:T(4,128)S(1)}, f32[3,4096]{1,0:T(4,128)S(1)}, u32[]{:S(2)}, u32[]{:S(2)}) collective-permute-start(f32[3,4096]{1,0:T(4,128)S(1)} %add.112), channel_id=1, source_target_pairs={{0,2},{2,0},{4,6},{6,4},{8,10},{10,8},{12,14},{14,12},{1,3},{3,1},... | collective-permute-start | bytes 147464 | tf_op jit(solution)/shard_map/ppermute | solution.py:288
  95.5 2.1 %collective-permute-done.13 = f32[3,4096]{1,0:T(4,128)S(1)} collective-permute-done((f32[3,4096]{1,0:T(4,128)S(1)}, f32[3,4096]{1,0:T(4,128)S(1)}, u32[]{:S(2)}, u32[]{:S(2)}) %collective-permute-start.13) | collective-permute-done | bytes 49184 | tf_op jit(solution)/shard_map/ppermute | solution.py:288
  98.3 0.7 pad_maximum_fusion.1
  (35 shorter events, 4.0 us)
Async XLA Ops:
  0.0 12.4 %collective-permute-start.1 = (bf16[384,512]{1,0:T(8,128)(2,1)}, bf16[384,512]{1,0:T(8,128)(2,1)S(1)}, u32[]{:S(2)}, u32[]{:S(2)}) collective-permute-start(bf16[384,512]{1,0:T(8,128)(2,1)} %bitcast.12), channel_id=1, source_target_pairs={{0,4},{4,8},{8,12},{12,14},{14,10},{10,6},{6,2},{2,0},{1,5},{5,9},... | collective-permute-start | bytes 1179656 | tf_op jit(solution)/shard_map/ppermute | solution.py:318
  3.0 10.8 %collective-permute-start.2 = (bf16[384,512]{1,0:T(8,128)(2,1)}, bf16[384,512]{1,0:T(8,128)(2,1)S(1)}, u32[]{:S(2)}, u32[]{:S(2)}) collective-permute-start(bf16[384,512]{1,0:T(8,128)(2,1)} %bitcast.13), channel_id=1, source_target_pairs={{4,0},{8,4},{12,8},{14,12},{10,14},{6,10},{2,6},{0,2},{5,1},{9,5},... | collective-permute-start | bytes 1179656 | tf_op jit(solution)/shard_map/ppermute | solution.py:318
  3.0 9.3 %collective-permute-start = (s32[1024]{0:T(1024)}, s32[1024]{0:T(1024)S(1)}, u32[]{:S(2)}, u32[]{:S(2)}) collective-permute-start(s32[1024]{0:T(1024)} %param.7), channel_id=1, source_target_pairs={{0,2},{2,0},{4,6},{6,4},{8,10},{10,8},{12,14},{14,12},{1,3},{3,1},... | collective-permute-start | bytes 12296 | tf_op jit(solution)/shard_map/ppermute | solution.py:331
  5.0 10.9 %copy-start.2 = (s32[1024]{0:T(1024)S(1)}, s32[1024]{0:T(1024)}, u32[]{:S(2)}) copy-start(s32[1024]{0:T(1024)} %param.7) | copy-start | bytes 12292
  13.8 11.1 %collective-permute-start.4 = (bf16[384,512]{1,0:T(8,128)(2,1)S(1)}, bf16[384,512]{1,0:T(8,128)(2,1)S(1)}, u32[]{:S(2)}, u32[]{:S(2)}) collective-permute-start(bf16[384,512]{1,0:T(8,128)(2,1)S(1)} %collective-permute-done.1.refs_1_), channel_id=1, source_target_pairs={{0,4},{4,8},{8,12},{12,14},{14,10},{10,6},{6,2},{2,0},{1,5},{5,9},... | collective-permute-start | bytes 1179656 | tf_op jit(solution)/shard_map/ppermute | solution.py:318
  15.4 9.6 %collective-permute-start.5 = (bf16[384,512]{1,0:T(8,128)(2,1)S(1)}, bf16[384,512]{1,0:T(8,128)(2,1)S(1)}, u32[]{:S(2)}, u32[]{:S(2)}) collective-permute-start(bf16[384,512]{1,0:T(8,128)(2,1)S(1)} %collective-permute-done.2.refs_2_), channel_id=1, source_target_pairs={{4,0},{8,4},{12,8},{14,12},{10,14},{6,10},{2,6},{0,2},{5,1},{9,5},... | collective-permute-start | bytes 1179656 | tf_op jit(solution)/shard_map/ppermute | solution.py:318
  15.8 9.1 %collective-permute-start.3 = (s32[2048]{0:T(1024)S(1)}, s32[2048]{0:T(1024)S(1)}, u32[]{:S(2)}, u32[]{:S(2)}) collective-permute-start(s32[2048]{0:T(1024)S(1)} %add_select_fusion.2), channel_id=1, source_target_pairs={{0,4},{2,6},{4,0},{6,2},{8,12},{10,14},{12,8},{14,10},{1,5},{3,7},... | collective-permute-start | bytes 24584 | tf_op jit(solution)/shard_map/ppermute | solution.py:331
  25.0 10.0 %collective-permute-start.8 = (bf16[384,512]{1,0:T(8,128)(2,1)S(1)}, bf16[384,512]{1,0:T(8,128)(2,1)S(1)}, u32[]{:S(2)}, u32[]{:S(2)}) collective-permute-start(bf16[384,512]{1,0:T(8,128)(2,1)S(1)} %collective-permute-done.5.refs_4_), channel_id=1, source_target_pairs={{4,0},{8,4},{12,8},{14,12},{10,14},{6,10},{2,6},{0,2},{5,1},{9,5},... | collective-permute-start | bytes 1179656 | tf_op jit(solution)/shard_map/ppermute | solution.py:318
  25.2 10.9 %collective-permute-start.7 = (bf16[384,512]{1,0:T(8,128)(2,1)S(1)}, bf16[384,512]{1,0:T(8,128)(2,1)S(1)}, u32[]{:S(2)}, u32[]{:S(2)}) collective-permute-start(bf16[384,512]{1,0:T(8,128)(2,1)S(1)} %collective-permute-done.4.refs_3_), channel_id=1, source_target_pairs={{0,4},{4,8},{8,12},{12,14},{14,10},{10,6},{6,2},{2,0},{1,5},{5,9},... | collective-permute-start | bytes 1179656 | tf_op jit(solution)/shard_map/ppermute | solution.py:318
  27.0 7.9 %collective-permute-start.6 = (s32[4096]{0:T(1024)S(1)}, s32[4096]{0:T(1024)S(1)}, u32[]{:S(2)}, u32[]{:S(2)}) collective-permute-start(s32[4096]{0:T(1024)S(1)} %add_select_fusion.1), channel_id=1, source_target_pairs={{0,8},{2,10},{4,12},{6,14},{8,0},{10,2},{12,4},{14,6},{1,9},{3,11}... | collective-permute-start | bytes 49160 | tf_op jit(solution)/shard_map/ppermute | solution.py:331
  29.7 12.2 %copy-start.1 = (bf16[3,128,512]{2,1,0:T(8,128)(2,1)S(1)}, bf16[3,128,512]{2,1,0:T(8,128)(2,1)}, u32[]{:S(2)}) copy-start(bf16[3,128,512]{2,1,0:T(8,128)(2,1)} %param.5) | copy-start | bytes 1179652
  34.9 6.3 %collective-permute-start.10 = (bf16[192,512]{1,0:T(8,128)(2,1)S(1)}, bf16[192,512]{1,0:T(8,128)(2,1)S(1)}, u32[]{:S(2)}, u32[]{:S(2)}) collective-permute-start(bf16[192,512]{1,0:T(8,128)(2,1)S(1)} %slice.17), channel_id=1, source_target_pairs={{4,0},{8,4},{12,8},{14,12},{10,14},{6,10},{2,6},{0,2},{5,1},{9,5},... | collective-permute-start | bytes 589832 | tf_op jit(solution)/shard_map/ppermute | solution.py:318
  36.1 5.7 %collective-permute-start.9 = (bf16[192,512]{1,0:T(8,128)(2,1)S(1)}, bf16[192,512]{1,0:T(8,128)(2,1)S(1)}, u32[]{:S(2)}, u32[]{:S(2)}) collective-permute-start(bf16[192,512]{1,0:T(8,128)(2,1)S(1)} %slice.16), channel_id=1, source_target_pairs={{0,4},{4,8},{8,12},{12,14},{14,10},{10,6},{6,2},{2,0},{1,5},{5,9},... | collective-permute-start | bytes 589832 | tf_op jit(solution)/shard_map/ppermute | solution.py:318
  41.9 2.3 %copy-start = (f32[8960,128]{1,0:T(8,128)S(1)}, f32[8960,128]{1,0:T(8,128)}, u32[]{:S(2)}) copy-start(f32[8960,128]{1,0:T(8,128)} %build_table.5.table_ref) | copy-start | bytes 13762564
  80.4 5.3 %collective-permute-start.11 = (f32[3,4096]{1,0:T(4,128)S(1)}, f32[3,4096]{1,0:T(4,128)S(1)}, u32[]{:S(2)}, u32[]{:S(2)}) collective-permute-start(f32[3,4096]{1,0:T(4,128)S(1)} %get-tuple-element.31), channel_id=1, source_target_pairs={{0,8},{2,10},{4,12},{6,14},{8,0},{10,2},{12,4},{14,6},{1,9},{3,11}... | collective-permute-start | bytes 147464 | tf_op jit(solution)/shard_map/ppermute | solution.py:288
  83.4 5.5 %collective-permute-start.14 = (f32[3,4096]{1,0:T(4,128)S(1)}, f32[3,4096]{1,0:T(4,128)S(1)}, u32[]{:S(2)}, u32[]{:S(2)}) collective-permute-start(f32[3,4096]{1,0:T(4,128)S(1)} %get-tuple-element.32), channel_id=1, source_target_pairs={{0,8},{2,10},{4,12},{6,14},{8,0},{10,2},{12,4},{14,6},{1,9},{3,11}... | collective-permute-start | bytes 147464 | tf_op jit(solution)/shard_map/ppermute | solution.py:288
  88.9 4.3 %collective-permute-start.12 = (f32[3,4096]{1,0:T(4,128)S(1)}, f32[3,4096]{1,0:T(4,128)S(1)}, u32[]{:S(2)}, u32[]{:S(2)}) collective-permute-start(f32[3,4096]{1,0:T(4,128)S(1)} %get-tuple-element.29), channel_id=1, source_target_pairs={{0,4},{2,6},{4,0},{6,2},{8,12},{10,14},{12,8},{14,10},{1,5},{3,7},... | collective-permute-start | bytes 147464 | tf_op jit(solution)/shard_map/ppermute | solution.py:288
  89.0 5.0 %collective-permute-start.15 = (f32[3,4096]{1,0:T(4,128)S(1)}, f32[3,4096]{1,0:T(4,128)S(1)}, u32[]{:S(2)}, u32[]{:S(2)}) collective-permute-start(f32[3,4096]{1,0:T(4,128)S(1)} %get-tuple-element.30), channel_id=1, source_target_pairs={{0,4},{2,6},{4,0},{6,2},{8,12},{10,14},{12,8},{14,10},{1,5},{3,7},... | collective-permute-start | bytes 147464 | tf_op jit(solution)/shard_map/ppermute | solution.py:288
  93.3 4.3 %collective-permute-start.13 = (f32[3,4096]{1,0:T(4,128)S(1)}, f32[3,4096]{1,0:T(4,128)S(1)}, u32[]{:S(2)}, u32[]{:S(2)}) collective-permute-start(f32[3,4096]{1,0:T(4,128)S(1)} %add.109), channel_id=1, source_target_pairs={{0,2},{2,0},{4,6},{6,4},{8,10},{10,8},{12,14},{14,12},{1,3},{3,1},... | collective-permute-start | bytes 147464 | tf_op jit(solution)/shard_map/ppermute | solution.py:288
  94.0 4.3 %collective-permute-start.16 = (f32[3,4096]{1,0:T(4,128)S(1)}, f32[3,4096]{1,0:T(4,128)S(1)}, u32[]{:S(2)}, u32[]{:S(2)}) collective-permute-start(f32[3,4096]{1,0:T(4,128)S(1)} %add.112), channel_id=1, source_target_pairs={{0,2},{2,0},{4,6},{6,4},{8,10},{10,8},{12,14},{14,12},{1,3},{3,1},... | collective-permute-start | bytes 147464 | tf_op jit(solution)/shard_map/ppermute | solution.py:288

commit v6 on v5

v6 whole, which is shorter than its diff:
```python
import functools
import math

import jax
import jax.numpy as jnp
from jax import lax
from jax.experimental import pallas as pl
from jax.experimental.pallas import tpu as pltpu
from jax.sharding import PartitionSpec as P

I32, F32, BF16 = jnp.int32, jnp.float32, jnp.bfloat16
LANES = 128
HALF = 16
SPARE = 8
SIGN_ROWS = 2
CHUNK = 512
MIB = 2**20
LAST_DIMS = (((1,), (1,)), ((), ()))


def signed(word):
    return word - 2**32 if word >= 2**31 else word


def parity(bits, count):
    shift = 1
    while shift < count:
        shift *= 2
    while shift > 1:
        shift //= 2
        bits = bits ^ (bits >> shift)
    return bits & 1


def table_kernel(flips_ref, hidden_ref, *refs, examples):
    table_ref = refs[-1]
    tile = flips_ref.shape[0]
    group = examples + SIGN_ROWS
    words = [None, None]
    for column in range(flips_ref.shape[1] // LANES):
        bit, part = column // 2, column % 2
        flips = flips_ref[:, column * LANES:(column + 1) * LANES]
        term = (flips >> 1) & 1 if bit == 0 else flips & jnp.int32(1 << bit)
        words[part] = term if words[part] is None else words[part] | term
    for part in range(2):
        table_ref[pl.ds(examples + part, tile, stride=group), :] = words[part].astype(F32)
    tokens = hidden_ref.shape[0] // examples
    for example in range(examples):
        block = hidden_ref[example * tokens:(example + 1) * tokens, :].astype(F32).T
        table_ref[pl.ds(example, tile, stride=group), :] = block[:tile]


def build_table(sign_flips, hidden, table, examples, tile, span):
    rows, width = sign_flips.shape
    first, count = span
    group = examples + SIGN_ROWS
    lanes = -(-tile // LANES) * LANES
    in_specs = [
        pl.BlockSpec((tile, width), lambda i: (i + first, 0)),
        pl.BlockSpec((hidden.shape[0], lanes), lambda i: (0, i + first)),
    ]
    args = [sign_flips, hidden]
    aliases = {}
    if table is not None:
        in_specs.append(pl.BlockSpec(memory_space=pl.ANY))
        args.append(table)
        aliases = {2: 0}
    return pl.pallas_call(
        functools.partial(table_kernel, examples=examples),
        grid=(count,),
        in_specs=in_specs,
        out_specs=pl.BlockSpec((tile * group, LANES), lambda i: (i + first, 0)),
        out_shape=jax.ShapeDtypeStruct((rows * group + SPARE, LANES), F32),
        input_output_aliases=aliases,
        compiler_params=pltpu.CompilerParams(vmem_limit_bytes=60 * MIB),
        cost_estimate=pl.CostEstimate(
            flops=2 * tile * count * width, bytes_accessed=4 * tile * count * width, transcendentals=0
        ),
        name="build_table",
    )(*args)


def hadamard_words(column):
    length = column.shape[1]
    lane = lax.broadcasted_iota(I32, (LANES, length), 0)
    words = -parity(lane & column, 7)

    def where_bit(bit, pattern):
        return -((column >> bit) & 1) & jnp.int32(signed(pattern))

    upper = where_bit(7, 0xFFFF0000)
    for bit, pattern in ((8, 0xAAAA), (9, 0xCCCC), (10, 0xF0F0), (11, 0xFF00)):
        upper = upper ^ where_bit(bit, pattern * 0x10001)
    return words ^ upper


def sign_columns(words, bits):
    pieces = []
    parts = [words.astype(jnp.int16), (words >> HALF).astype(jnp.int16)]
    for bit in bits:
        mask = jnp.int16((1 << bit) - (1 << HALF) * (bit == HALF - 1))
        for part in parts:
            pieces.append(jnp.where((part & mask) != 0, jnp.array(-1, BF16), jnp.array(1, BF16)))
    return jnp.concatenate(pieces, axis=1)


def join(scalars, cotangents, joined):
    depth = cotangents[0].shape[1]
    for at, cotangent in enumerate(cotangents):
        joined[:, pl.ds(pl.multiple_of(scalars[1 + at] * depth, depth), depth)] = cotangent[...]


def project(joined, words):
    columns = sign_columns(words, range(joined.shape[1] // (2 * LANES)))
    return lax.dot_general(joined[...], columns, LAST_DIMS, preferred_element_type=F32)


def weigh(total, picked, scalars, position, examples, per_shard, parties, scale):
    shard = position // per_shard
    sign = scale * (1 - 2 * parity(shard & scalars[0], parties.bit_length())).astype(F32)
    weighted = (total * picked.astype(F32)).reshape(examples, -1, total.shape[1])
    return jnp.sum(weighted, axis=1) * sign


def sample_kernel(
    scalars, rows_ref, offsets_ref, table_ref, *refs, blocks, examples, length, low_mask, per_shard, parties, scale
):
    cotangents, (out_ref, held, made, joined) = refs[:blocks], refs[blocks:]
    step, steps = pl.program_id(0), pl.num_programs(0)
    group = examples + SIGN_ROWS

    def copy_row(chunk, at, slot):
        row = rows_ref[chunk * length + at]
        held[slot, pl.ds(at * group, group), :] = table_ref[pl.ds(row, group), :]

    def copy_chunk(chunk):
        unroll = 32
        slot = lax.rem(chunk, 3)

        def copy_group(block, _):
            for at in range(unroll):
                copy_row(chunk, block * unroll + at, slot)
            return 0

        lax.fori_loop(0, length // unroll, copy_group, 0)

    def make_words(chunk):
        slot = lax.rem(chunk, 3)
        low, high = [held[slot, pl.ds(examples + part, length, stride=group), :].astype(I32) for part in range(2)]
        start = jnp.minimum(chunk, steps - 1) * length
        column = offsets_ref[:, pl.ds(pl.multiple_of(start, LANES), length)] & low_mask
        made[lax.rem(chunk, 2)] = (low | (high << HALF)) ^ hadamard_words(column).T

    @pl.when(step == 0)
    def _():
        join(scalars, cotangents, joined)
        copy_chunk(0)
        copy_chunk(jnp.minimum(1, steps - 1))
        make_words(0)

    words = made[lax.rem(step, 2)]
    third = jnp.minimum(step + 2, steps - 1)
    target = lax.rem(step + 2, 3)
    totals = []
    for start in range(0, length, length // 2):
        for at in range(start, start + length // 2):
            copy_row(third, at, target)
        totals.append(project(joined, words[start:start + length // 2]))
    total = jnp.concatenate(totals, axis=1)
    picked = [
        held[lax.rem(step, 3), pl.ds(example, length, stride=group), :].astype(BF16).T for example in range(examples)
    ]
    position = step * length + lax.broadcasted_iota(I32, (1, length), 1)
    out_ref[...] = weigh(
        total, jnp.concatenate(picked, axis=0), scalars, position, examples, per_shard, parties, scale
    )
    make_words(step + 1)


def sample(scalars, rows, offsets, table, cotangents, examples, width, per_shard, parties, scale):
    count = offsets.shape[1]
    tokens, depth = cotangents[0].shape
    length = CHUNK
    fixed = lambda i, *_: (0, 0)
    return pl.pallas_call(
        functools.partial(
            sample_kernel, blocks=len(cotangents), examples=examples, length=length, low_mask=width - 1,
            per_shard=per_shard, parties=parties, scale=scale,
        ),
        grid_spec=pltpu.PrefetchScalarGridSpec(
            num_scalar_prefetch=2,
            grid=(count // length,),
            in_specs=[pl.BlockSpec(offsets.shape, fixed), pl.BlockSpec(table.shape, fixed)]
            + [pl.BlockSpec(piece.shape, fixed) for piece in cotangents],
            out_specs=pl.BlockSpec((examples, length), lambda i, *_: (0, i)),
            scratch_shapes=[
                pltpu.VMEM((3, length * (examples + SIGN_ROWS) + SPARE, LANES), F32),
                pltpu.VMEM((2, length, LANES), I32),
                pltpu.VMEM((tokens, depth * len(cotangents)), BF16),
            ],
        ),
        out_shape=jax.ShapeDtypeStruct((examples, count), F32),
        compiler_params=pltpu.CompilerParams(vmem_limit_bytes=44 * MIB),
        cost_estimate=pl.CostEstimate(
            flops=2 * tokens * depth * len(cotangents) * count, bytes_accessed=6 * tokens * count, transcendentals=0
        ),
        name="sample_rows",
    )(scalars, rows, offsets, table, *cotangents)


def by_xor(parties, step):
    return [(source, source ^ step) for source in range(parties)]


def sum_shards(values, parties):
    step = parties // 2
    while step > 0:
        values = values + lax.ppermute(values, "param", by_xor(parties, step))
        step //= 2
    return values


def local(hidden, cotangent, sign_flips, offsets):
    examples, tokens, rows = hidden.shape
    width = sign_flips.shape[1]
    parties = lax.axis_size("param")
    own = lax.axis_index("param").astype(I32)
    per_shard = offsets.shape[0]
    count = per_shard * parties
    scale = 1.0 / math.sqrt(parties * width)
    flat = examples * tokens
    depth = cotangent.shape[2]
    held = cotangent.reshape(flat, depth)

    ringed = depth % (2 * LANES) == 0 and parties % 2 == 0
    pieces, numbers = [held], [own]
    if ringed:
        order = list(range(0, parties, 2)) + list(range(parties - 1, 0, -2))
        forward = [(order[at], order[(at + 1) % parties]) for at in range(parties)]
        backward = [(target, source) for source, target in forward]
        place = jnp.where(own % 2 == 0, own // 2, parties - 1 - own // 2)

        def shard_at(spot):
            spot = (spot + parties) % parties
            return jnp.where(spot < parties // 2, 2 * spot, 2 * (parties - spot) - 1)

        def pass_on(ahead, behind):
            return lax.ppermute(ahead, "param", forward), lax.ppermute(behind, "param", backward)

        ahead, behind = pass_on(held, held)
        arrived = []

    units = hidden.reshape(flat, rows)
    if rows % LANES:
        units = jnp.pad(units, ((0, 0), (0, -rows % LANES)))
    tile = 2 * LANES if rows % (2 * LANES) == 0 else LANES if rows % LANES == 0 else rows
    tiles = rows // tile
    table, built, step = None, 0, 1
    steps = parties.bit_length() - 1
    for at in range(steps):
        other = lax.ppermute(offsets, "param", by_xor(parties, step))
        until = -(-tiles * (at + 1) // steps)
        if until > built:
            table = build_table(sign_flips, units, table, examples, tile, (built, until - built))
            built = until
            table, other = lax.optimization_barrier((table, other))
        if ringed and at + 1 < min(steps, parties // 2):
            table, ahead, behind = lax.optimization_barrier((table, ahead, behind))
            arrived += [ahead, behind]
            ahead, behind = pass_on(ahead, behind)
        offsets = jnp.where(
            (own & step) == 0, jnp.concatenate([offsets, other]), jnp.concatenate([other, offsets])
        )
        step *= 2

    row_shift = width.bit_length() - 1
    unit_rows = (offsets >> row_shift) * (examples + SIGN_ROWS)
    line = offsets.reshape(1, count)
    if ringed:
        for step in range(1, parties // 2):
            if len(arrived) < 2 * step:
                arrived += [ahead, behind]
                if step + 1 < parties // 2:
                    ahead, behind = pass_on(ahead, behind)
                else:
                    middle = flat // 2
                    ahead, behind = pass_on(ahead[:middle], behind[middle:])
            pieces += arrived[2 * step - 2:2 * step]
            numbers += [shard_at(place - step), shard_at(place + step)]
        pieces.append(jnp.concatenate([ahead, behind], axis=0))
        numbers.append(shard_at(place + parties // 2))
    else:
        gathered = lax.all_gather(cotangent, "param", axis=2, tiled=True).reshape(flat, width)
        span = 4 * LANES
        pieces = [gathered[:, at:at + span] for at in range(0, width, span)]
        numbers = [jnp.int32(at) for at in range(len(pieces))]
    values = sample(
        jnp.stack([own] + numbers), unit_rows, line, table, pieces, examples, width, per_shard, parties, scale
    )
    half = count // 2
    return jnp.concatenate([sum_shards(part, parties) for part in (values[:, :half], values[:, half:])], axis=1)


def solution(mesh):
    return jax.shard_map(
        local,
        mesh=mesh,
        in_specs=(
            P(("groups", "dp"), None, "param"),
            P(("groups", "dp"), None, "param"),
            P("param", None),
            P("param"),
        ),
        out_specs=P(("groups", "dp"), None),
        check_vma=False,
    )
```

time: 99.2 us -> 99.1 us (level)
  no operation moved by 1% of the time
where the time goes in v6:
time: 99.1 us; the launch traced here: 99 us
  Pallas kernels  53.1 us (54%)
  starting transfers between devices  22.6 us (23%)
  waiting for transfers between devices  19.8 us (20%)
  local copies, waits for them, and re-layouts  2.44 us (2%)
    pallas_call x1, Pallas kernels, sample(): pl.pallas_call(functools.partial(sample_kernel, blocks=len(cotangents), e...  36.1 us
    pallas_call x3, Pallas kernels, build_table(): pl.pallas_call(functools.partial(table_kernel, examples=examples), grid=(...  17 us
    ppermute x6, waiting for transfers between devices, sum_shards(): values = values + lax.ppermute(values, 'param', by_xor(parties, step))  11.1 us
    ppermute x4, starting transfers between devices, pass_on(): lax.ppermute(ahead, 'param', forward)  7.89 us
    ppermute x6, starting transfers between devices, sum_shards(): values = values + lax.ppermute(values, 'param', by_xor(parties, step))  6.71 us
    ppermute x3, starting transfers between devices, local(): other = lax.ppermute(offsets, 'param', by_xor(parties, step))  6.11 us
    ppermute x4, waiting for transfers between devices, pass_on(): lax.ppermute(behind, 'param', backward)  4.97 us
    ppermute x3, waiting for transfers between devices, local(): other = lax.ppermute(offsets, 'param', by_xor(parties, step))  3.12 us
  transfers between devices with their start and end apart: 17, of which 12 were waited for; matrix products, arithmetic and copies ran while one was open for 0% of the time, Pallas kernels for 17%

profile of v6, /device:TPU:0, one launch (start us, length us, event | category | flops | bytes accessed | tf_op | source)
XLA Modules:
  0.0 99.0 jit_solution(9374584188861395422)
XLA Ops:
  0.0 3.0 %collective-permute-start.1 = (bf16[384,512]{1,0:T(8,128)(2,1)}, bf16[384,512]{1,0:T(8,128)(2,1)S(1)}, u32[]{:S(2)}, u32[]{:S(2)}) collective-permute-start(bf16[384,512]{1,0:T(8,128)(2,1)} %bitcast.12), channel_id=1, source_target_pairs={{0,4},{4,8},{8,12},{12,14},{14,10},{10,6},{6,2},{2,0},{1,5},{5,9},... | collective-permute-start | bytes 1179656 | tf_op jit(solution)/shard_map/ppermute | solution.py:248
  3.0 1.9 %collective-permute-start = (s32[1024]{0:T(1024)}, s32[1024]{0:T(1024)S(1)}, u32[]{:S(2)}, u32[]{:S(2)}) collective-permute-start(s32[1024]{0:T(1024)} %param.7), channel_id=1, source_target_pairs={{0,2},{2,0},{4,6},{6,4},{8,10},{10,8},{12,14},{14,12},{1,3},{3,1},... | collective-permute-start | bytes 12296 | tf_op jit(solution)/shard_map/ppermute | solution.py:261
  5.0 7.1 %build_table.3.refs_0_ = f32[8968,128]{1,0:T(8,128)} custom-call(s32[1792,4096]{1,0:T(8,128)} %flips_ref.5, bf16[384,1792]{1,0:T(8,128)(2,1)} %bitcast.15), custom_call_target="tpu_custom_call" | custom-call | flops 6291456 | bytes 12582912 | tf_op jit(solution)/shard_map/build_table/pallas_call | solution.py:68
  12.4 1.5 %collective-permute-done.2.refs_2_ = bf16[384,512]{1,0:T(8,128)(2,1)S(1)} collective-permute-done((bf16[384,512]{1,0:T(8,128)(2,1)}, bf16[384,512]{1,0:T(8,128)(2,1)S(1)}, u32[]{:S(2)}, u32[]{:S(2)}) %collective-permute-start.2) | collective-permute-done | bytes 393248 | tf_op jit(solution)/shard_map/ppermute | solution.py:248
  13.8 1.6 %collective-permute-start.4 = (bf16[384,512]{1,0:T(8,128)(2,1)S(1)}, bf16[384,512]{1,0:T(8,128)(2,1)S(1)}, u32[]{:S(2)}, u32[]{:S(2)}) collective-permute-start(bf16[384,512]{1,0:T(8,128)(2,1)S(1)} %collective-permute-done.1.refs_1_), channel_id=1, source_target_pairs={{0,4},{4,8},{8,12},{12,14},{14,10},{10,6},{6,2},{2,0},{1,5},{5,9},... | collective-permute-start | bytes 1179656 | tf_op jit(solution)/shard_map/ppermute | solution.py:248
  15.8 1.6 %collective-permute-start.3 = (s32[2048]{0:T(1024)S(1)}, s32[2048]{0:T(1024)S(1)}, u32[]{:S(2)}, u32[]{:S(2)}) collective-permute-start(s32[2048]{0:T(1024)S(1)} %add_select_fusion.2), channel_id=1, source_target_pairs={{0,4},{2,6},{4,0},{6,2},{8,12},{10,14},{12,8},{14,10},{1,5},{3,7},... | collective-permute-start | bytes 24584 | tf_op jit(solution)/shard_map/ppermute | solution.py:261
  17.4 5.0 %build_table.4.refs_0_ = f32[8968,128]{1,0:T(8,128)} custom-call(s32[1792,4096]{1,0:T(8,128)} %flips_ref.5, bf16[384,1792]{1,0:T(8,128)(2,1)} %bitcast.16, f32[8968,128]{1,0:T(8,128)} %build_table.3.refs_0_), custom_call_target="tpu_custom_call", output_to_operand_aliasing={{}: (2, {})} | custom-call | flops 4194304 | bytes 8388608 | tf_op jit(solution)/shard_map/build_table/pallas_call | solution.py:68
  22.4 2.6 %collective-permute-done.3 = s32[2048]{0:T(1024)S(1)} collective-permute-done((s32[2048]{0:T(1024)S(1)}, s32[2048]{0:T(1024)S(1)}, u32[]{:S(2)}, u32[]{:S(2)}) %collective-permute-start.3) | collective-permute-done | bytes 8224 | tf_op jit(solution)/shard_map/ppermute | solution.py:261
  25.2 1.8 %collective-permute-start.7 = (bf16[384,512]{1,0:T(8,128)(2,1)S(1)}, bf16[384,512]{1,0:T(8,128)(2,1)S(1)}, u32[]{:S(2)}, u32[]{:S(2)}) collective-permute-start(bf16[384,512]{1,0:T(8,128)(2,1)S(1)} %collective-permute-done.4.refs_3_), channel_id=1, source_target_pairs={{0,4},{4,8},{8,12},{12,14},{14,10},{10,6},{6,2},{2,0},{1,5},{5,9},... | collective-permute-start | bytes 1179656 | tf_op jit(solution)/shard_map/ppermute | solution.py:248
  27.0 2.6 %collective-permute-start.6 = (s32[4096]{0:T(1024)S(1)}, s32[4096]{0:T(1024)S(1)}, u32[]{:S(2)}, u32[]{:S(2)}) collective-permute-start(s32[4096]{0:T(1024)S(1)} %add_select_fusion.1), channel_id=1, source_target_pairs={{0,8},{2,10},{4,12},{6,14},{8,0},{10,2},{12,4},{14,6},{1,9},{3,11}... | collective-permute-start | bytes 49160 | tf_op jit(solution)/shard_map/ppermute | solution.py:261
  29.7 5.0 %build_table.5.table_ref = f32[8968,128]{1,0:T(8,128)} custom-call(s32[1792,4096]{1,0:T(8,128)} %flips_ref.5, bf16[384,1792]{1,0:T(8,128)(2,1)} %bitcast.17, f32[8968,128]{1,0:T(8,128)} %build_table.4.refs_0_), custom_call_target="tpu_custom_call", output_to_operand_aliasing={{}: (2, {})} | custom-call | flops 4194304 | bytes 8388608 | tf_op jit(solution)/shard_map/build_table/pallas_call | solution.py:68
  34.9 1.2 %collective-permute-start.10 = (bf16[192,512]{1,0:T(8,128)(2,1)S(1)}, bf16[192,512]{1,0:T(8,128)(2,1)S(1)}, u32[]{:S(2)}, u32[]{:S(2)}) collective-permute-start(bf16[192,512]{1,0:T(8,128)(2,1)S(1)} %slice.17), channel_id=1, source_target_pairs={{4,0},{8,4},{12,8},{14,12},{10,14},{6,10},{2,6},{0,2},{5,1},{9,5},... | collective-permute-start | bytes 589832 | tf_op jit(solution)/shard_map/ppermute | solution.py:248
  36.1 1.5 %collective-permute-start.9 = (bf16[192,512]{1,0:T(8,128)(2,1)S(1)}, bf16[192,512]{1,0:T(8,128)(2,1)S(1)}, u32[]{:S(2)}, u32[]{:S(2)}) collective-permute-start(bf16[192,512]{1,0:T(8,128)(2,1)S(1)} %slice.16), channel_id=1, source_target_pairs={{0,4},{4,8},{8,12},{12,14},{14,10},{10,6},{6,2},{2,0},{1,5},{5,9},... | collective-permute-start | bytes 589832 | tf_op jit(solution)/shard_map/ppermute | solution.py:248
  37.7 3.5 %collective-permute-done.10 = bf16[192,512]{1,0:T(8,128)(2,1)S(1)} collective-permute-done((bf16[192,512]{1,0:T(8,128)(2,1)S(1)}, bf16[192,512]{1,0:T(8,128)(2,1)S(1)}, u32[]{:S(2)}, u32[]{:S(2)}) %collective-permute-start.10) | collective-permute-done | bytes 196640 | tf_op jit(solution)/shard_map/ppermute | solution.py:248
  41.9 2.3 %copy-done = f32[8968,128]{1,0:T(8,128)S(1)} copy-done((f32[8968,128]{1,0:T(8,128)S(1)}, f32[8968,128]{1,0:T(8,128)}, u32[]{:S(2)}) %copy-start) | copy-done | bytes 4591640
  44.2 36.1 %sample_rows.1 = f32[3,8192]{1,0:T(4,128)S(1)} custom-call(s32[9]{0:T(128)S(1)} %stack.36.scalars, s32[8192]{0:T(1024)S(1)} %fusion.1.rows_ref, s32[1,8192]{1,0:T(1,128)S(1)} %broadcast_select_fusion.offsets_ref, f32[8968,128]{1,0:T(8,128)S(1)} %copy-done, bf16[384,512]{1,0:T(8,128)(2,1)S(1)} %bitcast.14, ...), custom_call_target="tpu_custom_call" | custom-call | flops 25769803776 | bytes 18874368 | tf_op jit(solution)/shard_map/sample_rows/pallas_call | solution.py:185
  80.3 3.0 %collective-permute-start.11 = (f32[3,4096]{1,0:T(4,128)S(1)}, f32[3,4096]{1,0:T(4,128)S(1)}, u32[]{:S(2)}, u32[]{:S(2)}) collective-permute-start(f32[3,4096]{1,0:T(4,128)S(1)} %get-tuple-element.31), channel_id=1, source_target_pairs={{0,8},{2,10},{4,12},{6,14},{8,0},{10,2},{12,4},{14,6},{1,9},{3,11}... | collective-permute-start | bytes 147464 | tf_op jit(solution)/shard_map/ppermute | solution.py:218
  83.4 2.3 %collective-permute-done.11 = f32[3,4096]{1,0:T(4,128)S(1)} collective-permute-done((f32[3,4096]{1,0:T(4,128)S(1)}, f32[3,4096]{1,0:T(4,128)S(1)}, u32[]{:S(2)}, u32[]{:S(2)}) %collective-permute-start.11) | collective-permute-done | bytes 49184 | tf_op jit(solution)/shard_map/ppermute | solution.py:218
  85.7 3.1 %collective-permute-done.14 = f32[3,4096]{1,0:T(4,128)S(1)} collective-permute-done((f32[3,4096]{1,0:T(4,128)S(1)}, f32[3,4096]{1,0:T(4,128)S(1)}, u32[]{:S(2)}, u32[]{:S(2)}) %collective-permute-start.14) | collective-permute-done | bytes 49184 | tf_op jit(solution)/shard_map/ppermute | solution.py:218
  88.9 2.0 %collective-permute-start.15 = (f32[3,4096]{1,0:T(4,128)S(1)}, f32[3,4096]{1,0:T(4,128)S(1)}, u32[]{:S(2)}, u32[]{:S(2)}) collective-permute-start(f32[3,4096]{1,0:T(4,128)S(1)} %get-tuple-element.30), channel_id=1, source_target_pairs={{0,4},{2,6},{4,0},{6,2},{8,12},{10,14},{12,8},{14,10},{1,5},{3,7},... | collective-permute-start | bytes 147464 | tf_op jit(solution)/shard_map/ppermute | solution.py:218
  91.0 2.2 %collective-permute-done.12 = f32[3,4096]{1,0:T(4,128)S(1)} collective-permute-done((f32[3,4096]{1,0:T(4,128)S(1)}, f32[3,4096]{1,0:T(4,128)S(1)}, u32[]{:S(2)}, u32[]{:S(2)}) %collective-permute-start.12) | collective-permute-done | bytes 49184 | tf_op jit(solution)/shard_map/ppermute | solution.py:218
  93.9 1.5 %collective-permute-start.16 = (f32[3,4096]{1,0:T(4,128)S(1)}, f32[3,4096]{1,0:T(4,128)S(1)}, u32[]{:S(2)}, u32[]{:S(2)}) collective-permute-start(f32[3,4096]{1,0:T(4,128)S(1)} %add.112), channel_id=1, source_target_pairs={{0,2},{2,0},{4,6},{6,4},{8,10},{10,8},{12,14},{14,12},{1,3},{3,1},... | collective-permute-start | bytes 147464 | tf_op jit(solution)/shard_map/ppermute | solution.py:218
  95.4 2.1 %collective-permute-done.13 = f32[3,4096]{1,0:T(4,128)S(1)} collective-permute-done((f32[3,4096]{1,0:T(4,128)S(1)}, f32[3,4096]{1,0:T(4,128)S(1)}, u32[]{:S(2)}, u32[]{:S(2)}) %collective-permute-start.13) | collective-permute-done | bytes 49184 | tf_op jit(solution)/shard_map/ppermute | solution.py:218
  98.3 0.7 pad_maximum_fusion.1
  (35 shorter events, 3.8 us)
Async XLA Ops:
  0.0 12.4 %collective-permute-start.1 = (bf16[384,512]{1,0:T(8,128)(2,1)}, bf16[384,512]{1,0:T(8,128)(2,1)S(1)}, u32[]{:S(2)}, u32[]{:S(2)}) collective-permute-start(bf16[384,512]{1,0:T(8,128)(2,1)} %bitcast.12), channel_id=1, source_target_pairs={{0,4},{4,8},{8,12},{12,14},{14,10},{10,6},{6,2},{2,0},{1,5},{5,9},... | collective-permute-start | bytes 1179656 | tf_op jit(solution)/shard_map/ppermute | solution.py:248
  3.0 10.8 %collective-permute-start.2 = (bf16[384,512]{1,0:T(8,128)(2,1)}, bf16[384,512]{1,0:T(8,128)(2,1)S(1)}, u32[]{:S(2)}, u32[]{:S(2)}) collective-permute-start(bf16[384,512]{1,0:T(8,128)(2,1)} %bitcast.13), channel_id=1, source_target_pairs={{4,0},{8,4},{12,8},{14,12},{10,14},{6,10},{2,6},{0,2},{5,1},{9,5},... | collective-permute-start | bytes 1179656 | tf_op jit(solution)/shard_map/ppermute | solution.py:248
  3.0 9.3 %collective-permute-start = (s32[1024]{0:T(1024)}, s32[1024]{0:T(1024)S(1)}, u32[]{:S(2)}, u32[]{:S(2)}) collective-permute-start(s32[1024]{0:T(1024)} %param.7), channel_id=1, source_target_pairs={{0,2},{2,0},{4,6},{6,4},{8,10},{10,8},{12,14},{14,12},{1,3},{3,1},... | collective-permute-start | bytes 12296 | tf_op jit(solution)/shard_map/ppermute | solution.py:261
  5.0 10.9 %copy-start.2 = (s32[1024]{0:T(1024)S(1)}, s32[1024]{0:T(1024)}, u32[]{:S(2)}) copy-start(s32[1024]{0:T(1024)} %param.7) | copy-start | bytes 12292
  13.8 11.1 %collective-permute-start.4 = (bf16[384,512]{1,0:T(8,128)(2,1)S(1)}, bf16[384,512]{1,0:T(8,128)(2,1)S(1)}, u32[]{:S(2)}, u32[]{:S(2)}) collective-permute-start(bf16[384,512]{1,0:T(8,128)(2,1)S(1)} %collective-permute-done.1.refs_1_), channel_id=1, source_target_pairs={{0,4},{4,8},{8,12},{12,14},{14,10},{10,6},{6,2},{2,0},{1,5},{5,9},... | collective-permute-start | bytes 1179656 | tf_op jit(solution)/shard_map/ppermute | solution.py:248
  15.4 9.6 %collective-permute-start.5 = (bf16[384,512]{1,0:T(8,128)(2,1)S(1)}, bf16[384,512]{1,0:T(8,128)(2,1)S(1)}, u32[]{:S(2)}, u32[]{:S(2)}) collective-permute-start(bf16[384,512]{1,0:T(8,128)(2,1)S(1)} %collective-permute-done.2.refs_2_), channel_id=1, source_target_pairs={{4,0},{8,4},{12,8},{14,12},{10,14},{6,10},{2,6},{0,2},{5,1},{9,5},... | collective-permute-start | bytes 1179656 | tf_op jit(solution)/shard_map/ppermute | solution.py:248
  15.8 9.1 %collective-permute-start.3 = (s32[2048]{0:T(1024)S(1)}, s32[2048]{0:T(1024)S(1)}, u32[]{:S(2)}, u32[]{:S(2)}) collective-permute-start(s32[2048]{0:T(1024)S(1)} %add_select_fusion.2), channel_id=1, source_target_pairs={{0,4},{2,6},{4,0},{6,2},{8,12},{10,14},{12,8},{14,10},{1,5},{3,7},... | collective-permute-start | bytes 24584 | tf_op jit(solution)/shard_map/ppermute | solution.py:261
  25.0 10.0 %collective-permute-start.8 = (bf16[384,512]{1,0:T(8,128)(2,1)S(1)}, bf16[384,512]{1,0:T(8,128)(2,1)S(1)}, u32[]{:S(2)}, u32[]{:S(2)}) collective-permute-start(bf16[384,512]{1,0:T(8,128)(2,1)S(1)} %collective-permute-done.5.refs_4_), channel_id=1, source_target_pairs={{4,0},{8,4},{12,8},{14,12},{10,14},{6,10},{2,6},{0,2},{5,1},{9,5},... | collective-permute-start | bytes 1179656 | tf_op jit(solution)/shard_map/ppermute | solution.py:248
  25.2 10.9 %collective-permute-start.7 = (bf16[384,512]{1,0:T(8,128)(2,1)S(1)}, bf16[384,512]{1,0:T(8,128)(2,1)S(1)}, u32[]{:S(2)}, u32[]{:S(2)}) collective-permute-start(bf16[384,512]{1,0:T(8,128)(2,1)S(1)} %collective-permute-done.4.refs_3_), channel_id=1, source_target_pairs={{0,4},{4,8},{8,12},{12,14},{14,10},{10,6},{6,2},{2,0},{1,5},{5,9},... | collective-permute-start | bytes 1179656 | tf_op jit(solution)/shard_map/ppermute | solution.py:248
  27.0 7.9 %collective-permute-start.6 = (s32[4096]{0:T(1024)S(1)}, s32[4096]{0:T(1024)S(1)}, u32[]{:S(2)}, u32[]{:S(2)}) collective-permute-start(s32[4096]{0:T(1024)S(1)} %add_select_fusion.1), channel_id=1, source_target_pairs={{0,8},{2,10},{4,12},{6,14},{8,0},{10,2},{12,4},{14,6},{1,9},{3,11}... | collective-permute-start | bytes 49160 | tf_op jit(solution)/shard_map/ppermute | solution.py:261
  29.7 12.2 %copy-start.1 = (bf16[3,128,512]{2,1,0:T(8,128)(2,1)S(1)}, bf16[3,128,512]{2,1,0:T(8,128)(2,1)}, u32[]{:S(2)}) copy-start(bf16[3,128,512]{2,1,0:T(8,128)(2,1)} %param.5) | copy-start | bytes 1179652
  34.9 6.3 %collective-permute-start.10 = (bf16[192,512]{1,0:T(8,128)(2,1)S(1)}, bf16[192,512]{1,0:T(8,128)(2,1)S(1)}, u32[]{:S(2)}, u32[]{:S(2)}) collective-permute-start(bf16[192,512]{1,0:T(8,128)(2,1)S(1)} %slice.17), channel_id=1, source_target_pairs={{4,0},{8,4},{12,8},{14,12},{10,14},{6,10},{2,6},{0,2},{5,1},{9,5},... | collective-permute-start | bytes 589832 | tf_op jit(solution)/shard_map/ppermute | solution.py:248
  36.1 5.7 %collective-permute-start.9 = (bf16[192,512]{1,0:T(8,128)(2,1)S(1)}, bf16[192,512]{1,0:T(8,128)(2,1)S(1)}, u32[]{:S(2)}, u32[]{:S(2)}) collective-permute-start(bf16[192,512]{1,0:T(8,128)(2,1)S(1)} %slice.16), channel_id=1, source_target_pairs={{0,4},{4,8},{8,12},{12,14},{14,10},{10,6},{6,2},{2,0},{1,5},{5,9},... | collective-permute-start | bytes 589832 | tf_op jit(solution)/shard_map/ppermute | solution.py:248
  41.9 2.3 %copy-start = (f32[8968,128]{1,0:T(8,128)S(1)}, f32[8968,128]{1,0:T(8,128)}, u32[]{:S(2)}) copy-start(f32[8968,128]{1,0:T(8,128)} %build_table.5.table_ref) | copy-start | bytes 13774852
  80.3 5.4 %collective-permute-start.11 = (f32[3,4096]{1,0:T(4,128)S(1)}, f32[3,4096]{1,0:T(4,128)S(1)}, u32[]{:S(2)}, u32[]{:S(2)}) collective-permute-start(f32[3,4096]{1,0:T(4,128)S(1)} %get-tuple-element.31), channel_id=1, source_target_pairs={{0,8},{2,10},{4,12},{6,14},{8,0},{10,2},{12,4},{14,6},{1,9},{3,11}... | collective-permute-start | bytes 147464 | tf_op jit(solution)/shard_map/ppermute | solution.py:218
  83.3 5.5 %collective-permute-start.14 = (f32[3,4096]{1,0:T(4,128)S(1)}, f32[3,4096]{1,0:T(4,128)S(1)}, u32[]{:S(2)}, u32[]{:S(2)}) collective-permute-start(f32[3,4096]{1,0:T(4,128)S(1)} %get-tuple-element.32), channel_id=1, source_target_pairs={{0,8},{2,10},{4,12},{6,14},{8,0},{10,2},{12,4},{14,6},{1,9},{3,11}... | collective-permute-start | bytes 147464 | tf_op jit(solution)/shard_map/ppermute | solution.py:218
  88.9 4.3 %collective-permute-start.12 = (f32[3,4096]{1,0:T(4,128)S(1)}, f32[3,4096]{1,0:T(4,128)S(1)}, u32[]{:S(2)}, u32[]{:S(2)}) collective-permute-start(f32[3,4096]{1,0:T(4,128)S(1)} %get-tuple-element.29), channel_id=1, source_target_pairs={{0,4},{2,6},{4,0},{6,2},{8,12},{10,14},{12,8},{14,10},{1,5},{3,7},... | collective-permute-start | bytes 147464 | tf_op jit(solution)/shard_map/ppermute | solution.py:218
  88.9 5.0 %collective-permute-start.15 = (f32[3,4096]{1,0:T(4,128)S(1)}, f32[3,4096]{1,0:T(4,128)S(1)}, u32[]{:S(2)}, u32[]{:S(2)}) collective-permute-start(f32[3,4096]{1,0:T(4,128)S(1)} %get-tuple-element.30), channel_id=1, source_target_pairs={{0,4},{2,6},{4,0},{6,2},{8,12},{10,14},{12,8},{14,10},{1,5},{3,7},... | collective-permute-start | bytes 147464 | tf_op jit(solution)/shard_map/ppermute | solution.py:218
  93.2 4.3 %collective-permute-start.13 = (f32[3,4096]{1,0:T(4,128)S(1)}, f32[3,4096]{1,0:T(4,128)S(1)}, u32[]{:S(2)}, u32[]{:S(2)}) collective-permute-start(f32[3,4096]{1,0:T(4,128)S(1)} %add.109), channel_id=1, source_target_pairs={{0,2},{2,0},{4,6},{6,4},{8,10},{10,8},{12,14},{14,12},{1,3},{3,1},... | collective-permute-start | bytes 147464 | tf_op jit(solution)/shard_map/ppermute | solution.py:218
  93.9 4.3 %collective-permute-start.16 = (f32[3,4096]{1,0:T(4,128)S(1)}, f32[3,4096]{1,0:T(4,128)S(1)}, u32[]{:S(2)}, u32[]{:S(2)}) collective-permute-start(f32[3,4096]{1,0:T(4,128)S(1)} %add.112), channel_id=1, source_target_pairs={{0,2},{2,0},{4,6},{6,4},{8,10},{10,8},{12,14},{14,12},{1,3},{3,1},... | collective-permute-start | bytes 147464 | tf_op jit(solution)/shard_map/ppermute | solution.py:218

commit v7 on v6

--- a/solution.py
+++ b/solution.py
@@ -13,7 +13,7 @@
 HALF = 16
 SPARE = 8
 SIGN_ROWS = 2
-CHUNK = 512
+CHUNK = 256
 MIB = 2**20
 LAST_DIMS = (((1,), (1,)), ((), ()))
 
@@ -161,12 +161,9 @@
     words = made[lax.rem(step, 2)]
     third = jnp.minimum(step + 2, steps - 1)
     target = lax.rem(step + 2, 3)
-    totals = []
-    for start in range(0, length, length // 2):
-        for at in range(start, start + length // 2):
-            copy_row(third, at, target)
-        totals.append(project(joined, words[start:start + length // 2]))
-    total = jnp.concatenate(totals, axis=1)
+    for at in range(length):
+        copy_row(third, at, target)
+    total = project(joined, words)
     picked = [
         held[lax.rem(step, 3), pl.ds(example, length, stride=group), :].astype(BF16).T for example in range(examples)
     ]

time: 99.1 us -> 98.8 us (level)
  no operation moved by 1% of the time
where the time goes in v7:
time: 98.8 us; the launch traced here: 98.6 us
  Pallas kernels  52.8 us (53%)
  starting transfers between devices  22.6 us (23%)
  waiting for transfers between devices  19.8 us (20%)
  local copies, waits for them, and re-layouts  2.44 us (2%)
    pallas_call x1, Pallas kernels, sample(): pl.pallas_call(functools.partial(sample_kernel, blocks=len(cotangents), e...  35.8 us
    pallas_call x3, Pallas kernels, build_table(): pl.pallas_call(functools.partial(table_kernel, examples=examples), grid=(...  17 us
    ppermute x6, waiting for transfers between devices, sum_shards(): values = values + lax.ppermute(values, 'param', by_xor(parties, step))  11.1 us
    ppermute x4, starting transfers between devices, pass_on(): lax.ppermute(ahead, 'param', forward)  7.89 us
    ppermute x6, starting transfers between devices, sum_shards(): values = values + lax.ppermute(values, 'param', by_xor(parties, step))  6.73 us
    ppermute x3, starting transfers between devices, local(): other = lax.ppermute(offsets, 'param', by_xor(parties, step))  6.11 us
    ppermute x4, waiting for transfers between devices, pass_on(): lax.ppermute(behind, 'param', backward)  4.97 us
    ppermute x3, waiting for transfers between devices, local(): other = lax.ppermute(offsets, 'param', by_xor(parties, step))  3.12 us
  transfers between devices with their start and end apart: 17, of which 12 were waited for; matrix products, arithmetic and copies ran while one was open for 0% of the time, Pallas kernels for 17%

profile of v7, /device:TPU:0, one launch (start us, length us, event | category | flops | bytes accessed | tf_op | source)
XLA Modules:
  0.0 98.6 jit_solution(12236222740302508305)
XLA Ops:
  0.0 3.0 %collective-permute-start.1 = (bf16[384,512]{1,0:T(8,128)(2,1)}, bf16[384,512]{1,0:T(8,128)(2,1)S(1)}, u32[]{:S(2)}, u32[]{:S(2)}) collective-permute-start(bf16[384,512]{1,0:T(8,128)(2,1)} %bitcast.12), channel_id=1, source_target_pairs={{0,4},{4,8},{8,12},{12,14},{14,10},{10,6},{6,2},{2,0},{1,5},{5,9},... | collective-permute-start | bytes 1179656 | tf_op jit(solution)/shard_map/ppermute | solution.py:245
  3.0 1.9 %collective-permute-start = (s32[1024]{0:T(1024)}, s32[1024]{0:T(1024)S(1)}, u32[]{:S(2)}, u32[]{:S(2)}) collective-permute-start(s32[1024]{0:T(1024)} %param.7), channel_id=1, source_target_pairs={{0,2},{2,0},{4,6},{6,4},{8,10},{10,8},{12,14},{14,12},{1,3},{3,1},... | collective-permute-start | bytes 12296 | tf_op jit(solution)/shard_map/ppermute | solution.py:258
  5.0 7.1 %build_table.3.refs_0_ = f32[8968,128]{1,0:T(8,128)} custom-call(s32[1792,4096]{1,0:T(8,128)} %flips_ref.5, bf16[384,1792]{1,0:T(8,128)(2,1)} %bitcast.15), custom_call_target="tpu_custom_call" | custom-call | flops 6291456 | bytes 12582912 | tf_op jit(solution)/shard_map/build_table/pallas_call | solution.py:68
  12.4 1.5 %collective-permute-done.2.refs_2_ = bf16[384,512]{1,0:T(8,128)(2,1)S(1)} collective-permute-done((bf16[384,512]{1,0:T(8,128)(2,1)}, bf16[384,512]{1,0:T(8,128)(2,1)S(1)}, u32[]{:S(2)}, u32[]{:S(2)}) %collective-permute-start.2) | collective-permute-done | bytes 393248 | tf_op jit(solution)/shard_map/ppermute | solution.py:245
  13.8 1.6 %collective-permute-start.4 = (bf16[384,512]{1,0:T(8,128)(2,1)S(1)}, bf16[384,512]{1,0:T(8,128)(2,1)S(1)}, u32[]{:S(2)}, u32[]{:S(2)}) collective-permute-start(bf16[384,512]{1,0:T(8,128)(2,1)S(1)} %collective-permute-done.1.refs_1_), channel_id=1, source_target_pairs={{0,4},{4,8},{8,12},{12,14},{14,10},{10,6},{6,2},{2,0},{1,5},{5,9},... | collective-permute-start | bytes 1179656 | tf_op jit(solution)/shard_map/ppermute | solution.py:245
  15.8 1.6 %collective-permute-start.3 = (s32[2048]{0:T(1024)S(1)}, s32[2048]{0:T(1024)S(1)}, u32[]{:S(2)}, u32[]{:S(2)}) collective-permute-start(s32[2048]{0:T(1024)S(1)} %add_select_fusion.2), channel_id=1, source_target_pairs={{0,4},{2,6},{4,0},{6,2},{8,12},{10,14},{12,8},{14,10},{1,5},{3,7},... | collective-permute-start | bytes 24584 | tf_op jit(solution)/shard_map/ppermute | solution.py:258
  17.4 5.0 %build_table.4.refs_0_ = f32[8968,128]{1,0:T(8,128)} custom-call(s32[1792,4096]{1,0:T(8,128)} %flips_ref.5, bf16[384,1792]{1,0:T(8,128)(2,1)} %bitcast.16, f32[8968,128]{1,0:T(8,128)} %build_table.3.refs_0_), custom_call_target="tpu_custom_call", output_to_operand_aliasing={{}: (2, {})} | custom-call | flops 4194304 | bytes 8388608 | tf_op jit(solution)/shard_map/build_table/pallas_call | solution.py:68
  22.4 2.6 %collective-permute-done.3 = s32[2048]{0:T(1024)S(1)} collective-permute-done((s32[2048]{0:T(1024)S(1)}, s32[2048]{0:T(1024)S(1)}, u32[]{:S(2)}, u32[]{:S(2)}) %collective-permute-start.3) | collective-permute-done | bytes 8224 | tf_op jit(solution)/shard_map/ppermute | solution.py:258
  25.2 1.8 %collective-permute-start.7 = (bf16[384,512]{1,0:T(8,128)(2,1)S(1)}, bf16[384,512]{1,0:T(8,128)(2,1)S(1)}, u32[]{:S(2)}, u32[]{:S(2)}) collective-permute-start(bf16[384,512]{1,0:T(8,128)(2,1)S(1)} %collective-permute-done.4.refs_3_), channel_id=1, source_target_pairs={{0,4},{4,8},{8,12},{12,14},{14,10},{10,6},{6,2},{2,0},{1,5},{5,9},... | collective-permute-start | bytes 1179656 | tf_op jit(solution)/shard_map/ppermute | solution.py:245
  27.0 2.6 %collective-permute-start.6 = (s32[4096]{0:T(1024)S(1)}, s32[4096]{0:T(1024)S(1)}, u32[]{:S(2)}, u32[]{:S(2)}) collective-permute-start(s32[4096]{0:T(1024)S(1)} %add_select_fusion.1), channel_id=1, source_target_pairs={{0,8},{2,10},{4,12},{6,14},{8,0},{10,2},{12,4},{14,6},{1,9},{3,11}... | collective-permute-start | bytes 49160 | tf_op jit(solution)/shard_map/ppermute | solution.py:258
  29.7 5.0 %build_table.5.table_ref = f32[8968,128]{1,0:T(8,128)} custom-call(s32[1792,4096]{1,0:T(8,128)} %flips_ref.5, bf16[384,1792]{1,0:T(8,128)(2,1)} %bitcast.17, f32[8968,128]{1,0:T(8,128)} %build_table.4.refs_0_), custom_call_target="tpu_custom_call", output_to_operand_aliasing={{}: (2, {})} | custom-call | flops 4194304 | bytes 8388608 | tf_op jit(solution)/shard_map/build_table/pallas_call | solution.py:68
  34.9 1.2 %collective-permute-start.10 = (bf16[192,512]{1,0:T(8,128)(2,1)S(1)}, bf16[192,512]{1,0:T(8,128)(2,1)S(1)}, u32[]{:S(2)}, u32[]{:S(2)}) collective-permute-start(bf16[192,512]{1,0:T(8,128)(2,1)S(1)} %slice.17), channel_id=1, source_target_pairs={{4,0},{8,4},{12,8},{14,12},{10,14},{6,10},{2,6},{0,2},{5,1},{9,5},... | collective-permute-start | bytes 589832 | tf_op jit(solution)/shard_map/ppermute | solution.py:245
  36.1 1.5 %collective-permute-start.9 = (bf16[192,512]{1,0:T(8,128)(2,1)S(1)}, bf16[192,512]{1,0:T(8,128)(2,1)S(1)}, u32[]{:S(2)}, u32[]{:S(2)}) collective-permute-start(bf16[192,512]{1,0:T(8,128)(2,1)S(1)} %slice.16), channel_id=1, source_target_pairs={{0,4},{4,8},{8,12},{12,14},{14,10},{10,6},{6,2},{2,0},{1,5},{5,9},... | collective-permute-start | bytes 589832 | tf_op jit(solution)/shard_map/ppermute | solution.py:245
  37.7 3.5 %collective-permute-done.10 = bf16[192,512]{1,0:T(8,128)(2,1)S(1)} collective-permute-done((bf16[192,512]{1,0:T(8,128)(2,1)S(1)}, bf16[192,512]{1,0:T(8,128)(2,1)S(1)}, u32[]{:S(2)}, u32[]{:S(2)}) %collective-permute-start.10) | collective-permute-done | bytes 196640 | tf_op jit(solution)/shard_map/ppermute | solution.py:245
  41.9 2.3 %copy-done = f32[8968,128]{1,0:T(8,128)S(1)} copy-done((f32[8968,128]{1,0:T(8,128)S(1)}, f32[8968,128]{1,0:T(8,128)}, u32[]{:S(2)}) %copy-start) | copy-done | bytes 4591640
  44.2 35.8 %sample_rows.1 = f32[3,8192]{1,0:T(4,128)S(1)} custom-call(s32[9]{0:T(128)S(1)} %stack.36.scalars, s32[8192]{0:T(1024)S(1)} %fusion.1.rows_ref, s32[1,8192]{1,0:T(1,128)S(1)} %broadcast_select_fusion.offsets_ref, f32[8968,128]{1,0:T(8,128)S(1)} %copy-done, bf16[384,512]{1,0:T(8,128)(2,1)S(1)} %bitcast.14, ...), custom_call_target="tpu_custom_call" | custom-call | flops 25769803776 | bytes 18874368 | tf_op jit(solution)/shard_map/sample_rows/pallas_call | solution.py:182
  80.0 3.0 %collective-permute-start.11 = (f32[3,4096]{1,0:T(4,128)S(1)}, f32[3,4096]{1,0:T(4,128)S(1)}, u32[]{:S(2)}, u32[]{:S(2)}) collective-permute-start(f32[3,4096]{1,0:T(4,128)S(1)} %get-tuple-element.31), channel_id=1, source_target_pairs={{0,8},{2,10},{4,12},{6,14},{8,0},{10,2},{12,4},{14,6},{1,9},{3,11}... | collective-permute-start | bytes 147464 | tf_op jit(solution)/shard_map/ppermute | solution.py:215
  83.1 2.3 %collective-permute-done.11 = f32[3,4096]{1,0:T(4,128)S(1)} collective-permute-done((f32[3,4096]{1,0:T(4,128)S(1)}, f32[3,4096]{1,0:T(4,128)S(1)}, u32[]{:S(2)}, u32[]{:S(2)}) %collective-permute-start.11) | collective-permute-done | bytes 49184 | tf_op jit(solution)/shard_map/ppermute | solution.py:215
  85.3 3.1 %collective-permute-done.14 = f32[3,4096]{1,0:T(4,128)S(1)} collective-permute-done((f32[3,4096]{1,0:T(4,128)S(1)}, f32[3,4096]{1,0:T(4,128)S(1)}, u32[]{:S(2)}, u32[]{:S(2)}) %collective-permute-start.14) | collective-permute-done | bytes 49184 | tf_op jit(solution)/shard_map/ppermute | solution.py:215
  88.6 2.0 %collective-permute-start.15 = (f32[3,4096]{1,0:T(4,128)S(1)}, f32[3,4096]{1,0:T(4,128)S(1)}, u32[]{:S(2)}, u32[]{:S(2)}) collective-permute-start(f32[3,4096]{1,0:T(4,128)S(1)} %get-tuple-element.30), channel_id=1, source_target_pairs={{0,4},{2,6},{4,0},{6,2},{8,12},{10,14},{12,8},{14,10},{1,5},{3,7},... | collective-permute-start | bytes 147464 | tf_op jit(solution)/shard_map/ppermute | solution.py:215
  90.6 2.2 %collective-permute-done.12 = f32[3,4096]{1,0:T(4,128)S(1)} collective-permute-done((f32[3,4096]{1,0:T(4,128)S(1)}, f32[3,4096]{1,0:T(4,128)S(1)}, u32[]{:S(2)}, u32[]{:S(2)}) %collective-permute-start.12) | collective-permute-done | bytes 49184 | tf_op jit(solution)/shard_map/ppermute | solution.py:215
  93.6 1.5 %collective-permute-start.16 = (f32[3,4096]{1,0:T(4,128)S(1)}, f32[3,4096]{1,0:T(4,128)S(1)}, u32[]{:S(2)}, u32[]{:S(2)}) collective-permute-start(f32[3,4096]{1,0:T(4,128)S(1)} %add.112), channel_id=1, source_target_pairs={{0,2},{2,0},{4,6},{6,4},{8,10},{10,8},{12,14},{14,12},{1,3},{3,1},... | collective-permute-start | bytes 147464 | tf_op jit(solution)/shard_map/ppermute | solution.py:215
  95.1 2.1 %collective-permute-done.13 = f32[3,4096]{1,0:T(4,128)S(1)} collective-permute-done((f32[3,4096]{1,0:T(4,128)S(1)}, f32[3,4096]{1,0:T(4,128)S(1)}, u32[]{:S(2)}, u32[]{:S(2)}) %collective-permute-start.13) | collective-permute-done | bytes 49184 | tf_op jit(solution)/shard_map/ppermute | solution.py:215
  97.9 0.7 pad_maximum_fusion.1
  (35 shorter events, 3.8 us)
Async XLA Ops:
  0.0 12.4 %collective-permute-start.1 = (bf16[384,512]{1,0:T(8,128)(2,1)}, bf16[384,512]{1,0:T(8,128)(2,1)S(1)}, u32[]{:S(2)}, u32[]{:S(2)}) collective-permute-start(bf16[384,512]{1,0:T(8,128)(2,1)} %bitcast.12), channel_id=1, source_target_pairs={{0,4},{4,8},{8,12},{12,14},{14,10},{10,6},{6,2},{2,0},{1,5},{5,9},... | collective-permute-start | bytes 1179656 | tf_op jit(solution)/shard_map/ppermute | solution.py:245
  3.0 10.8 %collective-permute-start.2 = (bf16[384,512]{1,0:T(8,128)(2,1)}, bf16[384,512]{1,0:T(8,128)(2,1)S(1)}, u32[]{:S(2)}, u32[]{:S(2)}) collective-permute-start(bf16[384,512]{1,0:T(8,128)(2,1)} %bitcast.13), channel_id=1, source_target_pairs={{4,0},{8,4},{12,8},{14,12},{10,14},{6,10},{2,6},{0,2},{5,1},{9,5},... | collective-permute-start | bytes 1179656 | tf_op jit(solution)/shard_map/ppermute | solution.py:245
  3.0 9.3 %collective-permute-start = (s32[1024]{0:T(1024)}, s32[1024]{0:T(1024)S(1)}, u32[]{:S(2)}, u32[]{:S(2)}) collective-permute-start(s32[1024]{0:T(1024)} %param.7), channel_id=1, source_target_pairs={{0,2},{2,0},{4,6},{6,4},{8,10},{10,8},{12,14},{14,12},{1,3},{3,1},... | collective-permute-start | bytes 12296 | tf_op jit(solution)/shard_map/ppermute | solution.py:258
  5.0 10.9 %copy-start.2 = (s32[1024]{0:T(1024)S(1)}, s32[1024]{0:T(1024)}, u32[]{:S(2)}) copy-start(s32[1024]{0:T(1024)} %param.7) | copy-start | bytes 12292
  13.8 11.1 %collective-permute-start.4 = (bf16[384,512]{1,0:T(8,128)(2,1)S(1)}, bf16[384,512]{1,0:T(8,128)(2,1)S(1)}, u32[]{:S(2)}, u32[]{:S(2)}) collective-permute-start(bf16[384,512]{1,0:T(8,128)(2,1)S(1)} %collective-permute-done.1.refs_1_), channel_id=1, source_target_pairs={{0,4},{4,8},{8,12},{12,14},{14,10},{10,6},{6,2},{2,0},{1,5},{5,9},... | collective-permute-start | bytes 1179656 | tf_op jit(solution)/shard_map/ppermute | solution.py:245
  15.4 9.6 %collective-permute-start.5 = (bf16[384,512]{1,0:T(8,128)(2,1)S(1)}, bf16[384,512]{1,0:T(8,128)(2,1)S(1)}, u32[]{:S(2)}, u32[]{:S(2)}) collective-permute-start(bf16[384,512]{1,0:T(8,128)(2,1)S(1)} %collective-permute-done.2.refs_2_), channel_id=1, source_target_pairs={{4,0},{8,4},{12,8},{14,12},{10,14},{6,10},{2,6},{0,2},{5,1},{9,5},... | collective-permute-start | bytes 1179656 | tf_op jit(solution)/shard_map/ppermute | solution.py:245
  15.8 9.1 %collective-permute-start.3 = (s32[2048]{0:T(1024)S(1)}, s32[2048]{0:T(1024)S(1)}, u32[]{:S(2)}, u32[]{:S(2)}) collective-permute-start(s32[2048]{0:T(1024)S(1)} %add_select_fusion.2), channel_id=1, source_target_pairs={{0,4},{2,6},{4,0},{6,2},{8,12},{10,14},{12,8},{14,10},{1,5},{3,7},... | collective-permute-start | bytes 24584 | tf_op jit(solution)/shard_map/ppermute | solution.py:258
  25.0 10.0 %collective-permute-start.8 = (bf16[384,512]{1,0:T(8,128)(2,1)S(1)}, bf16[384,512]{1,0:T(8,128)(2,1)S(1)}, u32[]{:S(2)}, u32[]{:S(2)}) collective-permute-start(bf16[384,512]{1,0:T(8,128)(2,1)S(1)} %collective-permute-done.5.refs_4_), channel_id=1, source_target_pairs={{4,0},{8,4},{12,8},{14,12},{10,14},{6,10},{2,6},{0,2},{5,1},{9,5},... | collective-permute-start | bytes 1179656 | tf_op jit(solution)/shard_map/ppermute | solution.py:245
  25.2 10.9 %collective-permute-start.7 = (bf16[384,512]{1,0:T(8,128)(2,1)S(1)}, bf16[384,512]{1,0:T(8,128)(2,1)S(1)}, u32[]{:S(2)}, u32[]{:S(2)}) collective-permute-start(bf16[384,512]{1,0:T(8,128)(2,1)S(1)} %collective-permute-done.4.refs_3_), channel_id=1, source_target_pairs={{0,4},{4,8},{8,12},{12,14},{14,10},{10,6},{6,2},{2,0},{1,5},{5,9},... | collective-permute-start | bytes 1179656 | tf_op jit(solution)/shard_map/ppermute | solution.py:245
  27.0 7.9 %collective-permute-start.6 = (s32[4096]{0:T(1024)S(1)}, s32[4096]{0:T(1024)S(1)}, u32[]{:S(2)}, u32[]{:S(2)}) collective-permute-start(s32[4096]{0:T(1024)S(1)} %add_select_fusion.1), channel_id=1, source_target_pairs={{0,8},{2,10},{4,12},{6,14},{8,0},{10,2},{12,4},{14,6},{1,9},{3,11}... | collective-permute-start | bytes 49160 | tf_op jit(solution)/shard_map/ppermute | solution.py:258
  29.7 12.2 %copy-start.1 = (bf16[3,128,512]{2,1,0:T(8,128)(2,1)S(1)}, bf16[3,128,512]{2,1,0:T(8,128)(2,1)}, u32[]{:S(2)}) copy-start(bf16[3,128,512]{2,1,0:T(8,128)(2,1)} %param.5) | copy-start | bytes 1179652
  34.9 6.3 %collective-permute-start.10 = (bf16[192,512]{1,0:T(8,128)(2,1)S(1)}, bf16[192,512]{1,0:T(8,128)(2,1)S(1)}, u32[]{:S(2)}, u32[]{:S(2)}) collective-permute-start(bf16[192,512]{1,0:T(8,128)(2,1)S(1)} %slice.17), channel_id=1, source_target_pairs={{4,0},{8,4},{12,8},{14,12},{10,14},{6,10},{2,6},{0,2},{5,1},{9,5},... | collective-permute-start | bytes 589832 | tf_op jit(solution)/shard_map/ppermute | solution.py:245
  36.1 5.7 %collective-permute-start.9 = (bf16[192,512]{1,0:T(8,128)(2,1)S(1)}, bf16[192,512]{1,0:T(8,128)(2,1)S(1)}, u32[]{:S(2)}, u32[]{:S(2)}) collective-permute-start(bf16[192,512]{1,0:T(8,128)(2,1)S(1)} %slice.16), channel_id=1, source_target_pairs={{0,4},{4,8},{8,12},{12,14},{14,10},{10,6},{6,2},{2,0},{1,5},{5,9},... | collective-permute-start | bytes 589832 | tf_op jit(solution)/shard_map/ppermute | solution.py:245
  41.9 2.3 %copy-start = (f32[8968,128]{1,0:T(8,128)S(1)}, f32[8968,128]{1,0:T(8,128)}, u32[]{:S(2)}) copy-start(f32[8968,128]{1,0:T(8,128)} %build_table.5.table_ref) | copy-start | bytes 13774852
  80.0 5.4 %collective-permute-start.11 = (f32[3,4096]{1,0:T(4,128)S(1)}, f32[3,4096]{1,0:T(4,128)S(1)}, u32[]{:S(2)}, u32[]{:S(2)}) collective-permute-start(f32[3,4096]{1,0:T(4,128)S(1)} %get-tuple-element.31), channel_id=1, source_target_pairs={{0,8},{2,10},{4,12},{6,14},{8,0},{10,2},{12,4},{14,6},{1,9},{3,11}... | collective-permute-start | bytes 147464 | tf_op jit(solution)/shard_map/ppermute | solution.py:215
  83.0 5.5 %collective-permute-start.14 = (f32[3,4096]{1,0:T(4,128)S(1)}, f32[3,4096]{1,0:T(4,128)S(1)}, u32[]{:S(2)}, u32[]{:S(2)}) collective-permute-start(f32[3,4096]{1,0:T(4,128)S(1)} %get-tuple-element.32), channel_id=1, source_target_pairs={{0,8},{2,10},{4,12},{6,14},{8,0},{10,2},{12,4},{14,6},{1,9},{3,11}... | collective-permute-start | bytes 147464 | tf_op jit(solution)/shard_map/ppermute | solution.py:215
  88.5 4.3 %collective-permute-start.12 = (f32[3,4096]{1,0:T(4,128)S(1)}, f32[3,4096]{1,0:T(4,128)S(1)}, u32[]{:S(2)}, u32[]{:S(2)}) collective-permute-start(f32[3,4096]{1,0:T(4,128)S(1)} %get-tuple-element.29), channel_id=1, source_target_pairs={{0,4},{2,6},{4,0},{6,2},{8,12},{10,14},{12,8},{14,10},{1,5},{3,7},... | collective-permute-start | bytes 147464 | tf_op jit(solution)/shard_map/ppermute | solution.py:215
  88.6 5.0 %collective-permute-start.15 = (f32[3,4096]{1,0:T(4,128)S(1)}, f32[3,4096]{1,0:T(4,128)S(1)}, u32[]{:S(2)}, u32[]{:S(2)}) collective-permute-start(f32[3,4096]{1,0:T(4,128)S(1)} %get-tuple-element.30), channel_id=1, source_target_pairs={{0,4},{2,6},{4,0},{6,2},{8,12},{10,14},{12,8},{14,10},{1,5},{3,7},... | collective-permute-start | bytes 147464 | tf_op jit(solution)/shard_map/ppermute | solution.py:215
  92.9 4.3 %collective-permute-start.13 = (f32[3,4096]{1,0:T(4,128)S(1)}, f32[3,4096]{1,0:T(4,128)S(1)}, u32[]{:S(2)}, u32[]{:S(2)}) collective-permute-start(f32[3,4096]{1,0:T(4,128)S(1)} %add.109), channel_id=1, source_target_pairs={{0,2},{2,0},{4,6},{6,4},{8,10},{10,8},{12,14},{14,12},{1,3},{3,1},... | collective-permute-start | bytes 147464 | tf_op jit(solution)/shard_map/ppermute | solution.py:215
  93.6 4.3 %collective-permute-start.16 = (f32[3,4096]{1,0:T(4,128)S(1)}, f32[3,4096]{1,0:T(4,128)S(1)}, u32[]{:S(2)}, u32[]{:S(2)}) collective-permute-start(f32[3,4096]{1,0:T(4,128)S(1)} %add.112), channel_id=1, source_target_pairs={{0,2},{2,0},{4,6},{6,4},{8,10},{10,8},{12,14},{14,12},{1,3},{3,1},... | collective-permute-start | bytes 147464 | tf_op jit(solution)/shard_map/ppermute | solution.py:215

commit v8 on v7

--- a/solution.py
+++ b/solution.py
@@ -209,11 +209,10 @@
     return [(source, source ^ step) for source in range(parties)]
 
 
-def sum_shards(values, parties):
-    step = parties // 2
-    while step > 0:
+def sum_shards(values, parties, turn):
+    steps = [parties >> (at + 1) for at in range(parties.bit_length() - 1)]
+    for step in steps[turn:] + steps[:turn]:
         values = values + lax.ppermute(values, "param", by_xor(parties, step))
-        step //= 2
     return values
 
 
@@ -295,7 +294,8 @@
         jnp.stack([own] + numbers), unit_rows, line, table, pieces, examples, width, per_shard, parties, scale
     )
     half = count // 2
-    return jnp.concatenate([sum_shards(part, parties) for part in (values[:, :half], values[:, half:])], axis=1)
+    parts = [sum_shards(part, parties, turn) for turn, part in enumerate((values[:, :half], values[:, half:]))]
+    return jnp.concatenate(parts, axis=1)
 
 
 def solution(mesh):

time: 98.8 us -> 98.4 us (level)
  no operation moved by 1% of the time
where the time goes in v8:
time: 98.4 us; the launch traced here: 98.3 us
  Pallas kernels  52.8 us (54%)
  starting transfers between devices  22.1 us (22%)
  waiting for transfers between devices  20 us (20%)
  local copies, waits for them, and re-layouts  2.44 us (2%)
    pallas_call x1, Pallas kernels, sample(): pl.pallas_call(functools.partial(sample_kernel, blocks=len(cotangents), e...  35.8 us
    pallas_call x3, Pallas kernels, build_table(): pl.pallas_call(functools.partial(table_kernel, examples=examples), grid=(...  17 us
    ppermute x6, waiting for transfers between devices, sum_shards(): values = values + lax.ppermute(values, 'param', by_xor(parties, step))  11.3 us
    ppermute x4, starting transfers between devices, pass_on(): lax.ppermute(ahead, 'param', forward)  7.89 us
    ppermute x6, starting transfers between devices, sum_shards(): values = values + lax.ppermute(values, 'param', by_xor(parties, step))  6.19 us
    ppermute x3, starting transfers between devices, local(): other = lax.ppermute(offsets, 'param', by_xor(parties, step))  6.11 us
    ppermute x4, waiting for transfers between devices, pass_on(): lax.ppermute(behind, 'param', backward)  4.97 us
    ppermute x3, waiting for transfers between devices, local(): other = lax.ppermute(offsets, 'param', by_xor(parties, step))  3.12 us
  transfers between devices with their start and end apart: 17, of which 12 were waited for; matrix products, arithmetic and copies ran while one was open for 0% of the time, Pallas kernels for 17%

profile of v8, /device:TPU:0, one launch (start us, length us, event | category | flops | bytes accessed | tf_op | source)
XLA Modules:
  0.0 98.3 jit_solution(6868726145315921509)
XLA Ops:
  0.0 3.0 %collective-permute-start.1 = (bf16[384,512]{1,0:T(8,128)(2,1)}, bf16[384,512]{1,0:T(8,128)(2,1)S(1)}, u32[]{:S(2)}, u32[]{:S(2)}) collective-permute-start(bf16[384,512]{1,0:T(8,128)(2,1)} %bitcast.12), channel_id=1, source_target_pairs={{0,4},{4,8},{8,12},{12,14},{14,10},{10,6},{6,2},{2,0},{1,5},{5,9},... | collective-permute-start | bytes 1179656 | tf_op jit(solution)/shard_map/ppermute | solution.py:244
  3.0 1.9 %collective-permute-start = (s32[1024]{0:T(1024)}, s32[1024]{0:T(1024)S(1)}, u32[]{:S(2)}, u32[]{:S(2)}) collective-permute-start(s32[1024]{0:T(1024)} %param.7), channel_id=1, source_target_pairs={{0,2},{2,0},{4,6},{6,4},{8,10},{10,8},{12,14},{14,12},{1,3},{3,1},... | collective-permute-start | bytes 12296 | tf_op jit(solution)/shard_map/ppermute | solution.py:257
  5.0 7.1 %build_table.3.refs_0_ = f32[8968,128]{1,0:T(8,128)} custom-call(s32[1792,4096]{1,0:T(8,128)} %flips_ref.5, bf16[384,1792]{1,0:T(8,128)(2,1)} %bitcast.15), custom_call_target="tpu_custom_call" | custom-call | flops 6291456 | bytes 12582912 | tf_op jit(solution)/shard_map/build_table/pallas_call | solution.py:68
  12.4 1.5 %collective-permute-done.2.refs_2_ = bf16[384,512]{1,0:T(8,128)(2,1)S(1)} collective-permute-done((bf16[384,512]{1,0:T(8,128)(2,1)}, bf16[384,512]{1,0:T(8,128)(2,1)S(1)}, u32[]{:S(2)}, u32[]{:S(2)}) %collective-permute-start.2) | collective-permute-done | bytes 393248 | tf_op jit(solution)/shard_map/ppermute | solution.py:244
  13.8 1.6 %collective-permute-start.4 = (bf16[384,512]{1,0:T(8,128)(2,1)S(1)}, bf16[384,512]{1,0:T(8,128)(2,1)S(1)}, u32[]{:S(2)}, u32[]{:S(2)}) collective-permute-start(bf16[384,512]{1,0:T(8,128)(2,1)S(1)} %collective-permute-done.1.refs_1_), channel_id=1, source_target_pairs={{0,4},{4,8},{8,12},{12,14},{14,10},{10,6},{6,2},{2,0},{1,5},{5,9},... | collective-permute-start | bytes 1179656 | tf_op jit(solution)/shard_map/ppermute | solution.py:244
  15.8 1.6 %collective-permute-start.3 = (s32[2048]{0:T(1024)S(1)}, s32[2048]{0:T(1024)S(1)}, u32[]{:S(2)}, u32[]{:S(2)}) collective-permute-start(s32[2048]{0:T(1024)S(1)} %add_select_fusion.2), channel_id=1, source_target_pairs={{0,4},{2,6},{4,0},{6,2},{8,12},{10,14},{12,8},{14,10},{1,5},{3,7},... | collective-permute-start | bytes 24584 | tf_op jit(solution)/shard_map/ppermute | solution.py:257
  17.4 5.0 %build_table.4.refs_0_ = f32[8968,128]{1,0:T(8,128)} custom-call(s32[1792,4096]{1,0:T(8,128)} %flips_ref.5, bf16[384,1792]{1,0:T(8,128)(2,1)} %bitcast.16, f32[8968,128]{1,0:T(8,128)} %build_table.3.refs_0_), custom_call_target="tpu_custom_call", output_to_operand_aliasing={{}: (2, {})} | custom-call | flops 4194304 | bytes 8388608 | tf_op jit(solution)/shard_map/build_table/pallas_call | solution.py:68
  22.4 2.6 %collective-permute-done.3 = s32[2048]{0:T(1024)S(1)} collective-permute-done((s32[2048]{0:T(1024)S(1)}, s32[2048]{0:T(1024)S(1)}, u32[]{:S(2)}, u32[]{:S(2)}) %collective-permute-start.3) | collective-permute-done | bytes 8224 | tf_op jit(solution)/shard_map/ppermute | solution.py:257
  25.2 1.8 %collective-permute-start.7 = (bf16[384,512]{1,0:T(8,128)(2,1)S(1)}, bf16[384,512]{1,0:T(8,128)(2,1)S(1)}, u32[]{:S(2)}, u32[]{:S(2)}) collective-permute-start(bf16[384,512]{1,0:T(8,128)(2,1)S(1)} %collective-permute-done.4.refs_3_), channel_id=1, source_target_pairs={{0,4},{4,8},{8,12},{12,14},{14,10},{10,6},{6,2},{2,0},{1,5},{5,9},... | collective-permute-start | bytes 1179656 | tf_op jit(solution)/shard_map/ppermute | solution.py:244
  27.0 2.6 %collective-permute-start.6 = (s32[4096]{0:T(1024)S(1)}, s32[4096]{0:T(1024)S(1)}, u32[]{:S(2)}, u32[]{:S(2)}) collective-permute-start(s32[4096]{0:T(1024)S(1)} %add_select_fusion.1), channel_id=1, source_target_pairs={{0,8},{2,10},{4,12},{6,14},{8,0},{10,2},{12,4},{14,6},{1,9},{3,11}... | collective-permute-start | bytes 49160 | tf_op jit(solution)/shard_map/ppermute | solution.py:257
  29.7 5.0 %build_table.5.table_ref = f32[8968,128]{1,0:T(8,128)} custom-call(s32[1792,4096]{1,0:T(8,128)} %flips_ref.5, bf16[384,1792]{1,0:T(8,128)(2,1)} %bitcast.17, f32[8968,128]{1,0:T(8,128)} %build_table.4.refs_0_), custom_call_target="tpu_custom_call", output_to_operand_aliasing={{}: (2, {})} | custom-call | flops 4194304 | bytes 8388608 | tf_op jit(solution)/shard_map/build_table/pallas_call | solution.py:68
  34.9 1.2 %collective-permute-start.10 = (bf16[192,512]{1,0:T(8,128)(2,1)S(1)}, bf16[192,512]{1,0:T(8,128)(2,1)S(1)}, u32[]{:S(2)}, u32[]{:S(2)}) collective-permute-start(bf16[192,512]{1,0:T(8,128)(2,1)S(1)} %slice.17), channel_id=1, source_target_pairs={{4,0},{8,4},{12,8},{14,12},{10,14},{6,10},{2,6},{0,2},{5,1},{9,5},... | collective-permute-start | bytes 589832 | tf_op jit(solution)/shard_map/ppermute | solution.py:244
  36.1 1.5 %collective-permute-start.9 = (bf16[192,512]{1,0:T(8,128)(2,1)S(1)}, bf16[192,512]{1,0:T(8,128)(2,1)S(1)}, u32[]{:S(2)}, u32[]{:S(2)}) collective-permute-start(bf16[192,512]{1,0:T(8,128)(2,1)S(1)} %slice.16), channel_id=1, source_target_pairs={{0,4},{4,8},{8,12},{12,14},{14,10},{10,6},{6,2},{2,0},{1,5},{5,9},... | collective-permute-start | bytes 589832 | tf_op jit(solution)/shard_map/ppermute | solution.py:244
  37.7 3.5 %collective-permute-done.10 = bf16[192,512]{1,0:T(8,128)(2,1)S(1)} collective-permute-done((bf16[192,512]{1,0:T(8,128)(2,1)S(1)}, bf16[192,512]{1,0:T(8,128)(2,1)S(1)}, u32[]{:S(2)}, u32[]{:S(2)}) %collective-permute-start.10) | collective-permute-done | bytes 196640 | tf_op jit(solution)/shard_map/ppermute | solution.py:244
  41.9 2.3 %copy-done = f32[8968,128]{1,0:T(8,128)S(1)} copy-done((f32[8968,128]{1,0:T(8,128)S(1)}, f32[8968,128]{1,0:T(8,128)}, u32[]{:S(2)}) %copy-start) | copy-done | bytes 4591640
  44.2 35.8 %sample_rows.1 = f32[3,8192]{1,0:T(4,128)S(1)} custom-call(s32[9]{0:T(128)S(1)} %stack.36.scalars, s32[8192]{0:T(1024)S(1)} %fusion.1.rows_ref, s32[1,8192]{1,0:T(1,128)S(1)} %broadcast_select_fusion.offsets_ref, f32[8968,128]{1,0:T(8,128)S(1)} %copy-done, bf16[384,512]{1,0:T(8,128)(2,1)S(1)} %bitcast.14, ...), custom_call_target="tpu_custom_call" | custom-call | flops 25769803776 | bytes 18874368 | tf_op jit(solution)/shard_map/sample_rows/pallas_call | solution.py:182
  80.0 3.0 %collective-permute-start.11 = (f32[3,4096]{1,0:T(4,128)S(1)}, f32[3,4096]{1,0:T(4,128)S(1)}, u32[]{:S(2)}, u32[]{:S(2)}) collective-permute-start(f32[3,4096]{1,0:T(4,128)S(1)} %get-tuple-element.31), channel_id=1, source_target_pairs={{0,8},{2,10},{4,12},{6,14},{8,0},{10,2},{12,4},{14,6},{1,9},{3,11}... | collective-permute-start | bytes 147464 | tf_op jit(solution)/shard_map/ppermute | solution.py:215
  83.2 2.0 %collective-permute-done.11 = f32[3,4096]{1,0:T(4,128)S(1)} collective-permute-done((f32[3,4096]{1,0:T(4,128)S(1)}, f32[3,4096]{1,0:T(4,128)S(1)}, u32[]{:S(2)}, u32[]{:S(2)}) %collective-permute-start.11) | collective-permute-done | bytes 49184 | tf_op jit(solution)/shard_map/ppermute | solution.py:215
  85.3 2.0 %collective-permute-done.14 = f32[3,4096]{1,0:T(4,128)S(1)} collective-permute-done((f32[3,4096]{1,0:T(4,128)S(1)}, f32[3,4096]{1,0:T(4,128)S(1)}, u32[]{:S(2)}, u32[]{:S(2)}) %collective-permute-start.14) | collective-permute-done | bytes 49184 | tf_op jit(solution)/shard_map/ppermute | solution.py:215
  88.1 0.8 collective-permute-start.15
  88.9 2.7 %collective-permute-done.12 = f32[3,4096]{1,0:T(4,128)S(1)} collective-permute-done((f32[3,4096]{1,0:T(4,128)S(1)}, f32[3,4096]{1,0:T(4,128)S(1)}, u32[]{:S(2)}, u32[]{:S(2)}) %collective-permute-start.12) | collective-permute-done | bytes 49184 | tf_op jit(solution)/shard_map/ppermute | solution.py:215
  92.4 1.2 %collective-permute-start.16 = (f32[3,4096]{1,0:T(4,128)S(1)}, f32[3,4096]{1,0:T(4,128)S(1)}, u32[]{:S(2)}, u32[]{:S(2)}) collective-permute-start(f32[3,4096]{1,0:T(4,128)S(1)} %add.112), channel_id=1, source_target_pairs={{0,8},{2,10},{4,12},{6,14},{8,0},{10,2},{12,4},{14,6},{1,9},{3,11}... | collective-permute-start | bytes 147464 | tf_op jit(solution)/shard_map/ppermute | solution.py:215
  93.5 2.5 %collective-permute-done.13 = f32[3,4096]{1,0:T(4,128)S(1)} collective-permute-done((f32[3,4096]{1,0:T(4,128)S(1)}, f32[3,4096]{1,0:T(4,128)S(1)}, u32[]{:S(2)}, u32[]{:S(2)}) %collective-permute-start.13) | collective-permute-done | bytes 49184 | tf_op jit(solution)/shard_map/ppermute | solution.py:215
  96.0 1.6 %collective-permute-done.16 = f32[3,4096]{1,0:T(4,128)S(1)} collective-permute-done((f32[3,4096]{1,0:T(4,128)S(1)}, f32[3,4096]{1,0:T(4,128)S(1)}, u32[]{:S(2)}, u32[]{:S(2)}) %collective-permute-start.16) | collective-permute-done | bytes 49184 | tf_op jit(solution)/shard_map/ppermute | solution.py:215
  (35 shorter events, 4.6 us)
Async XLA Ops:
  0.0 12.4 %collective-permute-start.1 = (bf16[384,512]{1,0:T(8,128)(2,1)}, bf16[384,512]{1,0:T(8,128)(2,1)S(1)}, u32[]{:S(2)}, u32[]{:S(2)}) collective-permute-start(bf16[384,512]{1,0:T(8,128)(2,1)} %bitcast.12), channel_id=1, source_target_pairs={{0,4},{4,8},{8,12},{12,14},{14,10},{10,6},{6,2},{2,0},{1,5},{5,9},... | collective-permute-start | bytes 1179656 | tf_op jit(solution)/shard_map/ppermute | solution.py:244
  3.0 10.8 %collective-permute-start.2 = (bf16[384,512]{1,0:T(8,128)(2,1)}, bf16[384,512]{1,0:T(8,128)(2,1)S(1)}, u32[]{:S(2)}, u32[]{:S(2)}) collective-permute-start(bf16[384,512]{1,0:T(8,128)(2,1)} %bitcast.13), channel_id=1, source_target_pairs={{4,0},{8,4},{12,8},{14,12},{10,14},{6,10},{2,6},{0,2},{5,1},{9,5},... | collective-permute-start | bytes 1179656 | tf_op jit(solution)/shard_map/ppermute | solution.py:244
  3.0 9.3 %collective-permute-start = (s32[1024]{0:T(1024)}, s32[1024]{0:T(1024)S(1)}, u32[]{:S(2)}, u32[]{:S(2)}) collective-permute-start(s32[1024]{0:T(1024)} %param.7), channel_id=1, source_target_pairs={{0,2},{2,0},{4,6},{6,4},{8,10},{10,8},{12,14},{14,12},{1,3},{3,1},... | collective-permute-start | bytes 12296 | tf_op jit(solution)/shard_map/ppermute | solution.py:257
  5.0 10.9 %copy-start.2 = (s32[1024]{0:T(1024)S(1)}, s32[1024]{0:T(1024)}, u32[]{:S(2)}) copy-start(s32[1024]{0:T(1024)} %param.7) | copy-start | bytes 12292
  13.8 11.1 %collective-permute-start.4 = (bf16[384,512]{1,0:T(8,128)(2,1)S(1)}, bf16[384,512]{1,0:T(8,128)(2,1)S(1)}, u32[]{:S(2)}, u32[]{:S(2)}) collective-permute-start(bf16[384,512]{1,0:T(8,128)(2,1)S(1)} %collective-permute-done.1.refs_1_), channel_id=1, source_target_pairs={{0,4},{4,8},{8,12},{12,14},{14,10},{10,6},{6,2},{2,0},{1,5},{5,9},... | collective-permute-start | bytes 1179656 | tf_op jit(solution)/shard_map/ppermute | solution.py:244
  15.4 9.6 %collective-permute-start.5 = (bf16[384,512]{1,0:T(8,128)(2,1)S(1)}, bf16[384,512]{1,0:T(8,128)(2,1)S(1)}, u32[]{:S(2)}, u32[]{:S(2)}) collective-permute-start(bf16[384,512]{1,0:T(8,128)(2,1)S(1)} %collective-permute-done.2.refs_2_), channel_id=1, source_target_pairs={{4,0},{8,4},{12,8},{14,12},{10,14},{6,10},{2,6},{0,2},{5,1},{9,5},... | collective-permute-start | bytes 1179656 | tf_op jit(solution)/shard_map/ppermute | solution.py:244
  15.8 9.1 %collective-permute-start.3 = (s32[2048]{0:T(1024)S(1)}, s32[2048]{0:T(1024)S(1)}, u32[]{:S(2)}, u32[]{:S(2)}) collective-permute-start(s32[2048]{0:T(1024)S(1)} %add_select_fusion.2), channel_id=1, source_target_pairs={{0,4},{2,6},{4,0},{6,2},{8,12},{10,14},{12,8},{14,10},{1,5},{3,7},... | collective-permute-start | bytes 24584 | tf_op jit(solution)/shard_map/ppermute | solution.py:257
  25.0 10.0 %collective-permute-start.8 = (bf16[384,512]{1,0:T(8,128)(2,1)S(1)}, bf16[384,512]{1,0:T(8,128)(2,1)S(1)}, u32[]{:S(2)}, u32[]{:S(2)}) collective-permute-start(bf16[384,512]{1,0:T(8,128)(2,1)S(1)} %collective-permute-done.5.refs_4_), channel_id=1, source_target_pairs={{4,0},{8,4},{12,8},{14,12},{10,14},{6,10},{2,6},{0,2},{5,1},{9,5},... | collective-permute-start | bytes 1179656 | tf_op jit(solution)/shard_map/ppermute | solution.py:244
  25.2 10.9 %collective-permute-start.7 = (bf16[384,512]{1,0:T(8,128)(2,1)S(1)}, bf16[384,512]{1,0:T(8,128)(2,1)S(1)}, u32[]{:S(2)}, u32[]{:S(2)}) collective-permute-start(bf16[384,512]{1,0:T(8,128)(2,1)S(1)} %collective-permute-done.4.refs_3_), channel_id=1, source_target_pairs={{0,4},{4,8},{8,12},{12,14},{14,10},{10,6},{6,2},{2,0},{1,5},{5,9},... | collective-permute-start | bytes 1179656 | tf_op jit(solution)/shard_map/ppermute | solution.py:244
  27.0 7.9 %collective-permute-start.6 = (s32[4096]{0:T(1024)S(1)}, s32[4096]{0:T(1024)S(1)}, u32[]{:S(2)}, u32[]{:S(2)}) collective-permute-start(s32[4096]{0:T(1024)S(1)} %add_select_fusion.1), channel_id=1, source_target_pairs={{0,8},{2,10},{4,12},{6,14},{8,0},{10,2},{12,4},{14,6},{1,9},{3,11}... | collective-permute-start | bytes 49160 | tf_op jit(solution)/shard_map/ppermute | solution.py:257
  29.7 12.2 %copy-start.1 = (bf16[3,128,512]{2,1,0:T(8,128)(2,1)S(1)}, bf16[3,128,512]{2,1,0:T(8,128)(2,1)}, u32[]{:S(2)}) copy-start(bf16[3,128,512]{2,1,0:T(8,128)(2,1)} %param.5) | copy-start | bytes 1179652
  34.9 6.3 %collective-permute-start.10 = (bf16[192,512]{1,0:T(8,128)(2,1)S(1)}, bf16[192,512]{1,0:T(8,128)(2,1)S(1)}, u32[]{:S(2)}, u32[]{:S(2)}) collective-permute-start(bf16[192,512]{1,0:T(8,128)(2,1)S(1)} %slice.17), channel_id=1, source_target_pairs={{4,0},{8,4},{12,8},{14,12},{10,14},{6,10},{2,6},{0,2},{5,1},{9,5},... | collective-permute-start | bytes 589832 | tf_op jit(solution)/shard_map/ppermute | solution.py:244
  36.1 5.7 %collective-permute-start.9 = (bf16[192,512]{1,0:T(8,128)(2,1)S(1)}, bf16[192,512]{1,0:T(8,128)(2,1)S(1)}, u32[]{:S(2)}, u32[]{:S(2)}) collective-permute-start(bf16[192,512]{1,0:T(8,128)(2,1)S(1)} %slice.16), channel_id=1, source_target_pairs={{0,4},{4,8},{8,12},{12,14},{14,10},{10,6},{6,2},{2,0},{1,5},{5,9},... | collective-permute-start | bytes 589832 | tf_op jit(solution)/shard_map/ppermute | solution.py:244
  41.9 2.3 %copy-start = (f32[8968,128]{1,0:T(8,128)S(1)}, f32[8968,128]{1,0:T(8,128)}, u32[]{:S(2)}) copy-start(f32[8968,128]{1,0:T(8,128)} %build_table.5.table_ref) | copy-start | bytes 13774852
  80.0 5.2 %collective-permute-start.11 = (f32[3,4096]{1,0:T(4,128)S(1)}, f32[3,4096]{1,0:T(4,128)S(1)}, u32[]{:S(2)}, u32[]{:S(2)}) collective-permute-start(f32[3,4096]{1,0:T(4,128)S(1)} %get-tuple-element.31), channel_id=1, source_target_pairs={{0,8},{2,10},{4,12},{6,14},{8,0},{10,2},{12,4},{14,6},{1,9},{3,11}... | collective-permute-start | bytes 147464 | tf_op jit(solution)/shard_map/ppermute | solution.py:215
  83.0 4.3 %collective-permute-start.14 = (f32[3,4096]{1,0:T(4,128)S(1)}, f32[3,4096]{1,0:T(4,128)S(1)}, u32[]{:S(2)}, u32[]{:S(2)}) collective-permute-start(f32[3,4096]{1,0:T(4,128)S(1)} %get-tuple-element.32), channel_id=1, source_target_pairs={{0,4},{2,6},{4,0},{6,2},{8,12},{10,14},{12,8},{14,10},{1,5},{3,7},... | collective-permute-start | bytes 147464 | tf_op jit(solution)/shard_map/ppermute | solution.py:215
  87.3 4.3 %collective-permute-start.12 = (f32[3,4096]{1,0:T(4,128)S(1)}, f32[3,4096]{1,0:T(4,128)S(1)}, u32[]{:S(2)}, u32[]{:S(2)}) collective-permute-start(f32[3,4096]{1,0:T(4,128)S(1)} %get-tuple-element.29), channel_id=1, source_target_pairs={{0,4},{2,6},{4,0},{6,2},{8,12},{10,14},{12,8},{14,10},{1,5},{3,7},... | collective-permute-start | bytes 147464 | tf_op jit(solution)/shard_map/ppermute | solution.py:215
  88.1 4.3 %collective-permute-start.15 = (f32[3,4096]{1,0:T(4,128)S(1)}, f32[3,4096]{1,0:T(4,128)S(1)}, u32[]{:S(2)}, u32[]{:S(2)}) collective-permute-start(f32[3,4096]{1,0:T(4,128)S(1)} %get-tuple-element.30), channel_id=1, source_target_pairs={{0,2},{2,0},{4,6},{6,4},{8,10},{10,8},{12,14},{14,12},{1,3},{3,1},... | collective-permute-start | bytes 147464 | tf_op jit(solution)/shard_map/ppermute | solution.py:215
  91.7 4.3 %collective-permute-start.13 = (f32[3,4096]{1,0:T(4,128)S(1)}, f32[3,4096]{1,0:T(4,128)S(1)}, u32[]{:S(2)}, u32[]{:S(2)}) collective-permute-start(f32[3,4096]{1,0:T(4,128)S(1)} %add.109), channel_id=1, source_target_pairs={{0,2},{2,0},{4,6},{6,4},{8,10},{10,8},{12,14},{14,12},{1,3},{3,1},... | collective-permute-start | bytes 147464 | tf_op jit(solution)/shard_map/ppermute | solution.py:215
  92.4 5.2 %collective-permute-start.16 = (f32[3,4096]{1,0:T(4,128)S(1)}, f32[3,4096]{1,0:T(4,128)S(1)}, u32[]{:S(2)}, u32[]{:S(2)}) collective-permute-start(f32[3,4096]{1,0:T(4,128)S(1)} %add.112), channel_id=1, source_target_pairs={{0,8},{2,10},{4,12},{6,14},{8,0},{10,2},{12,4},{14,6},{1,9},{3,11}... | collective-permute-start | bytes 147464 | tf_op jit(solution)/shard_map/ppermute | solution.py:215
